TPU v7x, 32 devices: a whole 2x2x4 slice. The times are simulated.
32 devices in a mesh: af: 8 (over z, core), ha: 4 (over y, x).
Axes of the slice: x: 2, y: 2, z: 4, core: 2. Of those that a mesh axis runs over, the one named last changes fastest.
Arguments:
- block_input: bfloat16 [4096, 1024], P(('af', 'ha')), may hold values from -6 to 6
- lengths: int32 [8, 3], P('af'), may hold values from 16 to 480, as said below
- cotangent: bfloat16 [4096, 1024], P(('af', 'ha')), may hold values from -6 to 6
- attngain_early: float32 [1024], replicated, may hold values from 0.25 to 1.75
- query_early: bfloat16 [1024, 1024], P('af', 'ha'), may hold values from -0.1875 to 0.1875
- keys_early: bfloat16 [1024, 1024], P('af', 'ha'), may hold values from -0.1875 to 0.1875
- values_early: bfloat16 [1024, 1024], P('af', 'ha'), may hold values from -0.1875 to 0.1875
- output_early: bfloat16 [1024, 1024], P('af', 'ha'), may hold values from -1.5 to 1.5
- ffngain_early: float32 [1024], replicated, may hold values from 0.25 to 1.75
- gate_early: bfloat16 [1024, 2816], P('af', 'ha'), may hold values from -0.1875 to 0.1875
- upward_early: bfloat16 [1024, 2816], P('af', 'ha'), may hold values from -0.1875 to 0.1875
- down_early: bfloat16 [1024, 2816], P('af', 'ha'), may hold values from -0.109375 to 0.109375
- attngain_later: float32 [1024], replicated, may hold values from 0.25 to 1.75
- query_later: bfloat16 [1024, 1024], P('af', 'ha'), may hold values from -0.1875 to 0.1875
- keys_later: bfloat16 [1024, 1024], P('af', 'ha'), may hold values from -0.1875 to 0.1875
- values_later: bfloat16 [1024, 1024], P('af', 'ha'), may hold values from -0.1875 to 0.1875
- output_later: bfloat16 [1024, 1024], P('af', 'ha'), may hold values from -1.5 to 1.5
- ffngain_later: float32 [1024], replicated, may hold values from 0.25 to 1.75
- gate_later: bfloat16 [1024, 2816], P('af', 'ha'), may hold values from -0.1875 to 0.1875
- upward_later: bfloat16 [1024, 2816], P('af', 'ha'), may hold values from -0.1875 to 0.1875
- down_later: bfloat16 [1024, 2816], P('af', 'ha'), may hold values from -0.109375 to 0.109375
Outputs:
- block_output: bfloat16 [4096, 1024], P(('af', 'ha'))
- input_grad: float32 [4096, 1024], P(('af', 'ha'))
- attngaingrad_early: float32 [1024], replicated
- querygrad_early: float32 [1024, 1024], P('af', 'ha')
- keysgrad_early: float32 [1024, 1024], P('af', 'ha')
- valuesgrad_early: float32 [1024, 1024], P('af', 'ha')
- outputgrad_early: float32 [1024, 1024], P('af', 'ha')
- ffngaingrad_early: float32 [1024], replicated
- gategrad_early: float32 [1024, 2816], P('af', 'ha')
- upwardgrad_early: float32 [1024, 2816], P('af', 'ha')
- downgrad_early: float32 [1024, 2816], P('af', 'ha')
- attngaingrad_later: float32 [1024], replicated
- querygrad_later: float32 [1024, 1024], P('af', 'ha')
- keysgrad_later: float32 [1024, 1024], P('af', 'ha')
- valuesgrad_later: float32 [1024, 1024], P('af', 'ha')
- outputgrad_later: float32 [1024, 1024], P('af', 'ha')
- ffngaingrad_later: float32 [1024], replicated
- gategrad_later: float32 [1024, 2816], P('af', 'ha')
- upwardgrad_later: float32 [1024, 2816], P('af', 'ha')
- downgrad_later: float32 [1024, 2816], P('af', 'ha')
Inputs may be any that keep to these rules, and one draw needn't show every extreme that they name: Row b lists the lengths of the 3 sequences of bucket b in their order; padding fills the rest of its 512 tokens and is at most 32 tokens. One sequence of every bucket begins within the bucket's first 128 tokens and ends within its last 128.
All inputs are finite; a program needn't handle non-finite values.
Results may differ from a plain program's by a relative error of at most 0.035.
Values may be sent and summed in bfloat16 or wider, within the bound.
A program may use at most 128 MiB of HBM per device.

v0:
```python
import jax
import jax.numpy as jnp
from jax import lax
from jax.sharding import PartitionSpec as P

HD = 64


epsilon = 1e-06
rope_base = 10000.0


def product(left, right):
    return jnp.dot(left, right, preferred_element_type=jnp.float32)


def against(left, right):
    return lax.dot_general(
        left, right, (((1,), (1,)), ((), ())), preferred_element_type=jnp.float32
    )


def across(left, right):
    return lax.dot_general(
        left, right, (((0,), (0,)), ((), ())), preferred_element_type=jnp.float32
    )


def normalize(values, gain):
    return values * lax.rsqrt(jnp.mean(values * values, axis=-1, keepdims=True) + epsilon) * gain


def norm_back(values, gain, grads):
    scaling = lax.rsqrt(jnp.mean(values * values, axis=-1, keepdims=True) + epsilon)
    weighted = gain * grads
    inner = jnp.mean(weighted * values, axis=-1, keepdims=True)
    return (
        scaling * weighted - values * scaling * scaling * scaling * inner,
        jnp.sum(grads * values * scaling, axis=0),
    )


def layout(lens_row, bucket):
    counted = lens_row.shape[0]
    ends = jnp.cumsum(lens_row)
    starts = ends - lens_row
    places = jnp.arange(bucket, dtype=jnp.int32)
    documents = jnp.sum((places[:, None] >= ends[None, :]).astype(jnp.int32), axis=1)
    validity = documents < counted
    matching = documents[:, None] == jnp.arange(counted, dtype=jnp.int32)[None, :]
    beginning = jnp.sum(jnp.where(matching, starts[None, :], 0), axis=1)
    offsets = (places - beginning).astype(jnp.float32)
    halfway = HD // 2
    frequency = rope_base ** (-jnp.arange(halfway, dtype=jnp.float32) / halfway)
    angles = offsets[:, None] * frequency[None, :]
    return (documents, places, validity, jnp.cos(angles)[:, None, :], jnp.sin(angles)[:, None, :])


def rotate(values, cos_table, sin_table):
    halfway = values.shape[-1] // 2
    former = values[..., :halfway]
    latter = values[..., halfway:]
    return jnp.concatenate(
        [former * cos_table - latter * sin_table, latter * cos_table + former * sin_table], axis=-1
    )


def rotate_back(grads, cos_table, sin_table):
    halfway = grads.shape[-1] // 2
    former = grads[..., :halfway]
    latter = grads[..., halfway:]
    return jnp.concatenate(
        [former * cos_table + latter * sin_table, latter * cos_table - former * sin_table], axis=-1
    )


def allowed_pairs(query_docs, query_places, query_valid, documents, places):
    causal = (
        (query_docs[:, None] == documents[None, :])
        & (places[None, :] <= query_places[:, None])
        & query_valid[:, None]
    )
    return causal | (places[None, :] == query_places[:, None])


def attend(queries, keys_rot, values_low, geometry):
    documents, places, validity = (geometry[0], geometry[1], geometry[2])
    bucket, head_count, width = queries.shape
    block_rows = min(512, bucket)
    block_count = bucket // block_rows
    scaling = width ** (-0.5)

    def attend_block(item):
        query_block, query_docs, query_places, query_valid = item
        allowed = allowed_pairs(query_docs, query_places, query_valid, documents, places)
        scores = (
            jnp.einsum("qhd,khd->hqk", query_block, keys_rot, preferred_element_type=jnp.float32)
            * scaling
        )
        masked = jnp.where(allowed[None], scores, -1000000000.0)
        maximum = jnp.max(masked, axis=-1, keepdims=True)
        weights = jnp.exp(masked - maximum)
        totals = jnp.sum(weights, axis=-1, keepdims=True)
        probs = (weights / totals).astype(jnp.bfloat16)
        result = jnp.einsum("hqk,khd->qhd", probs, values_low, preferred_element_type=jnp.float32)
        return (result, (maximum + jnp.log(totals))[..., 0])

    items = (
        queries.reshape(block_count, block_rows, head_count, width),
        documents.reshape(block_count, block_rows),
        places.reshape(block_count, block_rows),
        validity.reshape(block_count, block_rows),
    )
    result, logsum = lax.map(attend_block, items)
    return (result.reshape(bucket, head_count, width), logsum)


def attend_back(queries, keys_rot, values_low, geometry, logsum, grads_out):
    documents, places, validity = (geometry[0], geometry[1], geometry[2])
    bucket, head_count, width = queries.shape
    block_rows = min(512, bucket)
    block_count = bucket // block_rows
    scaling = width ** (-0.5)

    def step_block(carry, item):
        keys_total, values_total = carry
        query_block, query_docs, query_places, query_valid, block_log, grad_block = item
        allowed = allowed_pairs(query_docs, query_places, query_valid, documents, places)
        scores = (
            jnp.einsum("qhd,khd->hqk", query_block, keys_rot, preferred_element_type=jnp.float32)
            * scaling
        )
        masked = jnp.where(allowed[None], scores, -1000000000.0)
        probs = jnp.exp(masked - block_log[..., None])
        prob_grads = jnp.einsum(
            "qhd,khd->hqk", grad_block, values_low, preferred_element_type=jnp.float32
        )
        values_total = values_total + jnp.einsum(
            "hqk,qhd->khd",
            probs.astype(jnp.bfloat16),
            grad_block,
            preferred_element_type=jnp.float32,
        )
        inner = jnp.sum(probs * prob_grads, axis=-1, keepdims=True)
        raw_grads = (probs * (prob_grads - inner) * scaling).astype(jnp.bfloat16)
        query_part = jnp.einsum(
            "hqk,khd->qhd", raw_grads, keys_rot, preferred_element_type=jnp.float32
        )
        keys_total = keys_total + jnp.einsum(
            "hqk,qhd->khd", raw_grads, query_block, preferred_element_type=jnp.float32
        )
        return ((keys_total, values_total), query_part)

    zeros = jnp.zeros((bucket, head_count, width), jnp.float32)
    items = (
        queries.reshape(block_count, block_rows, head_count, width),
        documents.reshape(block_count, block_rows),
        places.reshape(block_count, block_rows),
        validity.reshape(block_count, block_rows),
        logsum,
        grads_out.reshape(block_count, block_rows, head_count, width),
    )
    (keys_total, values_total), query_parts = lax.scan(step_block, (zeros, zeros), items)
    return (query_parts.reshape(bucket, head_count, width), keys_total, values_total)


def fetch_weights(query, keys, values, output, gate, upward, downward):
    return (
        lax.all_gather(query, "af", axis=0, tiled=True),
        lax.all_gather(keys, "af", axis=0, tiled=True),
        lax.all_gather(values, "af", axis=0, tiled=True),
        lax.all_gather(output, "af", axis=0, tiled=True),
        lax.all_gather(gate, "af", axis=0, tiled=True),
        lax.all_gather(upward, "af", axis=0, tiled=True),
        lax.all_gather(downward, "af", axis=0, tiled=True),
    )


def spread_rows(normed):
    return lax.all_gather(normed, "ha", axis=0, tiled=True)


def spread_grads(grads):
    return lax.all_gather(grads, "ha", axis=0, tiled=True)


def branch_rows(source, weight):
    return lax.psum_scatter(
        against(source, weight).astype(jnp.bfloat16), "ha", scatter_dimension=0, tiled=True
    ).astype(jnp.float32)


def attention_branch(flat_attended, weight):
    return branch_rows(flat_attended, weight)


def input_rows(sources, weights, row_count):
    summed = jnp.zeros((lax.axis_size("ha") * row_count, weights[0].shape[0]), jnp.float32)
    for source, weight in zip(sources, weights):
        summed = summed + against(source, weight)
    return lax.psum_scatter(
        summed.astype(jnp.bfloat16), "ha", scatter_dimension=0, tiled=True
    ).astype(jnp.float32)


def attention_inputs(current, gain, fetched, geometry, first_values, gathered):
    gathered = spread_rows(normalize(current, gain).astype(jnp.bfloat16))
    bucket = gathered.shape[0]
    query_raw = product(gathered, fetched[0])
    keys_raw = product(gathered, fetched[1])
    values_raw = product(gathered, fetched[2])
    mixed = values_raw if first_values is None else 0.5 * values_raw + 0.5 * first_values
    queries = rotate(query_raw.reshape(bucket, -1, HD), geometry[3], geometry[4]).astype(
        jnp.bfloat16
    )
    keys_rot = rotate(keys_raw.reshape(bucket, -1, HD), geometry[3], geometry[4]).astype(
        jnp.bfloat16
    )
    values_low = mixed.reshape(bucket, -1, HD).astype(jnp.bfloat16)
    attended, logsum = attend(queries, keys_rot, values_low, geometry)
    return (gathered, values_raw, queries, keys_rot, values_low, attended, logsum)


def ffn_inputs(current, gain, fetched, gathered):
    gathered = spread_rows(normalize(current, gain).astype(jnp.bfloat16))
    gate_raw = product(gathered, fetched[4])
    upward_raw = product(gathered, fetched[5])
    hidden = (jax.nn.silu(gate_raw) * upward_raw).astype(jnp.bfloat16)
    return (gathered, gate_raw, upward_raw, hidden)


def per_device(
    block_input,
    lengths,
    cotangent,
    attngain_early,
    query_early,
    keys_early,
    values_early,
    output_early,
    ffngain_early,
    gate_early,
    upward_early,
    down_early,
    attngain_later,
    query_later,
    keys_later,
    values_later,
    output_later,
    ffngain_later,
    gate_later,
    upward_later,
    down_later,
):
    row_count = block_input.shape[0]
    bucket = row_count * lax.axis_size("ha")
    geometry = layout(lengths[0], bucket)
    layers = (
        (
            attngain_early,
            query_early,
            keys_early,
            values_early,
            output_early,
            ffngain_early,
            gate_early,
            upward_early,
            down_early,
        ),
        (
            attngain_later,
            query_later,
            keys_later,
            values_later,
            output_later,
            ffngain_later,
            gate_later,
            upward_later,
            down_later,
        ),
    )
    current = block_input.astype(jnp.float32)
    stored = []
    first_values = None
    for layer_index in range(2):
        params = layers[layer_index]
        fetched = fetch_weights(
            params[1], params[2], params[3], params[4], params[6], params[7], params[8]
        )
        gathered_attn, values_raw, queries, keys_rot, values_low, attended, logsum = (
            attention_inputs(current, params[0], fetched, geometry, first_values, None)
        )
        flat_attended = attended.reshape(bucket, -1).astype(jnp.bfloat16)
        middle = current + attention_branch(flat_attended, fetched[3])
        gathered_ffn, gate_raw, upward_raw, hidden = ffn_inputs(middle, params[5], fetched, None)
        layer_out = middle + branch_rows(hidden, fetched[6])
        saved_rows = (None, None)
        stored.append((current, middle, saved_rows))
        if layer_index == 0:
            first_values = values_raw
        current = layer_out
    block_output = current.astype(jnp.bfloat16)
    grads = cotangent.astype(jnp.float32)
    carried_values = None
    matrix_grads = [None, None]
    gain_grads = [None, None]
    for layer_index in (1, 0):
        params = layers[layer_index]
        fetched = fetch_weights(
            params[1], params[2], params[3], params[4], params[6], params[7], params[8]
        )
        start_rows, middle, saved_rows = stored[layer_index]
        earlier = first_values if layer_index == 1 else None
        gathered_attn, values_raw, queries, keys_rot, values_low, attended, logsum = (
            attention_inputs(start_rows, params[0], fetched, geometry, earlier, saved_rows[0])
        )
        gathered_ffn, gate_raw, upward_raw, hidden = ffn_inputs(
            middle, params[5], fetched, saved_rows[1]
        )
        ffn_grads = spread_grads(grads.astype(jnp.bfloat16))
        hidden_grads = product(ffn_grads, fetched[6])
        down_grad = across(ffn_grads, hidden)
        sigmoid_gate = jax.nn.sigmoid(gate_raw)
        gate_grads = (
            hidden_grads * upward_raw * sigmoid_gate * (1.0 + gate_raw * (1.0 - sigmoid_gate))
        ).astype(jnp.bfloat16)
        upward_grads = (hidden_grads * gate_raw * sigmoid_gate).astype(jnp.bfloat16)
        gate_grad = across(gathered_ffn, gate_grads)
        upward_grad = across(gathered_ffn, upward_grads)
        normed_grads = input_rows((gate_grads, upward_grads), (fetched[4], fetched[5]), row_count)
        middle_part, ffngain_grad = norm_back(middle, params[5], normed_grads)
        middle_grads = grads + middle_part
        attn_grads = spread_grads(middle_grads.astype(jnp.bfloat16))
        flat_attended = attended.reshape(bucket, -1).astype(jnp.bfloat16)
        output_grad = across(attn_grads, flat_attended)
        attended_grads = (
            product(attn_grads, fetched[3]).astype(jnp.bfloat16).reshape(bucket, -1, HD)
        )
        query_rot_grads, keys_rot_grads, values_low_grads = attend_back(
            queries, keys_rot, values_low, geometry, logsum, attended_grads
        )
        if layer_index == 1:
            values_total = 0.5 * values_low_grads
            carried_values = 0.5 * values_low_grads
        else:
            values_total = values_low_grads + carried_values
        values_round = values_total.reshape(bucket, -1).astype(jnp.bfloat16)
        query_round = (
            rotate_back(query_rot_grads, geometry[3], geometry[4])
            .reshape(bucket, -1)
            .astype(jnp.bfloat16)
        )
        keys_round = (
            rotate_back(keys_rot_grads, geometry[3], geometry[4])
            .reshape(bucket, -1)
            .astype(jnp.bfloat16)
        )
        query_grad = across(gathered_attn, query_round)
        keys_grad = across(gathered_attn, keys_round)
        values_grad = across(gathered_attn, values_round)
        normed_first = input_rows(
            (query_round, keys_round, values_round), (fetched[0], fetched[1], fetched[2]), row_count
        )
        start_part, attngain_grad = norm_back(start_rows, params[0], normed_first)
        grads = middle_grads + start_part
        matrices = (
            query_grad,
            keys_grad,
            values_grad,
            output_grad,
            gate_grad,
            upward_grad,
            down_grad,
        )
        matrices = (
            lax.psum_scatter(
                query_grad.astype(jnp.bfloat16), "af", scatter_dimension=0, tiled=True
            ).astype(jnp.float32),
            lax.psum_scatter(
                keys_grad.astype(jnp.bfloat16), "af", scatter_dimension=0, tiled=True
            ).astype(jnp.float32),
            lax.psum_scatter(
                values_grad.astype(jnp.bfloat16), "af", scatter_dimension=0, tiled=True
            ).astype(jnp.float32),
            lax.psum_scatter(
                output_grad.astype(jnp.bfloat16), "af", scatter_dimension=0, tiled=True
            ).astype(jnp.float32),
            lax.psum_scatter(
                gate_grad.astype(jnp.bfloat16), "af", scatter_dimension=0, tiled=True
            ).astype(jnp.float32),
            lax.psum_scatter(
                upward_grad.astype(jnp.bfloat16), "af", scatter_dimension=0, tiled=True
            ).astype(jnp.float32),
            lax.psum_scatter(
                down_grad.astype(jnp.bfloat16), "af", scatter_dimension=0, tiled=True
            ).astype(jnp.float32),
        )
        matrix_grads[layer_index] = matrices
        gain_grads[layer_index] = (attngain_grad, ffngain_grad)
    gain_totals = lax.psum(
        (gain_grads[0][0], gain_grads[0][1], gain_grads[1][0], gain_grads[1][1]), ("af", "ha")
    )
    early_mats = matrix_grads[0]
    later_mats = matrix_grads[1]
    return (
        block_output,
        grads,
        gain_totals[0],
        early_mats[0],
        early_mats[1],
        early_mats[2],
        early_mats[3],
        gain_totals[1],
        early_mats[4],
        early_mats[5],
        early_mats[6],
        gain_totals[2],
        later_mats[0],
        later_mats[1],
        later_mats[2],
        later_mats[3],
        gain_totals[3],
        later_mats[4],
        later_mats[5],
        later_mats[6],
    )


def solution(mesh):
    in_specs = (
        P(("af", "ha"), None),
        P("af", None),
        P(("af", "ha"), None),
        P(),
        P("af", "ha"),
        P("af", "ha"),
        P("af", "ha"),
        P("af", "ha"),
        P(),
        P("af", "ha"),
        P("af", "ha"),
        P("af", "ha"),
        P(),
        P("af", "ha"),
        P("af", "ha"),
        P("af", "ha"),
        P("af", "ha"),
        P(),
        P("af", "ha"),
        P("af", "ha"),
        P("af", "ha"),
    )
    out_specs = (
        P(("af", "ha"), None),
        P(("af", "ha"), None),
        P(),
        P("af", "ha"),
        P("af", "ha"),
        P("af", "ha"),
        P("af", "ha"),
        P(),
        P("af", "ha"),
        P("af", "ha"),
        P("af", "ha"),
        P(),
        P("af", "ha"),
        P("af", "ha"),
        P("af", "ha"),
        P("af", "ha"),
        P(),
        P("af", "ha"),
        P("af", "ha"),
        P("af", "ha"),
    )
    return jax.shard_map(
        per_device, mesh=mesh, in_specs=in_specs, out_specs=out_specs, check_vma=False
    )
```

profile of v0, /device:TPU:0, one launch (start us, length us, event | category | flops | bytes accessed | tf_op | source)
XLA Modules:
  0.0 1233.1 jit_solution(5812060965833601104)
XLA Ops:
  13.0 16.8 %all_gather.86 = bf16[1024,256]{1,0:T(8,128)(2,1)S(1)} all-gather(bf16[128,256]{1,0:T(8,128)(2,1)} %param.25), channel_id=1, replica_groups=mesh['af'=8,'ha'=4] {'af'}, dimensions={0}, use_global_device_ids=true | all-gather | bytes 589824 | tf_op jit(solution)/shard_map/all_gather | solution.py:169
  29.8 14.9 %all_gather.87 = bf16[1024,256]{1,0:T(8,128)(2,1)S(1)} all-gather(bf16[128,256]{1,0:T(8,128)(2,1)} %param.26), channel_id=1, replica_groups=mesh['af'=8,'ha'=4] {'af'}, dimensions={0}, use_global_device_ids=true | all-gather | bytes 589824 | tf_op jit(solution)/shard_map/all_gather | solution.py:170
  44.8 15.1 %all_gather.85 = bf16[1024,256]{1,0:T(8,128)(2,1)S(1)} all-gather(bf16[128,256]{1,0:T(8,128)(2,1)S(1)} %copy-done.51), channel_id=1, replica_groups=mesh['af'=8,'ha'=4] {'af'}, dimensions={0}, use_global_device_ids=true | all-gather | bytes 589824 | tf_op jit(solution)/shard_map/all_gather | solution.py:171
  59.9 15.1 %all_gather.88 = bf16[1024,256]{1,0:T(8,128)(2,1)S(1)} all-gather(bf16[128,256]{1,0:T(8,128)(2,1)S(1)} %copy-done.52), channel_id=1, replica_groups=mesh['af'=8,'ha'=4] {'af'}, dimensions={0}, use_global_device_ids=true | all-gather | bytes 589824 | tf_op jit(solution)/shard_map/all_gather | solution.py:172
  84.8 28.7 %reduce-scatter.35.cloned.1.call-done = bf16[128,1024]{1,0:T(8,128)(2,1)} async-done(((bf16[512,1024]{1,0:T(8,128)(2,1)}), bf16[128,1024]{1,0:T(8,128)(2,1)}) %reduce-scatter.35.cloned.1.call-update) | async-done | bytes 262160 | tf_op jit(solution)/shard_map/reduce_scatter | solution.py:188
  117.9 25.2 %all-gather.17.cloned.1.call-done = bf16[512,1024]{1,0:T(8,128)(2,1)} async-done(((bf16[128,1024]{1,0:T(8,128)(2,1)}), bf16[512,1024]{1,0:T(8,128)(2,1)}) %all-gather.17.cloned.1.call-update) | async-done | bytes 1048592 | tf_op jit(solution)/shard_map/all_gather | solution.py:180
  143.0 3.8 fusion.131
  146.9 23.9 %all-gather.21.cloned.1.call-done = bf16[1024,704]{0,1:T(8,128)(2,1)} async-done(((bf16[128,704]{0,1:T(8,128)(2,1)}), bf16[1024,704]{0,1:T(8,128)(2,1)}) %all-gather.21.cloned.1.call-update) | async-done | bytes 1441808 | tf_op jit(solution)/shard_map/all_gather | solution.py:174
  170.8 4.2 multiply_convert_fusion.7
  175.0 22.6 %all-gather.23.cloned.1.call-done = bf16[1024,704]{0,1:T(8,128)(2,1)} async-done(((bf16[128,704]{0,1:T(8,128)(2,1)}), bf16[1024,704]{0,1:T(8,128)(2,1)}) %all-gather.23.cloned.1.call-update) | async-done | bytes 1441808 | tf_op jit(solution)/shard_map/all_gather | solution.py:175
  197.6 3.6 convolution_convert_fusion.8
  201.3 26.7 %reduce-scatter.37.cloned.1.call-done = bf16[128,1024]{1,0:T(8,128)(2,1)} async-done(((bf16[512,1024]{1,0:T(8,128)(2,1)}), bf16[128,1024]{1,0:T(8,128)(2,1)}) %reduce-scatter.37.cloned.1.call-update) | async-done | bytes 262160 | tf_op jit(solution)/shard_map/reduce_scatter | solution.py:188
  230.1 15.9 %all_gather.95 = bf16[1024,256]{1,0:T(8,128)(2,1)} all-gather(bf16[128,256]{1,0:T(8,128)(2,1)S(1)} %copy-done.53), channel_id=1, replica_groups=mesh['af'=8,'ha'=4] {'af'}, dimensions={0}, use_global_device_ids=true | all-gather | bytes 589824 | tf_op jit(solution)/shard_map/all_gather | solution.py:169
  245.9 16.3 %all_gather.96 = bf16[1024,256]{1,0:T(8,128)(2,1)} all-gather(bf16[128,256]{1,0:T(8,128)(2,1)S(1)} %copy-done.54), channel_id=1, replica_groups=mesh['af'=8,'ha'=4] {'af'}, dimensions={0}, use_global_device_ids=true | all-gather | bytes 589824 | tf_op jit(solution)/shard_map/all_gather | solution.py:170
  262.2 15.9 %all_gather.94 = bf16[1024,256]{1,0:T(8,128)(2,1)} all-gather(bf16[128,256]{1,0:T(8,128)(2,1)S(1)} %copy-done.55), channel_id=1, replica_groups=mesh['af'=8,'ha'=4] {'af'}, dimensions={0}, use_global_device_ids=true | all-gather | bytes 589824 | tf_op jit(solution)/shard_map/all_gather | solution.py:171
  278.2 16.0 %all_gather.97 = bf16[1024,256]{1,0:T(8,128)(2,1)} all-gather(bf16[128,256]{1,0:T(8,128)(2,1)S(1)} %copy-done.56), channel_id=1, replica_groups=mesh['af'=8,'ha'=4] {'af'}, dimensions={0}, use_global_device_ids=true | all-gather | bytes 589824 | tf_op jit(solution)/shard_map/all_gather | solution.py:172
  304.0 27.2 %reduce-scatter.39.cloned.1.call-done = bf16[128,1024]{1,0:T(8,128)(2,1)} async-done(((bf16[512,1024]{1,0:T(8,128)(2,1)}), bf16[128,1024]{1,0:T(8,128)(2,1)}) %reduce-scatter.39.cloned.1.call-update) | async-done | bytes 262160 | tf_op jit(solution)/shard_map/reduce_scatter | solution.py:188
  335.9 24.7 %all-gather.27.cloned.1.call-done = bf16[512,1024]{1,0:T(8,128)(2,1)} async-done(((bf16[128,1024]{1,0:T(8,128)(2,1)}), bf16[512,1024]{1,0:T(8,128)(2,1)}) %all-gather.27.cloned.1.call-update) | async-done | bytes 1048592 | tf_op jit(solution)/shard_map/all_gather | solution.py:180
  360.7 3.7 fusion.135
  364.4 24.0 %all-gather.29.cloned.1.call-done = bf16[1024,704]{0,1:T(8,128)(2,1)} async-done(((bf16[128,704]{0,1:T(8,128)(2,1)}), bf16[1024,704]{0,1:T(8,128)(2,1)}) %all-gather.29.cloned.1.call-update) | async-done | bytes 1441808 | tf_op jit(solution)/shard_map/all_gather | solution.py:173
  388.4 3.7 fusion.134
  392.1 23.5 %all-gather.35.cloned.1.call-done = bf16[512,1024]{1,0:T(8,128)(2,1)} async-done(((bf16[128,1024]{1,0:T(8,128)(2,1)}), bf16[512,1024]{1,0:T(8,128)(2,1)}) %all-gather.35.cloned.1.call-update) | async-done | bytes 1048592 | tf_op jit(solution)/shard_map/all_gather | solution.py:184
  415.6 27.8 %all-gather.33.cloned.1.call-done = bf16[1024,704]{0,1:T(8,128)(2,1)} async-done(((bf16[128,704]{0,1:T(8,128)(2,1)}), bf16[1024,704]{0,1:T(8,128)(2,1)}) %all-gather.33.cloned.1.call-update) | async-done | bytes 1441808 | tf_op jit(solution)/shard_map/all_gather | solution.py:175
  443.4 5.0 multiply_convert_fusion.4
  452.4 26.7 %reduce-scatter.43.cloned.1.call-done = bf16[128,1024]{1,0:T(8,128)(2,1)} async-done(((bf16[512,1024]{1,0:T(8,128)(2,1)}), bf16[128,1024]{1,0:T(8,128)(2,1)}) %reduce-scatter.43.cloned.1.call-update) | async-done | bytes 262160 | tf_op jit(solution)/shard_map/reduce_scatter | solution.py:201
  484.9 25.2 %all-gather.37.cloned.1.call-done = bf16[512,1024]{1,0:T(8,128)(2,1)} async-done(((bf16[128,1024]{1,0:T(8,128)(2,1)}), bf16[512,1024]{1,0:T(8,128)(2,1)}) %all-gather.37.cloned.1.call-update) | async-done | bytes 1048592 | tf_op jit(solution)/shard_map/all_gather | solution.py:184
  512.0 3.8 fusion.137
  517.5 8.8 fusion.51
  526.3 8.8 fusion.54
  539.9 3.6 convolution_convert_fusion.6
  543.6 24.1 %reduce-scatter.45.cloned.1.call-done = bf16[128,1024]{1,0:T(8,128)(2,1)} async-done(((bf16[512,1024]{1,0:T(8,128)(2,1)}), bf16[128,1024]{1,0:T(8,128)(2,1)}) %reduce-scatter.45.cloned.1.call-update) | async-done | bytes 262160 | tf_op jit(solution)/shard_map/reduce_scatter | solution.py:201
  570.0 28.6 %reduce-scatter.41.cloned.1.call-done = bf16[128,1024]{1,0:T(8,128)(2,1)} async-done(((bf16[512,1024]{1,0:T(8,128)(2,1)}), bf16[128,1024]{1,0:T(8,128)(2,1)}) %reduce-scatter.41.cloned.1.call-update) | async-done | bytes 262160 | tf_op jit(solution)/shard_map/reduce_scatter | solution.py:188
  598.6 2.6 fusion.123
  601.3 26.7 %all-gather.39.cloned.1.call-done = bf16[512,1024]{1,0:T(8,128)(2,1)} async-done(((bf16[128,1024]{1,0:T(8,128)(2,1)}), bf16[512,1024]{1,0:T(8,128)(2,1)}) %all-gather.39.cloned.1.call-update) | async-done | bytes 1048592 | tf_op jit(solution)/shard_map/all_gather | solution.py:184
  628.1 4.0 multiply_convert_fusion.2
  636.3 27.6 %reduce-scatter.47.cloned.1.call-done = bf16[128,1024]{1,0:T(8,128)(2,1)} async-done(((bf16[512,1024]{1,0:T(8,128)(2,1)}), bf16[128,1024]{1,0:T(8,128)(2,1)}) %reduce-scatter.47.cloned.1.call-update) | async-done | bytes 262160 | tf_op jit(solution)/shard_map/reduce_scatter | solution.py:201
  667.1 3.5 fusion.44
  673.2 3.5 convolution_convert_fusion
  679.4 3.5 convolution_convert_fusion.1
  682.8 2.6 copy.79
  693.3 3.5 convolution_convert_fusion.2
  696.8 2.7 copy.77
  699.5 3.1 convolution_convert_fusion.3
  702.7 2.6 copy.75
  705.4 3.1 convolution_convert_fusion.4
  715.7 3.2 fusion.65
  720.1 2.8 fusion.141
  723.3 8.4 fusion.45
  731.7 9.1 fusion.48
  751.9 12.5 %reduce-scatter.75.cloned.1.call-done = bf16[128,704]{1,0:T(8,128)(2,1)} async-done(((bf16[1024,704]{1,0:T(8,128)(2,1)}), bf16[128,704]{1,0:T(8,128)(2,1)}) %reduce-scatter.75.cloned.1.call-update) | async-done | bytes 180240
  766.2 32.7 %reduce-scatter.73.cloned.1.call-done = bf16[128,704]{1,0:T(8,128)(2,1)} async-done(((bf16[1024,704]{1,0:T(8,128)(2,1)}), bf16[128,704]{1,0:T(8,128)(2,1)}) %reduce-scatter.73.cloned.1.call-update) | async-done | bytes 180240
  800.7 29.7 %reduce-scatter.65.cloned.1.call-done = bf16[128,256]{1,0:T(8,128)(2,1)} async-done(((bf16[1024,256]{1,0:T(8,128)(2,1)}), bf16[128,256]{1,0:T(8,128)(2,1)}) %reduce-scatter.65.cloned.1.call-update) | async-done | bytes 65552 | tf_op jit(solution)/shard_map/reduce_scatter | solution.py:385
  831.9 29.8 %reduce-scatter.63.cloned.1.call-done = bf16[128,256]{1,0:T(8,128)(2,1)} async-done(((bf16[1024,256]{1,0:T(8,128)(2,1)}), bf16[128,256]{1,0:T(8,128)(2,1)}) %reduce-scatter.63.cloned.1.call-update) | async-done | bytes 65552 | tf_op jit(solution)/shard_map/reduce_scatter | solution.py:382
  863.3 30.0 %reduce-scatter.61.cloned.1.call-done = bf16[128,256]{1,0:T(8,128)(2,1)} async-done(((bf16[1024,256]{1,0:T(8,128)(2,1)}), bf16[128,256]{1,0:T(8,128)(2,1)}) %reduce-scatter.61.cloned.1.call-update) | async-done | bytes 65552 | tf_op jit(solution)/shard_map/reduce_scatter | solution.py:379
  894.8 29.8 %reduce-scatter.59.cloned.1.call-done = bf16[128,256]{1,0:T(8,128)(2,1)} async-done(((bf16[1024,256]{1,0:T(8,128)(2,1)}), bf16[128,256]{1,0:T(8,128)(2,1)}) %reduce-scatter.59.cloned.1.call-update) | async-done | bytes 65552 | tf_op jit(solution)/shard_map/reduce_scatter | solution.py:376
  926.1 33.0 %reduce-scatter.71.cloned.1.call-done = bf16[128,704]{1,0:T(8,128)(2,1)} async-done(((bf16[1024,704]{1,0:T(8,128)(2,1)}), bf16[128,704]{1,0:T(8,128)(2,1)}) %reduce-scatter.71.cloned.1.call-update) | async-done | bytes 180240
  960.9 32.5 %reduce-scatter.69.cloned.1.call-done = bf16[128,704]{1,0:T(8,128)(2,1)} async-done(((bf16[1024,704]{1,0:T(8,128)(2,1)}), bf16[128,704]{1,0:T(8,128)(2,1)}) %reduce-scatter.69.cloned.1.call-update) | async-done | bytes 180240
  995.2 32.7 %reduce-scatter.67.cloned.1.call-done = bf16[128,704]{1,0:T(8,128)(2,1)} async-done(((bf16[1024,704]{1,0:T(8,128)(2,1)}), bf16[128,704]{1,0:T(8,128)(2,1)}) %reduce-scatter.67.cloned.1.call-update) | async-done | bytes 180240
  1029.8 29.5 %reduce-scatter.57.cloned.1.call-done = bf16[128,256]{1,0:T(8,128)(2,1)} async-done(((bf16[1024,256]{1,0:T(8,128)(2,1)}), bf16[128,256]{1,0:T(8,128)(2,1)}) %reduce-scatter.57.cloned.1.call-update) | async-done | bytes 65552 | tf_op jit(solution)/shard_map/reduce_scatter | solution.py:385
  1060.8 29.6 %reduce-scatter.55.cloned.1.call-done = bf16[128,256]{1,0:T(8,128)(2,1)} async-done(((bf16[1024,256]{1,0:T(8,128)(2,1)}), bf16[128,256]{1,0:T(8,128)(2,1)}) %reduce-scatter.55.cloned.1.call-update) | async-done | bytes 65552 | tf_op jit(solution)/shard_map/reduce_scatter | solution.py:382
  1091.9 30.3 %reduce-scatter.51.cloned.1.call-done = bf16[128,256]{1,0:T(8,128)(2,1)} async-done(((bf16[1024,256]{1,0:T(8,128)(2,1)}), bf16[128,256]{1,0:T(8,128)(2,1)}) %reduce-scatter.51.cloned.1.call-update) | async-done | bytes 65552 | tf_op jit(solution)/shard_map/reduce_scatter | solution.py:376
  1123.7 29.8 %reduce-scatter.53.cloned.1.call-done = bf16[128,256]{1,0:T(8,128)(2,1)} async-done(((bf16[1024,256]{1,0:T(8,128)(2,1)}), bf16[128,256]{1,0:T(8,128)(2,1)}) %reduce-scatter.53.cloned.1.call-update) | async-done | bytes 65552 | tf_op jit(solution)/shard_map/reduce_scatter | solution.py:379
  1155.0 27.3 %reduce-scatter.49.cloned.1.call-done = bf16[128,1024]{1,0:T(8,128)(2,1)} async-done(((bf16[512,1024]{1,0:T(8,128)(2,1)}), bf16[128,1024]{1,0:T(8,128)(2,1)}) %reduce-scatter.49.cloned.1.call-update) | async-done | bytes 262160 | tf_op jit(solution)/shard_map/reduce_scatter | solution.py:201
  1183.5 39.6 %all-reduce = (f32[1024]{0:T(1024)}, f32[1024]{0:T(1024)}, f32[1024]{0:T(1024)}, f32[1024]{0:T(1024)}) all-reduce(f32[1024]{0:T(1024)S(1)} %get-tuple-element.186, f32[1024]{0:T(1024)S(1)} %get-tuple-element.184, f32[1024]{0:T(1024)S(1)} %copy-done.67, f32[1024]{0:T(1024)S(1)} %copy-done.66), channel_id=1, replica_groups=mesh['af'=8,'ha'=4] {'af','ha'}, use_global_device_ids=true, to_apply=%region_26.27 | all-reduce | flops 4096 | bytes 32768 | tf_op jit(solution)/shard_map/psum | solution.py:400
  (351 shorter events, 120.2 us)
Async XLA Ops:
  8.0 36.7 %copy-start.51 = (bf16[128,256]{1,0:T(8,128)(2,1)S(1)}, bf16[128,256]{1,0:T(8,128)(2,1)}, u32[]{:S(2)}) copy-start(bf16[128,256]{1,0:T(8,128)(2,1)} %param.27) | copy-start | bytes 196612
  8.0 51.9 %copy-start.52 = (bf16[128,256]{1,0:T(8,128)(2,1)S(1)}, bf16[128,256]{1,0:T(8,128)(2,1)}, u32[]{:S(2)}) copy-start(bf16[128,256]{1,0:T(8,128)(2,1)} %param.28) | copy-start | bytes 196612
  8.0 67.3 %all-gather.15.cloned.1.call-start = ((), (), s32[]{:S(2)}) async-start(), calls=%async_computation.22 | async-start | bytes 1310720 | tf_op jit(solution)/shard_map/all_gather | solution.py:180
  11.0 102.5 %reduce-scatter.35.cloned.1.call-start = ((), (), s32[]{:S(2)}) async-start(), calls=%async_computation.23 | async-start | bytes 1310720 | tf_op jit(solution)/shard_map/reduce_scatter | solution.py:188
  29.8 47.8 %copy-start.16 = (bf16[1024,256]{1,0:T(8,128)(2,1)}, bf16[1024,256]{1,0:T(8,128)(2,1)S(1)}, u32[]{:S(2)}) copy-start(bf16[1024,256]{1,0:T(8,128)(2,1)S(1)} %all_gather.86) | copy-start | bytes 1572868
  44.8 32.9 %copy-start.18 = (bf16[1024,256]{1,0:T(8,128)(2,1)}, bf16[1024,256]{1,0:T(8,128)(2,1)S(1)}, u32[]{:S(2)}) copy-start(bf16[1024,256]{1,0:T(8,128)(2,1)S(1)} %all_gather.87) | copy-start | bytes 1572868
  82.6 33.8 %copy-start.32 = (bf16[4,64,512]{2,1,0:T(8,128)(2,1)}, bf16[4,64,512]{2,1,0:T(8,128)(2,1)S(1)}, u32[]{:S(2)}) copy-start(bf16[4,64,512]{2,1,0:T(8,128)(2,1)S(1)} %fusion.69) | copy-start | bytes 786436
  82.6 30.9 %copy-start.2 = (bf16[128,1024]{1,0:T(8,128)(2,1)S(1)}, bf16[128,1024]{1,0:T(8,128)(2,1)}, u32[]{:S(2)}) copy-start(bf16[128,1024]{1,0:T(8,128)(2,1)} %param.21) | copy-start | bytes 786436
  82.6 32.0 %copy-start.50 = (f32[1024]{0:T(1024)S(1)}, f32[1024]{0:T(1024)}, u32[]{:S(2)}) copy-start(f32[1024]{0:T(1024)} %param.29) | copy-start | bytes 12292
  84.2 33.7 %all-gather.19.cloned.1.call-start = ((), (), s32[]{:S(2)}) async-start(), calls=%async_computation.25 | async-start | bytes 1622016 | tf_op jit(solution)/shard_map/all_gather | solution.py:173
  84.8 58.3 %all-gather.17.cloned.1.call-start = ((), (), s32[]{:S(2)}) async-start(), calls=%async_computation.24 | async-start | bytes 1310720 | tf_op jit(solution)/shard_map/all_gather | solution.py:180
  114.7 32.2 %copy-start.68 = (f32[128]{0:T(128)}, f32[128]{0:T(128)S(1)}, u32[]{:S(2)}) copy-start(f32[128]{0:T(128)S(1)} %add_rsqrt_fusion.2) | copy-start | bytes 1540
  116.5 54.3 %all-gather.21.cloned.1.call-start = ((), (), s32[]{:S(2)}) async-start(), calls=%async_computation.26 | async-start | bytes 1622016 | tf_op jit(solution)/shard_map/all_gather | solution.py:174
  117.1 80.5 %all-gather.23.cloned.1.call-start = ((), (), s32[]{:S(2)}) async-start(), calls=%async_computation.27 | async-start | bytes 1622016 | tf_op jit(solution)/shard_map/all_gather | solution.py:175
  117.8 110.2 %reduce-scatter.37.cloned.1.call-start = ((), (), s32[]{:S(2)}) async-start(), calls=%async_computation.28 | async-start | bytes 1310720 | tf_op jit(solution)/shard_map/reduce_scatter | solution.py:188
  143.0 27.8 %copy-start.81 = (bf16[512,1024]{1,0:T(8,128)(2,1)S(1)}, bf16[512,1024]{1,0:T(8,128)(2,1)}, u32[]{:S(2)}) copy-start(bf16[512,1024]{1,0:T(8,128)(2,1)} %all-gather.17.cloned.1.call-done) | copy-start | bytes 3145732
  197.6 30.4 %copy-start.6 = (bf16[128,1024]{1,0:T(8,128)(2,1)S(1)}, bf16[128,1024]{1,0:T(8,128)(2,1)}, u32[]{:S(2)}) copy-start(bf16[128,1024]{1,0:T(8,128)(2,1)} %reduce-scatter.35.cloned.1.call-done) | copy-start | bytes 786436
  201.2 28.0 %copy-start.57 = (f32[1024]{0:T(1024)S(1)}, f32[1024]{0:T(1024)}, u32[]{:S(2)}) copy-start(f32[1024]{0:T(1024)} %param.33) | copy-start | bytes 12292
  201.2 28.9 %copy-start.53 = (bf16[128,256]{1,0:T(8,128)(2,1)S(1)}, bf16[128,256]{1,0:T(8,128)(2,1)}, u32[]{:S(2)}) copy-start(bf16[128,256]{1,0:T(8,128)(2,1)} %param.34) | copy-start | bytes 196612
  201.2 44.8 %copy-start.54 = (bf16[128,256]{1,0:T(8,128)(2,1)S(1)}, bf16[128,256]{1,0:T(8,128)(2,1)}, u32[]{:S(2)}) copy-start(bf16[128,256]{1,0:T(8,128)(2,1)} %param.35) | copy-start | bytes 196612
  201.2 61.1 %copy-start.55 = (bf16[128,256]{1,0:T(8,128)(2,1)S(1)}, bf16[128,256]{1,0:T(8,128)(2,1)}, u32[]{:S(2)}) copy-start(bf16[128,256]{1,0:T(8,128)(2,1)} %param.36) | copy-start | bytes 196612
  201.2 77.0 %copy-start.56 = (bf16[128,256]{1,0:T(8,128)(2,1)S(1)}, bf16[128,256]{1,0:T(8,128)(2,1)}, u32[]{:S(2)}) copy-start(bf16[128,256]{1,0:T(8,128)(2,1)} %param.37) | copy-start | bytes 196612
  201.2 92.9 %all-gather.25.cloned.1.call-start = ((), (), s32[]{:S(2)}) async-start(), calls=%async_computation.29 | async-start | bytes 1310720 | tf_op jit(solution)/shard_map/all_gather | solution.py:180
  229.1 67.0 %copy-start.73 = (f32[128]{0:T(128)}, f32[128]{0:T(128)S(1)}, u32[]{:S(2)}) copy-start(f32[128]{0:T(128)S(1)} %add_rsqrt_fusion.1) | copy-start | bytes 1540
  230.0 101.2 %reduce-scatter.39.cloned.1.call-start = ((), (), s32[]{:S(2)}) async-start(), calls=%async_computation.30 | async-start | bytes 1310720 | tf_op jit(solution)/shard_map/reduce_scatter | solution.py:188
  301.5 32.6 %copy-start.34 = (bf16[4,64,512]{2,1,0:T(8,128)(2,1)}, bf16[4,64,512]{2,1,0:T(8,128)(2,1)S(1)}, u32[]{:S(2)}) copy-start(bf16[4,64,512]{2,1,0:T(8,128)(2,1)S(1)} %fusion.68) | copy-start | bytes 786436
  301.5 30.8 %copy-start.49 = (f32[1024]{0:T(1024)S(1)}, f32[1024]{0:T(1024)}, u32[]{:S(2)}) copy-start(f32[1024]{0:T(1024)} %param.38) | copy-start | bytes 12292
  303.2 32.7 %all-gather.31.cloned.1.call-start = ((), (), s32[]{:S(2)}) async-start(), calls=%async_computation.33 | async-start | bytes 1622016 | tf_op jit(solution)/shard_map/all_gather | solution.py:174
  304.0 56.7 %all-gather.27.cloned.1.call-start = ((), (), s32[]{:S(2)}) async-start(), calls=%async_computation.31 | async-start | bytes 1310720 | tf_op jit(solution)/shard_map/all_gather | solution.py:180
  334.1 54.3 %all-gather.29.cloned.1.call-start = ((), (), s32[]{:S(2)}) async-start(), calls=%async_computation.32 | async-start | bytes 1622016 | tf_op jit(solution)/shard_map/all_gather | solution.py:173
  334.7 80.9 %all-gather.35.cloned.1.call-start = ((), (), s32[]{:S(2)}) async-start(), calls=%async_computation.36 | async-start | bytes 1310720 | tf_op jit(solution)/shard_map/all_gather | solution.py:184
  335.3 108.1 %all-gather.33.cloned.1.call-start = ((), (), s32[]{:S(2)}) async-start(), calls=%async_computation.34 | async-start | bytes 1622016 | tf_op jit(solution)/shard_map/all_gather | solution.py:175
  335.9 143.2 %reduce-scatter.43.cloned.1.call-start = ((), (), s32[]{:S(2)}) async-start(), calls=%async_computation.37 | async-start | bytes 1310720 | tf_op jit(solution)/shard_map/reduce_scatter | solution.py:201
  450.3 28.8 %copy-start.7 = (bf16[128,1024]{1,0:T(8,128)(2,1)S(1)}, bf16[128,1024]{1,0:T(8,128)(2,1)}, u32[]{:S(2)}) copy-start(bf16[128,1024]{1,0:T(8,128)(2,1)} %reduce-scatter.39.cloned.1.call-done) | copy-start | bytes 786436
  452.4 57.8 %all-gather.37.cloned.1.call-start = ((), (), s32[]{:S(2)}) async-start(), calls=%async_computation.38 | async-start | bytes 1310720 | tf_op jit(solution)/shard_map/all_gather | solution.py:184
  483.4 84.4 %reduce-scatter.45.cloned.1.call-start = ((), (), s32[]{:S(2)}) async-start(), calls=%async_computation.39 | async-start | bytes 1310720 | tf_op jit(solution)/shard_map/reduce_scatter | solution.py:201
  539.9 58.8 %reduce-scatter.41.cloned.1.call-start = ((), (), s32[]{:S(2)}) async-start(), calls=%async_computation.35 | async-start | bytes 1310720 | tf_op jit(solution)/shard_map/reduce_scatter | solution.py:188
  543.6 84.5 %all-gather.39.cloned.1.call-start = ((), (), s32[]{:S(2)}) async-start(), calls=%async_computation.40 | async-start | bytes 1310720 | tf_op jit(solution)/shard_map/all_gather | solution.py:184
  601.3 62.6 %reduce-scatter.47.cloned.1.call-start = ((), (), s32[]{:S(2)}) async-start(), calls=%async_computation.41 | async-start | bytes 1310720 | tf_op jit(solution)/shard_map/reduce_scatter | solution.py:201
  634.0 30.0 %copy-start.69 = (f32[128]{0:T(128)S(1)}, f32[128]{0:T(128)}, u32[]{:S(2)}) copy-start(f32[128]{0:T(128)} %copy-done.68) | copy-start | bytes 1540
  636.0 29.1 %copy-start.11 = (f32[128,1024]{1,0:T(8,128)S(1)}, f32[128,1024]{1,0:T(8,128)}, u32[]{:S(2)}) copy-start(f32[128,1024]{1,0:T(8,128)} %get-tuple-element.204) | copy-start | bytes 1572868
  636.0 75.3 %all-gather.41.cloned.1.call-start = ((), (), s32[]{:S(2)}) async-start(), calls=%async_computation.42 | async-start | bytes 1310720 | tf_op jit(solution)/shard_map/all_gather | solution.py:184
  667.0 83.0 %reduce-scatter.77.cloned.1.call-start = ((), (), s32[]{:S(2)}) async-start(), calls=%async_computation.57 | async-start | bytes 1769472
  673.1 91.2 %reduce-scatter.75.cloned.1.call-start = ((), (), s32[]{:S(2)}) async-start(), calls=%async_computation.56 | async-start | bytes 1769472
  679.3 119.6 %reduce-scatter.73.cloned.1.call-start = ((), (), s32[]{:S(2)}) async-start(), calls=%async_computation.55 | async-start | bytes 1769472
  685.5 144.9 %reduce-scatter.65.cloned.1.call-start = ((), (), s32[]{:S(2)}) async-start(), calls=%async_computation.51 | async-start | bytes 589824 | tf_op jit(solution)/shard_map/reduce_scatter | solution.py:385
  688.2 173.6 %reduce-scatter.63.cloned.1.call-start = ((), (), s32[]{:S(2)}) async-start(), calls=%async_computation.50 | async-start | bytes 589824 | tf_op jit(solution)/shard_map/reduce_scatter | solution.py:382
  689.5 203.7 %reduce-scatter.61.cloned.1.call-start = ((), (), s32[]{:S(2)}) async-start(), calls=%async_computation.49 | async-start | bytes 589824 | tf_op jit(solution)/shard_map/reduce_scatter | solution.py:379
  691.9 232.7 %reduce-scatter.59.cloned.1.call-start = ((), (), s32[]{:S(2)}) async-start(), calls=%async_computation.48 | async-start | bytes 589824 | tf_op jit(solution)/shard_map/reduce_scatter | solution.py:376
  693.2 265.8 %reduce-scatter.71.cloned.1.call-start = ((), (), s32[]{:S(2)}) async-start(), calls=%async_computation.54 | async-start | bytes 1769472
  699.5 293.9 %reduce-scatter.69.cloned.1.call-start = ((), (), s32[]{:S(2)}) async-start(), calls=%async_computation.53 | async-start | bytes 1769472
  705.3 322.6 %reduce-scatter.67.cloned.1.call-start = ((), (), s32[]{:S(2)}) async-start(), calls=%async_computation.52 | async-start | bytes 1769472
  711.2 348.1 %reduce-scatter.57.cloned.1.call-start = ((), (), s32[]{:S(2)}) async-start(), calls=%async_computation.47 | async-start | bytes 589824 | tf_op jit(solution)/shard_map/reduce_scatter | solution.py:385
  713.9 376.6 %reduce-scatter.55.cloned.1.call-start = ((), (), s32[]{:S(2)}) async-start(), calls=%async_computation.46 | async-start | bytes 589824 | tf_op jit(solution)/shard_map/reduce_scatter | solution.py:382
  723.0 399.2 %reduce-scatter.51.cloned.1.call-start = ((), (), s32[]{:S(2)}) async-start(), calls=%async_computation.44 | async-start | bytes 589824 | tf_op jit(solution)/shard_map/reduce_scatter | solution.py:376
  744.0 409.5 %reduce-scatter.53.cloned.1.call-start = ((), (), s32[]{:S(2)}) async-start(), calls=%async_computation.45 | async-start | bytes 589824 | tf_op jit(solution)/shard_map/reduce_scatter | solution.py:379
  746.4 435.9 %reduce-scatter.49.cloned.1.call-start = ((), (), s32[]{:S(2)}) async-start(), calls=%async_computation.43 | async-start | bytes 1310720 | tf_op jit(solution)/shard_map/reduce_scatter | solution.py:201
  831.9 350.4 %copy-start.58 = (f32[1024]{0:T(1024)S(1)}, f32[1024]{0:T(1024)}, u32[]{:S(2)}) copy-start(f32[1024]{0:T(1024)} %param.24) | copy-start | bytes 12292
  831.9 350.4 %copy-start.72 = (f32[128]{0:T(128)S(1)}, f32[128]{0:T(128)}, u32[]{:S(2)}) copy-start(f32[128]{0:T(128)} %copy-done.71) | copy-start | bytes 1540
  894.8 288.7 %copy-start.66 = (f32[1024]{0:T(1024)S(1)}, f32[1024]{0:T(1024)}, u32[]{:S(2)}) copy-start(f32[1024]{0:T(1024)} %get-tuple-element.180) | copy-start | bytes 12292
  894.8 288.7 %copy-start.67 = (f32[1024]{0:T(1024)S(1)}, f32[1024]{0:T(1024)}, u32[]{:S(2)}) copy-start(f32[1024]{0:T(1024)} %get-tuple-element.182) | copy-start | bytes 12292
  926.0 297.1 %copy-start.25 = (bf16[128,1024]{1,0:T(8,128)(2,1)S(1)}, bf16[128,1024]{1,0:T(8,128)(2,1)}, u32[]{:S(2)}) copy-start(bf16[128,1024]{1,0:T(8,128)(2,1)} %reduce-scatter.47.cloned.1.call-done) | copy-start | bytes 786436
  926.0 297.1 %copy-start.70 = (f32[128]{0:T(128)S(1)}, f32[128]{0:T(128)}, u32[]{:S(2)}) copy-start(f32[128]{0:T(128)} %copy-done.68) | copy-start | bytes 1540
  926.1 297.1 %copy-start.75 = (f32[128]{0:T(128)S(1)}, f32[128]{0:T(128)}, u32[]{:S(2)}) copy-start(f32[128]{0:T(128)} %copy-done.74) | copy-start | bytes 1540
  (59 other events, 156.1 us)
Sparse Core Ops, SparseCore 0:
  11.3 29.3 all-gather.14
  84.3 29.1 reduce-scatter.34
  201.3 26.5 reduce-scatter.36
  230.2 26.6 all-gather.24
  303.3 27.7 reduce-scatter.38
  452.5 26.5 reduce-scatter.42
  483.5 26.6 all-gather.36
  540.0 27.7 reduce-scatter.44
  570.9 27.6 reduce-scatter.40
  601.4 26.6 all-gather.38
  636.2 27.7 reduce-scatter.46
Sparse Core Ops, SparseCore 1:
  86.3 27.6 all-gather.18
  116.6 26.4 all-gather.16
  144.6 26.2 all-gather.20
  172.5 25.0 all-gather.22
  305.7 26.2 all-gather.30
  334.6 26.0 all-gather.26
  362.2 26.2 all-gather.28
  390.3 25.3 all-gather.34
  417.2 26.2 all-gather.32
  667.1 26.4 all-gather.40
  695.9 33.9 reduce-scatter.76
  732.2 32.0 reduce-scatter.74
  766.6 32.2 reduce-scatter.72
  801.2 29.1 reduce-scatter.64
  832.7 29.0 reduce-scatter.62
  864.1 29.1 reduce-scatter.60
  895.5 28.9 reduce-scatter.58
  927.0 32.0 reduce-scatter.70
  961.3 32.0 reduce-scatter.68
  995.8 32.1 reduce-scatter.66
  1030.2 29.0 reduce-scatter.56
  1061.4 29.0 reduce-scatter.54
  1093.2 28.9 reduce-scatter.50
  1124.5 28.9 reduce-scatter.52
  1156.5 25.8 reduce-scatter.48
where the time goes:
time: 1240 us; the launch traced here: 1230 us
  waiting for transfers between devices  827 us (67%)
  blocking collectives  166 us (13%)
  matrix products  140 us (11%)
  other arithmetic  51.6 us (4%)
  local copies, waits for them, and re-layouts  28.9 us (2%)
  between operations  17.4 us (1%)
    unnamed x42, waiting for transfers between devices  148 us
    reduce_scatter x4, waiting for transfers between devices, branch_rows(): lax.psum_scatter(against(source, weight).astype(jnp.bfloat16), 'ha', scat...  111 us
    reduce_scatter x4, waiting for transfers between devices, input_rows(): lax.psum_scatter(summed.astype(jnp.bfloat16), 'ha', scatter_dimension=0,...  106 us
    all_gather x4, waiting for transfers between devices, spread_grads(): return lax.all_gather(grads, 'ha', axis=0, tiled=True)  75.5 us
    reduce_scatter x2, waiting for transfers between devices, per_device(): lax.psum_scatter(query_grad.astype(jnp.bfloat16), 'af', scatter_dimension...  60.1 us
    reduce_scatter x2, waiting for transfers between devices, per_device(): lax.psum_scatter(keys_grad.astype(jnp.bfloat16), 'af', scatter_dimension=...  59.8 us
    reduce_scatter x2, waiting for transfers between devices, per_device(): lax.psum_scatter(values_grad.astype(jnp.bfloat16), 'af', scatter_dimensio...  59.4 us
    reduce_scatter x2, waiting for transfers between devices, per_device(): lax.psum_scatter(output_grad.astype(jnp.bfloat16), 'af', scatter_dimensio...  59.2 us
  transfers between devices with their start and end apart: 36, of which 30 were waited for; matrix products, arithmetic and copies ran while one was open for 11% of the time, Pallas kernels for 0%

commit v1 on v0

v1 whole, which is shorter than its diff:
```python
import functools

import jax
import jax.numpy as jnp
from jax import lax
from jax.experimental import pallas as pl
from jax.experimental.pallas import tpu as pltpu
from jax.sharding import PartitionSpec as P

HD = 64
epsilon = 1e-06
rope_base = 10000.0
MESH = pl.DeviceIdType.MESH
VMEM = pl.BlockSpec(memory_space=pltpu.VMEM)
ANY = pl.BlockSpec(memory_space=pl.ANY)
F32 = jnp.float32
BF16 = jnp.bfloat16


def mm(left, right):
    return jnp.dot(left, right, preferred_element_type=F32)


def mm_nt(left, right):
    return lax.dot_general(left, right, (((1,), (1,)), ((), ())), preferred_element_type=F32)


def mm_tn(left, right):
    return lax.dot_general(left, right, (((0,), (0,)), ((), ())), preferred_element_type=F32)


def normalize(values, gain):
    return values * lax.rsqrt(jnp.mean(values * values, axis=-1, keepdims=True) + epsilon) * gain


def norm_back(values, gain, grads):
    scaling = lax.rsqrt(jnp.mean(values * values, axis=-1, keepdims=True) + epsilon)
    weighted = gain * grads
    inner = jnp.mean(weighted * values, axis=-1, keepdims=True)
    return (
        scaling * weighted - values * scaling * scaling * scaling * inner,
        jnp.sum(grads * values * scaling, axis=0, keepdims=True),
    )


def layout(lens_row, bucket, head_count):
    counted = lens_row.shape[0]
    ends = jnp.cumsum(lens_row)
    starts = ends - lens_row
    places = jnp.arange(bucket, dtype=jnp.int32)
    documents = jnp.sum((places[:, None] >= ends[None, :]).astype(jnp.int32), axis=1)
    matching = documents[:, None] == jnp.arange(counted, dtype=jnp.int32)[None, :]
    beginning = jnp.sum(jnp.where(matching, starts[None, :], 0), axis=1)
    offsets = (places - beginning).astype(F32)
    halfway = HD // 2
    frequency = rope_base ** (-jnp.arange(halfway, dtype=F32) / halfway)
    angles = offsets[:, None] * frequency[None, :]
    cosine, sine = jnp.cos(angles), jnp.sin(angles)
    cos_table = jnp.tile(jnp.concatenate([cosine, cosine], axis=1), (1, head_count))
    sin_table = jnp.tile(jnp.concatenate([-sine, sine], axis=1), (1, head_count))
    query_docs = jnp.where(documents < counted, documents, -1)[:, None]
    return (cos_table, sin_table, query_docs, documents[None, :])


def other(me, k):
    result, bit = me, 1
    while bit <= k:
        if k & bit:
            result = result + bit * (1 - 2 * lax.rem(lax.div(me, bit), 2))
        bit *= 2
    return result


def greet(n, me):
    barrier = pltpu.get_barrier_semaphore()
    for k in range(1, n):
        pl.semaphore_signal(barrier, inc=1, device_id={"ha": other(me, k)}, device_id_type=MESH)


def met(n):
    pl.semaphore_wait(pltpu.get_barrier_semaphore(), n - 1)


def rows_of(index, count):
    return pl.ds(pl.multiple_of(index * count, count), count)


def gather_copy(buffer, me, target, rows, send, recv, slot):
    mine = buffer.at[rows_of(me, rows)]
    return pltpu.make_async_remote_copy(
        src_ref=mine, dst_ref=mine, send_sem=send.at[slot], recv_sem=recv.at[slot],
        device_id={"ha": target}, device_id_type=MESH,
    )


def start_gather(buffer, n, me, rows, send, recv):
    for k in range(1, n):
        gather_copy(buffer, me, other(me, k), rows, send, recv, k).start()


def wait_block(buffer, me, k, rows, send, recv):
    theirs = buffer.at[rows_of(other(me, k), rows)]
    pltpu.make_async_remote_copy(
        src_ref=theirs, dst_ref=theirs, send_sem=send.at[k], recv_sem=recv.at[k],
        device_id={"ha": other(me, k)}, device_id_type=MESH,
    ).wait_recv()


def wait_sent(buffer, n, me, rows, send, recv):
    for k in range(1, n):
        gather_copy(buffer, me, other(me, k), rows, send, recv, k).wait_send()


def part_copy(sbuf, rbuf, k, target, send, recv):
    return pltpu.make_async_remote_copy(
        src_ref=sbuf.at[k], dst_ref=rbuf.at[k], send_sem=send.at[k], recv_sem=recv.at[k],
        device_id={"ha": target}, device_id_type=MESH,
    )


def finish_parts(own, sbuf, rbuf, n, me, send, recv):
    total = own[...]
    for k in range(1, n):
        copy = part_copy(sbuf, rbuf, k, other(me, k), send, recv)
        copy.wait_recv()
        total = total + rbuf[k].astype(F32)
    for k in range(1, n):
        part_copy(sbuf, rbuf, k, other(me, k), send, recv).wait_send()
    return total


def ship_static(part, index, me, n, own, sbuf, rbuf, send, recv):
    for k in range(n):
        @pl.when(me == (index ^ k))
        def _(k=k):
            if k == 0:
                own[...] = part
            else:
                sbuf[k] = part.astype(BF16)
                part_copy(sbuf, rbuf, k, index, send, recv).start()


def swap_halves(values):
    width = values.shape[-1]
    lane = lax.broadcasted_iota(jnp.int32, values.shape, 1)
    half = HD // 2
    return jnp.where(
        lax.rem(lane, HD) < half,
        pltpu.roll(values, width - half, 1),
        pltpu.roll(values, half, 1),
    )


def head_masks(width, kind):
    lane = lax.broadcasted_iota(jnp.int32, (1, width), 1)
    return [(lax.div(lane, HD) == h).astype(kind) for h in range(width // HD)]


def stack_heads(block, masks):
    return jnp.concatenate([block * mask for mask in masks], axis=0)


def unstack_heads(stacked, masks, rows):
    total = None
    for h, mask in enumerate(masks):
        piece = stacked[h * rows:(h + 1) * rows] * mask
        total = piece if total is None else total + piece
    return total


def allowed_block(qdoc, kdoc, first, rows, span):
    places_q = first + lax.broadcasted_iota(jnp.int32, (rows, span), 0)
    places_k = lax.broadcasted_iota(jnp.int32, (rows, span), 1)
    return ((qdoc == kdoc) & (places_k <= places_q)) | (places_k == places_q)


def softmax_parts(scores, allowed, heads, rows):
    result = []
    for h in range(heads):
        masked = jnp.where(allowed, scores[h * rows:(h + 1) * rows] * (HD ** -0.5), -1000000000.0)
        weights = jnp.exp(masked - jnp.max(masked, axis=-1, keepdims=True))
        result.append(weights * (1.0 / jnp.sum(weights, axis=-1, keepdims=True)))
    return result


def attn_fwd_kernel(n, later, *refs):
    if later:
        (x, gain, w, cos, sin, qdoc, kdoc, first,
         middle, ng, q, k, v, att,
         wv, own, sbuf, rbuf, wsem, gs, gr, ps, pr) = refs
    else:
        (x, ng, w, cos, sin, qdoc, kdoc,
         middle, q, k, v, att, vraw,
         wv, own, sbuf, rbuf, wsem, ps, pr) = refs
    me = lax.axis_index("ha")
    rows, depth = x.shape
    width = q.shape[1]
    heads = width // HD
    greet(n, me)
    copies = [pltpu.make_async_copy(w.at[:, j], wv.at[j], wsem.at[j]) for j in range(4)]
    for copy in copies:
        copy.start()
    if later:
        ng[rows_of(me, rows)] = normalize(x[...], gain[...]).astype(BF16)
    met(n)
    if later:
        start_gather(ng, n, me, rows, gs, gr)
    for copy in copies[:3]:
        copy.wait()

    def project(block):
        where = rows_of(block, rows)
        source = ng[where]
        cosine, sine = cos[where], sin[where]
        raw = mm(source, wv[0].reshape(depth, width))
        q[where] = (raw * cosine + swap_halves(raw) * sine).astype(BF16)
        raw = mm(source, wv[1].reshape(depth, width))
        k[where] = (raw * cosine + swap_halves(raw) * sine).astype(BF16)
        raw = mm(source, wv[2].reshape(depth, width))
        if later:
            v[where] = (0.5 * raw + 0.5 * first[where]).astype(BF16)
        else:
            vraw[where] = raw
            v[where] = raw.astype(BF16)

    if later:
        project(me)
        for j in range(1, n):
            wait_block(ng, me, j, rows, gs, gr)
            project(other(me, j))
    else:
        for j in range(n):
            project(j)
    copies[3].wait()
    masks = head_masks(width, BF16)
    masks32 = head_masks(width, F32)
    for i in range(n):
        span = (i + 1) * rows
        allowed = allowed_block(qdoc[i * rows:span], kdoc[:, :span], i * rows, rows, span)
        scores = mm_nt(stack_heads(q[i * rows:span], masks), k[:span])
        probs = [p.astype(BF16) for p in softmax_parts(scores, allowed, heads, rows)]
        mixed = mm(jnp.concatenate(probs, axis=0), v[:span])
        block = unstack_heads(mixed, masks32, rows).astype(BF16)
        att[i * rows:span] = block
        ship_static(mm_nt(block, wv[3].reshape(depth, width)), i, me, n, own, sbuf, rbuf, ps, pr)
    middle[...] = x[...] + finish_parts(own, sbuf, rbuf, n, me, ps, pr)
    if later:
        wait_sent(ng, n, me, rows, gs, gr)


def ffn_fwd_kernel(n, middle, gain, w, out, ng, gate, up, wv, own, sbuf, rbuf, wsem, gs, gr, ps, pr):
    me = lax.axis_index("ha")
    rows, depth = middle.shape
    hidden = gate.shape[1]
    greet(n, me)
    copies = [pltpu.make_async_copy(w.at[:, j], wv.at[j], wsem.at[j]) for j in range(3)]
    for copy in copies:
        copy.start()
    ng[rows_of(me, rows)] = normalize(middle[...], gain[...]).astype(BF16)
    met(n)
    start_gather(ng, n, me, rows, gs, gr)
    for copy in copies:
        copy.wait()

    def branch(block):
        where = rows_of(block, rows)
        source = ng[where]
        g = mm(source, wv[0].reshape(depth, hidden))
        u = mm(source, wv[1].reshape(depth, hidden))
        gate[where] = g
        up[where] = u
        return mm_nt((g * jax.nn.sigmoid(g) * u).astype(BF16), wv[2].reshape(depth, hidden))

    own[...] = branch(me)
    for k in range(1, n):
        wait_block(ng, me, k, rows, gs, gr)
        sbuf[k] = branch(other(me, k)).astype(BF16)
        part_copy(sbuf, rbuf, k, other(me, k), ps, pr).start()
    out[...] = middle[...] + finish_parts(own, sbuf, rbuf, n, me, ps, pr)
    wait_sent(ng, n, me, rows, gs, gr)


def ffn_back_kernel(n, turn, *refs):
    if turn:
        (middle, gain, w, gy, gg,
         gmiddle, ggain, dw, ypart,
         ng, hid, ggate, gup, wv, own, sbuf, rbuf, wsem, gs, gr, ps, pr) = refs
    else:
        (middle, gain, w, gy, ng, gate_hbm, up_hbm,
         gmiddle, ggain, dw,
         gate, up, gg, hid, ggate, gup, wv, own, sbuf, rbuf, wsem, gs, gr, ps, pr) = refs
    me = lax.axis_index("ha")
    rows, depth = middle.shape
    hidden = hid.shape[1]
    greet(n, me)
    copies = [pltpu.make_async_copy(w.at[:, j], wv.at[j], wsem.at[j]) for j in range(3)]
    if not turn:
        copies.append(pltpu.make_async_copy(gate_hbm, gate, wsem.at[3]))
        copies.append(pltpu.make_async_copy(up_hbm, up, wsem.at[4]))
    for copy in copies:
        copy.start()
    if turn:
        moving = ng
        ng[rows_of(me, rows)] = normalize(middle[...], gain[...]).astype(BF16)
    else:
        moving = gg
        gg[rows_of(me, rows)] = gy[...].astype(BF16)
    met(n)
    start_gather(moving, n, me, rows, gs, gr)
    for copy in copies:
        copy.wait()

    def branch(block):
        where = rows_of(block, rows)
        if turn:
            source = ng[where]
            g = mm(source, wv[0].reshape(depth, hidden))
            u = mm(source, wv[1].reshape(depth, hidden))
        else:
            g, u = gate[where], up[where]
        s = jax.nn.sigmoid(g)
        h = (g * s * u).astype(BF16)
        hid[where] = h
        if turn:
            ypart[where] = mm_nt(h, wv[2].reshape(depth, hidden)).astype(BF16)
        gh = mm(gg[where], wv[2].reshape(depth, hidden))
        a = (gh * u * s * (1.0 + g * (1.0 - s))).astype(BF16)
        b = (gh * g * s).astype(BF16)
        ggate[where] = a
        gup[where] = b
        return mm_nt(a, wv[0].reshape(depth, hidden)) + mm_nt(b, wv[1].reshape(depth, hidden))

    own[...] = branch(me)
    for k in range(1, n):
        wait_block(moving, me, k, rows, gs, gr)
        sbuf[k] = branch(other(me, k)).astype(BF16)
        part_copy(sbuf, rbuf, k, other(me, k), ps, pr).start()
    shape = (w.shape[0], w.shape[2], hidden)
    dw[:, 0] = mm_tn(ng[...], ggate[...]).astype(BF16).reshape(shape)
    dw[:, 1] = mm_tn(ng[...], gup[...]).astype(BF16).reshape(shape)
    dw[:, 2] = mm_tn(gg[...], hid[...]).astype(BF16).reshape(shape)
    total = finish_parts(own, sbuf, rbuf, n, me, ps, pr)
    back, gain_part = norm_back(middle[...], gain[...], total)
    gmiddle[...] = gy[...].astype(F32) + back
    ggain[...] = gain_part
    wait_sent(moving, n, me, rows, gs, gr)


def attn_back_kernel(n, later, *refs):
    if later:
        (x, gain, w, gmid, ng, q, k, v, att, cos, sin, qdoc, kdoc,
         gx, ggain, dw, carry,
         gg, gat, gq, gk, gv, gka, gva, wv, own, sbuf, rbuf, wsem, gs, gr, ps, pr) = refs
    else:
        (x, gain, w, gmid, ng, q, k, v, att, cos, sin, qdoc, kdoc, carry,
         gx, ggain, dw,
         gg, gat, gq, gk, gv, gka, gva, wv, own, sbuf, rbuf, wsem, gs, gr, ps, pr) = refs
    me = lax.axis_index("ha")
    rows, depth = x.shape
    width = q.shape[1]
    heads = width // HD
    greet(n, me)
    copies = [pltpu.make_async_copy(w.at[:, j], wv.at[j], wsem.at[j]) for j in range(4)]
    for copy in copies:
        copy.start()
    gg[rows_of(me, rows)] = gmid[...].astype(BF16)
    met(n)
    start_gather(gg, n, me, rows, gs, gr)
    gka[...] = jnp.zeros_like(gka)
    gva[...] = jnp.zeros_like(gva)
    for copy in copies:
        copy.wait()

    def pull(block):
        where = rows_of(block, rows)
        gat[where] = mm(gg[where], wv[3].reshape(depth, width)).astype(BF16)

    pull(me)
    for j in range(1, n):
        wait_block(gg, me, j, rows, gs, gr)
        pull(other(me, j))
    masks = head_masks(width, BF16)
    masks32 = head_masks(width, F32)
    for i in reversed(range(n)):
        span = (i + 1) * rows
        here = slice(i * rows, span)
        allowed = allowed_block(qdoc[here], kdoc[:, :span], i * rows, rows, span)
        qs = stack_heads(q[here], masks)
        gas = stack_heads(gat[here], masks)
        probs = softmax_parts(mm_nt(qs, k[:span]), allowed, heads, rows)
        gprobs = mm_nt(gas, v[:span])
        raws = []
        for h in range(heads):
            p = probs[h]
            gp = gprobs[h * rows:(h + 1) * rows]
            inner = jnp.sum(p * gp, axis=-1, keepdims=True)
            raws.append((p * (gp - inner) * (HD ** -0.5)).astype(BF16))
        raw = jnp.concatenate(raws, axis=0)
        low = jnp.concatenate([p.astype(BF16) for p in probs], axis=0)
        gva[:span] += mm_tn(low, gas)
        gka[:span] += mm_tn(raw, qs)
        cosine, sine = cos[here], sin[here]
        gqr = unstack_heads(mm(raw, k[:span]), masks32, rows)
        gqr = (gqr * cosine - swap_halves(gqr) * sine).astype(BF16)
        gkr = gka[here]
        gkr = (gkr * cosine - swap_halves(gkr) * sine).astype(BF16)
        if later:
            half = 0.5 * gva[here]
            carry[here] = half
            gvr = half.astype(BF16)
        else:
            gvr = (gva[here] + carry[here]).astype(BF16)
        gq[here] = gqr
        gk[here] = gkr
        gv[here] = gvr
        part = (
            mm_nt(gqr, wv[0].reshape(depth, width))
            + mm_nt(gkr, wv[1].reshape(depth, width))
            + mm_nt(gvr, wv[2].reshape(depth, width))
        )
        ship_static(part, i, me, n, own, sbuf, rbuf, ps, pr)
    shape = (w.shape[0], w.shape[2], width)
    dw[:, 3] = mm_tn(gg[...], att[...]).astype(BF16).reshape(shape)
    dw[:, 0] = mm_tn(ng[...], gq[...]).astype(BF16).reshape(shape)
    dw[:, 1] = mm_tn(ng[...], gk[...]).astype(BF16).reshape(shape)
    dw[:, 2] = mm_tn(ng[...], gv[...]).astype(BF16).reshape(shape)
    total = finish_parts(own, sbuf, rbuf, n, me, ps, pr)
    back, gain_part = norm_back(x[...], gain[...], total)
    gx[...] = gmid[...] + back
    ggain[...] = gain_part
    wait_sent(gg, n, me, rows, gs, gr)


def gains_kernel(n, g, parts, out, abuf, bbuf, asend, arecv, bsend, brecv):
    ha = lax.axis_index("ha")
    af = lax.axis_index("af")
    barrier = pltpu.get_barrier_semaphore()
    for k in range(1, n):
        pl.semaphore_signal(barrier, inc=1, device_id={"ha": other(ha, k)}, device_id_type=MESH)
    for k in range(1, g):
        pl.semaphore_signal(barrier, inc=1, device_id={"af": other(af, k)}, device_id_type=MESH)
    pl.semaphore_wait(barrier, n + g - 2)

    def exchange(axis, me, count, buffer, send, recv):
        copies = []
        for k in range(1, count):
            copies.append(pltpu.make_async_remote_copy(
                src_ref=buffer.at[me], dst_ref=buffer.at[me], send_sem=send.at[k], recv_sem=recv.at[k],
                device_id={axis: other(me, k)}, device_id_type=MESH,
            ))
            copies[-1].start()
        for k in range(1, count):
            theirs = buffer.at[other(me, k)]
            pltpu.make_async_remote_copy(
                src_ref=theirs, dst_ref=theirs, send_sem=send.at[k], recv_sem=recv.at[k],
                device_id={axis: other(me, k)}, device_id_type=MESH,
            ).wait_recv()
        total = buffer[0]
        for j in range(1, count):
            total = total + buffer[j]
        for copy in copies:
            copy.wait_send()
        return total

    abuf[ha] = parts[...]
    bbuf[af] = exchange("ha", ha, n, abuf, asend, arecv)
    out[...] = exchange("af", af, g, bbuf, bsend, brecv)


def sems(count):
    return pltpu.SemaphoreType.DMA((count,))


def traffic(n, rows, depth):
    return [
        pltpu.VMEM((rows, depth), F32),
        pltpu.VMEM((n, rows, depth), BF16),
        pltpu.VMEM((n, rows, depth), BF16),
    ]


def launch(kernel, name, number, args, in_any, outs, scratch, flops):
    return pl.pallas_call(
        kernel,
        out_shape=outs,
        in_specs=[ANY if j in in_any else VMEM for j in range(len(args))],
        out_specs=[VMEM] * len(outs),
        scratch_shapes=scratch,
        compiler_params=pltpu.CompilerParams(
            collective_id=number, has_side_effects=True, vmem_limit_bytes=48 * 1024 * 1024
        ),
        cost_estimate=pl.CostEstimate(flops=flops, bytes_accessed=16 * 1024 * 1024, transcendentals=0),
        name=name,
    )(*args)


def per_device(
    block_input, lengths, cotangent,
    attngain_early, query_early, keys_early, values_early, output_early,
    ffngain_early, gate_early, upward_early, down_early,
    attngain_later, query_later, keys_later, values_later, output_later,
    ffngain_later, gate_later, upward_later, down_later,
):
    n, g = lax.axis_size("ha"), lax.axis_size("af")
    rows, depth = block_input.shape
    bucket = rows * n
    wrows, width = query_early.shape
    hidden = gate_early.shape[1]
    shape = jax.ShapeDtypeStruct
    cos, sin, qdoc, kdoc = layout(lengths[0], bucket, width // HD)

    def gather(*matrices):
        return lax.all_gather(jnp.stack(matrices), "af", axis=0, tiled=False)

    x = block_input.astype(F32)
    gain_rows = [v[None, :] for v in (attngain_early, ffngain_early, attngain_later, ffngain_later)]
    attn_early = gather(query_early, keys_early, values_early, output_early)
    ng1 = lax.all_gather(normalize(x, gain_rows[0]).astype(BF16), "ha", axis=0, tiled=True)
    ffn_early = gather(gate_early, upward_early, down_early)
    attn_later = gather(query_later, keys_later, values_later, output_later)
    cot = lax.all_gather(cotangent, "ha", axis=0, tiled=True)
    ffn_later = gather(gate_later, upward_later, down_later)

    tokens16 = shape((bucket, depth), BF16)
    heads16 = shape((bucket, width), BF16)
    heads32 = shape((bucket, width), F32)
    own32 = shape((rows, depth), F32)
    gain32 = shape((1, depth), F32)
    wide = pltpu.VMEM((bucket, hidden), BF16)
    tall = pltpu.VMEM((bucket, depth), BF16)
    slim = pltpu.VMEM((bucket, width), BF16)
    slim32 = pltpu.VMEM((bucket, width), F32)
    attn_w = pltpu.VMEM((4, g, wrows, width), BF16)
    ffn_w = pltpu.VMEM((3, g, wrows, hidden), BF16)
    moves = traffic(n, rows, depth)
    attn_flops = 2 * bucket * depth * width * 4
    ffn_flops = 2 * bucket * depth * hidden * 3

    middle1, q1, k1, v1, att1, vraw1 = launch(
        functools.partial(attn_fwd_kernel, n, False), "attn_fwd_early", 1,
        [x, ng1, attn_early, cos, sin, qdoc, kdoc], (2,),
        [own32, heads16, heads16, heads16, heads16, heads32],
        [attn_w, *moves, sems(4), sems(n), sems(n)], attn_flops,
    )
    out1, ng2, gate1, up1 = launch(
        functools.partial(ffn_fwd_kernel, n), "ffn_fwd_early", 2,
        [middle1, gain_rows[1], ffn_early], (2,),
        [own32, tokens16, shape((bucket, hidden), F32), shape((bucket, hidden), F32)],
        [ffn_w, *moves, sems(3), sems(n), sems(n), sems(n), sems(n)], ffn_flops,
    )
    middle2, ng3, q2, k2, v2, att2 = launch(
        functools.partial(attn_fwd_kernel, n, True), "attn_fwd_later", 3,
        [out1, gain_rows[2], attn_later, cos, sin, qdoc, kdoc, vraw1], (2,),
        [own32, tokens16, heads16, heads16, heads16, heads16],
        [attn_w, *moves, sems(4), sems(n), sems(n), sems(n), sems(n)], attn_flops,
    )
    gmid2, ffngain2, dffn2, ypart = launch(
        functools.partial(ffn_back_kernel, n, True), "ffn_turn_later", 4,
        [middle2, gain_rows[3], ffn_later, cotangent, cot], (2,),
        [own32, gain32, shape((g, 3, wrows, hidden), BF16), tokens16],
        [tall, wide, wide, wide, ffn_w, *moves, sems(3), sems(n), sems(n), sems(n), sems(n)], 3 * ffn_flops,
    )
    gout1, attngain2, dattn2, carry = launch(
        functools.partial(attn_back_kernel, n, True), "attn_back_later", 5,
        [out1, gain_rows[2], attn_later, gmid2, ng3, q2, k2, v2, att2, cos, sin, qdoc, kdoc], (2,),
        [own32, gain32, shape((g, 4, wrows, width), BF16), heads32],
        [tall, slim, slim, slim, slim, slim32, slim32, attn_w, *moves,
         sems(4), sems(n), sems(n), sems(n), sems(n)], 2 * attn_flops,
    )
    gmid1, ffngain1, dffn1 = launch(
        functools.partial(ffn_back_kernel, n, False), "ffn_back_early", 6,
        [middle1, gain_rows[1], ffn_early, gout1, ng2, gate1, up1], (2, 5, 6),
        [own32, gain32, shape((g, 3, wrows, hidden), BF16)],
        [pltpu.VMEM((bucket, hidden), F32), pltpu.VMEM((bucket, hidden), F32),
         tall, wide, wide, wide, ffn_w, *moves, sems(5), sems(n), sems(n), sems(n), sems(n)], 2 * ffn_flops,
    )
    grads, attngain1, dattn1 = launch(
        functools.partial(attn_back_kernel, n, False), "attn_back_early", 7,
        [x, gain_rows[0], attn_early, gmid1, ng1, q1, k1, v1, att1, cos, sin, qdoc, kdoc, carry], (2,),
        [own32, gain32, shape((g, 4, wrows, width), BF16)],
        [tall, slim, slim, slim, slim, slim32, slim32, attn_w, *moves,
         sems(4), sems(n), sems(n), sems(n), sems(n)], 2 * attn_flops,
    )

    def scatter(partial_sums):
        return lax.psum_scatter(partial_sums, "af", scatter_dimension=0, tiled=False).astype(F32)

    block_output = (
        middle2 + lax.psum_scatter(ypart, "ha", scatter_dimension=0, tiled=True).astype(F32)
    ).astype(BF16)
    fl, al, fe, ae = scatter(dffn2), scatter(dattn2), scatter(dffn1), scatter(dattn1)
    parts = jnp.concatenate([attngain1, ffngain1, attngain2, ffngain2], axis=0)
    gains, = launch(
        functools.partial(gains_kernel, n, g), "gain_sums", 8, [parts], (), [shape(parts.shape, F32)],
        [pltpu.VMEM((n, *parts.shape), F32), pltpu.VMEM((g, *parts.shape), F32),
         sems(n), sems(n), sems(g), sems(g)], 0,
    )
    return (
        block_output, grads,
        gains[0], ae[0], ae[1], ae[2], ae[3], gains[1], fe[0], fe[1], fe[2],
        gains[2], al[0], al[1], al[2], al[3], gains[3], fl[0], fl[1], fl[2],
    )


def solution(mesh):
    tokens = P(("af", "ha"), None)
    matrix = P("af", "ha")
    layer = (P(), matrix, matrix, matrix, matrix, P(), matrix, matrix, matrix)
    return jax.shard_map(
        per_device, mesh=mesh,
        in_specs=(tokens, P("af", None), tokens, *layer, *layer),
        out_specs=(tokens, tokens, *layer, *layer),
        check_vma=False,
    )
```

time: 1240 us -> 557 us (0.45)
  waiting for transfers between devices: 827 us -> 250 us
  Pallas kernels: 0 us -> 223 us
  blocking collectives: 166 us -> 0 us
  matrix products: 140 us -> 0 us
  other arithmetic: 51.6 us -> 15.1 us
  local copies, waits for them, and re-layouts: 28.9 us -> 47.8 us
    reduce_scatter x16 -> x5, waiting for transfers between devices: 455 us -> 124 us  [the longest x4 124 us: scatter(): lax.psum_scatter(partial_sums, 'af', scatter_dimension=0, tiled=False)]
    pallas_call x0 -> x8, Pallas kernels: none -> 223 us  [launch(): pl.pallas_call(kernel, out_shape=outs, in_specs=[ANY if j in in_any else...]
    unnamed x42 -> x11, waiting for transfers between devices: 148 us -> 1.87 us
    dot_general x54 -> x0, matrix products: 140 us -> none  [the longest x14 34.8 us: product(): return jnp.dot(left, right, preferred_element_type=jnp.float32)]
    all_gather x8 -> x0, blocking collectives: 126 us -> none  [the longest x2 32.7 us: fetch_weights(): lax.all_gather(query, 'af', axis=0, tiled=True)]
    all_gather x14 -> x6, waiting for transfers between devices: 224 us -> 124 us  [the longest x4 102 us: gather(): return lax.all_gather(jnp.stack(matrices), 'af', axis=0, tiled=False)]
    psum x1 -> x0, blocking collectives: 39.6 us -> none  [per_device(): lax.psum((gain_grads[0][0], gain_grads[0][1], gain_grads[1][0], gain_grad...]
    convert_element_type x22 -> x8, other arithmetic: 29.3 us -> 7.84 us  [the longest x4 4.27 us: scatter(): lax.psum_scatter(partial_sums, 'af', scatter_dimension=0, tiled=False)]
  transfers between devices with their start and end apart: 36 -> 11, of which waited for: 30 -> 7; matrix products, arithmetic and copies ran while one was open for 11% -> 5% of each run, Pallas kernels for 0% -> 35%
where the time goes in v1:
time: 557 us; the launch traced here: 551 us
  waiting for transfers between devices  250 us (45%)
  Pallas kernels  223 us (40%)
  local copies, waits for them, and re-layouts  47.8 us (9%)
  other arithmetic  15.1 us (3%)
  between operations  14.7 us (3%)
    pallas_call x8, Pallas kernels, launch(): pl.pallas_call(kernel, out_shape=outs, in_specs=[ANY if j in in_any else...  223 us
    reduce_scatter x4, waiting for transfers between devices, scatter(): lax.psum_scatter(partial_sums, 'af', scatter_dimension=0, tiled=False)  124 us
    all_gather x4, waiting for transfers between devices, gather(): return lax.all_gather(jnp.stack(matrices), 'af', axis=0, tiled=False)  102 us
    unnamed x105, local copies, waits for them, and re-layouts  31.6 us
    all_gather x1, waiting for transfers between devices, per_device(): lax.all_gather(normalize(x, gain_rows[0]).astype(BF16), 'ha', axis=0, til...  21.6 us
    all_gather x2, local copies, waits for them, and re-layouts, gather(): return lax.all_gather(jnp.stack(matrices), 'af', axis=0, tiled=False)  13.1 us
  transfers between devices with their start and end apart: 11, of which 7 were waited for; matrix products, arithmetic and copies ran while one was open for 5% of the time, Pallas kernels for 35%

profile of v1, /device:TPU:0, one launch (start us, length us, event | category | flops | bytes accessed | tf_op | source)
XLA Modules:
  0.0 550.9 jit_solution(8492820002991388149)
XLA Ops:
  7.3 1.2 multiply_reduce_fusion
  8.5 1.8 multiply_convert_fusion
  10.4 1.7 pad_maximum_fusion.2
  12.2 2.0 pad_maximum_fusion
  14.3 0.9 pad_maximum_fusion.1
  15.3 0.7 pad_maximum_fusion.3
  18.2 21.6 %all-gather.11.cloned.1.call-done.refs_1_.refs_4_ = bf16[512,1024]{1,0:T(8,128)(2,1)} async-done(((bf16[128,1024]{1,0:T(8,128)(2,1)}), bf16[512,1024]{1,0:T(8,128)(2,1)}) %all-gather.11.cloned.1.call-update) | async-done | bytes 1048592 | tf_op jit(solution)/shard_map/all_gather | solution.py:518
  39.8 31.3 %all-gather.15.cloned.1.call-done = bf16[32,128,256]{2,1,0:T(8,128)(2,1)} async-done(((bf16[4,128,256]{2,1,0:T(8,128)(2,1)}), bf16[32,128,256]{2,1,0:T(8,128)(2,1)}) %all-gather.15.cloned.1.call-update) | async-done | bytes 2097168 | tf_op jit(solution)/shard_map/all_gather | solution.py:513
  71.1 1.2 copy-done
  72.4 18.3 %attn_fwd_early.1 = (f32[128,1024]{1,0:T(8,128)S(1)}, bf16[512,256]{1,0:T(8,128)(2,1)S(1)}, bf16[512,256]{1,0:T(8,128)(2,1)S(1)}, bf16[512,256]{1,0:T(8,128)(2,1...) custom-call(f32[128,1024]{1,0:T(8,128)S(1)} %convert_element_type.38.refs_0_, bf16[512,1024]{1,0:T(8,128)(2,1)S(1)} %copy-done, ...), custom_call_target="tpu_custom_call" | custom-call | flops 1073741824 | bytes 16777216 | tf_op jit(solution)/shard_map/attn_fwd_early/pallas_call | solution.py:483
  90.7 0.7 copy-done.14
  91.3 0.7 copy-done.16
  92.1 28.7 %all-gather.17.cloned.1.call-done = bf16[24,128,704]{1,2,0:T(8,128)(2,1)} async-done(((bf16[3,128,704]{1,2,0:T(8,128)(2,1)}), bf16[24,128,704]{1,2,0:T(8,128)(2,1)}) %all-gather.17.cloned.1.call-update) | async-done | bytes 4325392 | tf_op jit(solution)/shard_map/all_gather | solution.py:513
  120.8 6.5 %copy.89 = bf16[24,128,704]{2,1,0:T(8,128)(2,1)} copy(bf16[24,128,704]{1,2,0:T(8,128)(2,1)} %all-gather.17.cloned.1.call-done) | data formatting | bytes 8650752 | tf_op jit(solution)/shard_map/all_gather | solution.py:513
  127.3 42.2 %all-gather.21.cloned.1.call-done = bf16[24,128,704]{1,2,0:T(8,128)(2,1)} async-done(((bf16[3,128,704]{1,2,0:T(8,128)(2,1)}), bf16[24,128,704]{1,2,0:T(8,128)(2,1)}) %all-gather.21.cloned.1.call-update) | async-done | bytes 4325392 | tf_op jit(solution)/shard_map/all_gather | solution.py:513
  169.5 6.5 %copy.92 = bf16[24,128,704]{2,1,0:T(8,128)(2,1)} copy(bf16[24,128,704]{1,2,0:T(8,128)(2,1)} %all-gather.21.cloned.1.call-done) | data formatting | bytes 8650752 | tf_op jit(solution)/shard_map/all_gather | solution.py:513
  176.0 26.6 %ffn_fwd_early.1 = (f32[128,1024]{1,0:T(8,128)S(1)}, bf16[512,1024]{1,0:T(8,128)(2,1)S(1)}, f32[512,704]{1,0:T(8,128)S(1)}, f32[512,704]{1,0:T(8,128)S(1)}) custom-call(f32[128,1024]{1,0:T(8,128)S(1)} %get-tuple-element.50.middle.refs_0_, f32[1,1024]{1,0:T(1,128)S(1)} %bitcast.75, bf16[8,3,128,704]{3,2,1,0:T(8,128)(2,1)} %bitcast.77), custom_call_target="tpu_custom_call" | custom-call | flops 2214592512 | bytes 16777216 | tf_op jit(solution)/shard_map/ffn_fwd_early/pallas_call | solution.py:483
  202.6 1.1 copy-done.34
  203.8 1.2 copy-done.36
  205.0 1.0 copy-done.38
  206.0 35.3 %attn_fwd_later.1 = (f32[128,1024]{1,0:T(8,128)S(1)}, bf16[512,1024]{1,0:T(8,128)(2,1)S(1)}, bf16[512,256]{1,0:T(8,128)(2,1)S(1)}, bf16[512,256]{1,0:T(8,128)(2,...) custom-call(f32[128,1024]{1,0:T(8,128)S(1)} %get-tuple-element.51.refs_0_, f32[1,1024]{1,0:T(1,128)S(1)} %bitcast.71, ...), custom_call_target="tpu_custom_call" | custom-call | flops 1073741824 | bytes 16777216 | tf_op jit(solution)/shard_map/attn_fwd_later/pallas_call | solution.py:483
  241.3 1.0 copy-done.6
  242.3 0.7 copy-done.18
  243.0 0.7 copy-done.20
  243.7 0.7 copy-done.22
  244.4 0.7 copy-done.24
  245.1 0.9 copy-done.2
  246.0 1.2 copy-done.5
  247.3 29.1 %ffn_turn_later.1 = (f32[128,1024]{1,0:T(8,128)S(1)}, f32[1,1024]{1,0:T(1,128)S(1)}, bf16[8,3,128,704]{3,2,1,0:T(8,128)(2,1)}, bf16[512,1024]{1,0:T(8,128)(2,1)}) custom-call(f32[128,1024]{1,0:T(8,128)S(1)} %get-tuple-element.53.refs_0_, f32[1,1024]{1,0:T(1,128)S(1)} %bitcast.74, bf16[8,3,128,704]{3,2,1,0:T(8,128)(2,1)} %bitcast.79, ...), custom_call_target="tpu_custom_call" | custom-call | flops 6643777536 | bytes 16777216 | tf_op jit(solution)/shard_map/ffn_turn_later/pallas_call | solution.py:483
  276.4 0.8 copy-done.32
  277.4 1.2 copy-done.7
  278.7 0.9 copy-done.21
  279.6 0.9 copy-done.23
  280.6 0.9 copy-done.25
  281.5 1.0 copy-done.33
  282.5 40.6 %attn_back_later.1 = (f32[128,1024]{1,0:T(8,128)S(1)}, f32[1,1024]{1,0:T(1,128)S(1)}, bf16[8,4,128,256]{3,2,1,0:T(8,128)(2,1)}, f32[512,256]{1,0:T(8,128)S(1)}) custom-call(f32[128,1024]{1,0:T(8,128)S(1)} %get-tuple-element.51.refs_0_, f32[1,1024]{1,0:T(1,128)S(1)} %bitcast.72, bf16[8,4,128,256]{3,2,1,0:T(8,128)(2,1)} %bitcast.81, ...), custom_call_target="tpu_custom_call" | custom-call | flops 2147483648 | bytes 16777216 | tf_op jit(solution)/shard_map/attn_back_later/pallas_call | solution.py:483
  323.2 0.8 copy-done.28
  324.0 0.8 copy-done.30
  325.1 0.8 copy-done.9
  325.8 1.0 copy-done.31
  326.9 1.4 copy-done.35
  328.3 1.5 copy-done.37
  329.8 1.2 copy-done.39
  331.1 27.2 %ffn_back_early.1 = (f32[128,1024]{1,0:T(8,128)S(1)}, f32[1,1024]{1,0:T(1,128)S(1)}, bf16[8,3,128,704]{3,2,1,0:T(8,128)(2,1)}) custom-call(f32[128,1024]{1,0:T(8,128)S(1)} %copy-done.9, f32[1,1024]{1,0:T(1,128)S(1)} %bitcast.76, bf16[8,3,128,704]{3,2,1,0:T(8,128)(2,1)} %bitcast.78, f32[128,1024]{1,0:T(8,128)S(1)} %copy-done.31, ...), custom_call_target="tpu_custom_call" | custom-call | flops 4429185024 | bytes 16777216 | tf_op jit(solution)/shard_map/ffn_back_early/pallas_call | solution.py:483
  358.3 31.3 %attn_back_early.1 = (f32[128,1024]{1,0:T(8,128)S(1)}, f32[1,1024]{1,0:T(1,128)S(1)}, bf16[8,4,128,256]{3,2,1,0:T(8,128)(2,1)}) custom-call(f32[128,1024]{1,0:T(8,128)S(1)} %convert_element_type.38.refs_0_, f32[1,1024]{1,0:T(1,128)S(1)} %bitcast.73, bf16[8,4,128,256]{3,2,1,0:T(8,128)(2,1)} %bitcast.85, f32[128,1024]{1,0:T(8,128)S(1)} %get-tuple-element.65.refs_3_, ...), custom_call_target="tpu_custom_call" | custom-call | flops 2147483648 | bytes 16777216 | tf_op jit(solution)/shard_map/attn_back_early/pallas_call | solution.py:483
  390.3 0.7 reduce-scatter.10.cloned.1.call-update
  391.0 14.1 %gain_sums.1 = f32[4,1024]{1,0:T(4,128)S(1)} custom-call(f32[4,1024]{1,0:T(4,128)S(1)} %pad_maximum_fusion.6.parts), custom_call_target="tpu_custom_call" | custom-call | bytes 16777216 | tf_op jit(solution)/shard_map/gain_sums/pallas_call | solution.py:483
  405.8 1.7 add_convert_fusion
  407.5 1.0 convert_element_type.46
  408.5 18.0 %reduce-scatter.8.cloned.1.call-done = bf16[1,4,128,256]{3,2,1,0:T(8,128)(2,1)} async-done(((bf16[8,4,128,256]{3,2,1,0:T(8,128)(2,1)}), bf16[1,4,128,256]{3,2,1,0:T(8,128)(2,1)}) %reduce-scatter.8.cloned.1.call-update) | async-done | bytes 262160 | tf_op jit(solution)/shard_map/reduce_scatter | solution.py:586
  426.5 1.0 convert_element_type.44
  427.5 0.8 slice_bitcast_fusion.6
  428.3 0.8 slice_bitcast_fusion.10
  429.1 54.5 %reduce-scatter.14.cloned.1.call-done = bf16[1,3,128,704]{3,2,1,0:T(8,128)(2,1)} async-done(((bf16[8,3,128,704]{3,2,1,0:T(8,128)(2,1)}), bf16[1,3,128,704]{3,2,1,0:T(8,128)(2,1)}) %reduce-scatter.14.cloned.1.call-update) | async-done | bytes 540688 | tf_op jit(solution)/shard_map/reduce_scatter | solution.py:586
  483.6 1.1 convert_element_type.47
  484.8 0.9 copy.102
  485.7 0.9 copy.101
  486.6 0.9 copy.100
  487.6 51.8 %reduce-scatter.10.cloned.1.call-done = bf16[1,3,128,704]{3,2,1,0:T(8,128)(2,1)} async-done(((bf16[8,3,128,704]{3,2,1,0:T(8,128)(2,1)}), bf16[1,3,128,704]{3,2,1,0:T(8,128)(2,1)}) %reduce-scatter.10.cloned.1.call-update) | async-done | bytes 540688 | tf_op jit(solution)/shard_map/reduce_scatter | solution.py:586
  539.3 1.1 convert_element_type.45
  540.6 0.9 copy.99
  541.5 0.9 copy.98
  542.4 0.9 copy.97
  543.3 0.8 copy.104
  (117 shorter events, 4.4 us)
Async XLA Ops:
  7.2 7.1 %copy-start.41 = (bf16[128,704]{0,1:T(8,128)(2,1)S(1)}, bf16[128,704]{0,1:T(8,128)(2,1)}, u32[]{:S(2)}) copy-start(bf16[128,704]{0,1:T(8,128)(2,1)} %param.41) | copy-start | bytes 540676
  7.2 7.1 %copy-start.42 = (bf16[128,704]{0,1:T(8,128)(2,1)S(1)}, bf16[128,704]{0,1:T(8,128)(2,1)}, u32[]{:S(2)}) copy-start(bf16[128,704]{0,1:T(8,128)(2,1)} %param.40) | copy-start | bytes 540676
  7.2 7.1 %copy-start.43 = (bf16[128,704]{0,1:T(8,128)(2,1)S(1)}, bf16[128,704]{0,1:T(8,128)(2,1)}, u32[]{:S(2)}) copy-start(bf16[128,704]{0,1:T(8,128)(2,1)} %param.39) | copy-start | bytes 540676
  7.2 32.6 %all-gather.11.cloned.1.call-start = ((), (), s32[]{:S(2)}) async-start(), calls=%async_computation.5 | async-start | bytes 1310720 | tf_op jit(solution)/shard_map/all_gather | solution.py:518
  10.3 5.0 copy-start.44
  10.3 5.0 copy-start.45
  10.3 5.0 copy-start.46
  10.3 5.0 copy-start.47
  10.3 60.8 %all-gather.15.cloned.1.call-start = ((), (), s32[]{:S(2)}) async-start(), calls=%async_computation.12 | async-start | bytes 2359296 | tf_op jit(solution)/shard_map/all_gather | solution.py:513
  12.1 108.6 %all-gather.17.cloned.1.call-start = ((), (), s32[]{:S(2)}) async-start(), calls=%async_computation.13 | async-start | bytes 4866048 | tf_op jit(solution)/shard_map/all_gather | solution.py:513
  12.2 4.5 copy-start.48
  12.2 4.8 copy-start.40
  14.2 155.2 %all-gather.21.cloned.1.call-start = ((), (), s32[]{:S(2)}) async-start(), calls=%async_computation.15 | async-start | bytes 4866048 | tf_op jit(solution)/shard_map/all_gather | solution.py:513
  15.2 190.7 %all-gather.19.cloned.1.call-start = ((), (), s32[]{:S(2)}) async-start(), calls=%async_computation.14 | async-start | bytes 2359296 | tf_op jit(solution)/shard_map/all_gather | solution.py:513
  16.1 229.0 %all-gather.13.cloned.1.call-start = ((), (), s32[]{:S(2)}) async-start(), calls=%async_computation.6 | async-start | bytes 1310720 | tf_op jit(solution)/shard_map/all_gather | solution.py:521
  16.6 389.1 %reduce-scatter.6.cloned.1.call-start = ((), (), s32[]{:S(2)}) async-start(), calls=%async_computation.7 | async-start | bytes 1310720 | tf_op jit(solution)/shard_map/reduce_scatter | solution.py:589
  71.1 1.2 copy-start
  90.6 0.7 copy-start.14
  91.3 0.7 copy-start.16
  92.1 35.2 %copy-start.10 = (bf16[512,256]{1,0:T(8,128)(2,1)}, bf16[512,256]{1,0:T(8,128)(2,1)S(1)}, u32[]{:S(2)}) copy-start(bf16[512,256]{1,0:T(8,128)(2,1)S(1)} %get-tuple-element.66.refs_5_) | copy-start | bytes 786436
  92.1 35.2 %copy-start.12 = (bf16[512,256]{1,0:T(8,128)(2,1)}, bf16[512,256]{1,0:T(8,128)(2,1)S(1)}, u32[]{:S(2)}) copy-start(bf16[512,256]{1,0:T(8,128)(2,1)S(1)} %get-tuple-element.67.refs_6_) | copy-start | bytes 786436
  92.1 83.9 %copy-start.8 = (f32[128,1024]{1,0:T(8,128)}, f32[128,1024]{1,0:T(8,128)S(1)}, u32[]{:S(2)}) copy-start(f32[128,1024]{1,0:T(8,128)S(1)} %get-tuple-element.50.middle.refs_0_) | copy-start | bytes 1572868
  127.3 48.7 %copy-start.27 = (f32[1024]{0:T(1024)S(1)}, f32[1024]{0:T(1024)}, u32[]{:S(2)}) copy-start(f32[1024]{0:T(1024)} %param.29) | copy-start | bytes 12292
  176.0 29.9 %copy-start.3 = (f32[1024]{0:T(1024)S(1)}, f32[1024]{0:T(1024)}, u32[]{:S(2)}) copy-start(f32[1024]{0:T(1024)} %param.33) | copy-start | bytes 12292
  202.6 1.1 copy-start.34
  203.8 1.2 copy-start.36
  204.9 1.0 copy-start.38
  206.0 39.1 %copy-start.26 = (f32[1024]{0:T(1024)S(1)}, f32[1024]{0:T(1024)}, u32[]{:S(2)}) copy-start(f32[1024]{0:T(1024)} %param.38) | copy-start | bytes 12292
  241.3 1.0 copy-start.6
  242.3 0.7 copy-start.18
  243.0 0.7 copy-start.20
  243.7 0.7 copy-start.22
  244.4 0.7 copy-start.24
  245.1 1.0 copy-start.2
  246.0 1.2 copy-start.5
  247.3 30.2 %copy-start.19 = (bf16[512,256]{1,0:T(8,128)(2,1)S(1)}, bf16[512,256]{1,0:T(8,128)(2,1)}, u32[]{:S(2)}) copy-start(bf16[512,256]{1,0:T(8,128)(2,1)} %copy-done.18) | copy-start | bytes 786436
  276.4 0.8 copy-start.32
  277.2 130.3 %reduce-scatter.12.cloned.1.call-start = ((), (), s32[]{:S(2)}) async-start(), calls=%async_computation.10 | async-start | bytes 2359296 | tf_op jit(solution)/shard_map/reduce_scatter | solution.py:586
  277.4 1.2 copy-start.7
  278.7 0.9 copy-start.21
  279.6 0.9 copy-start.23
  280.6 0.9 copy-start.25
  281.5 1.0 copy-start.33
  323.2 0.8 copy-start.28
  324.0 0.8 copy-start.30
  324.8 1.0 copy-start.9
  324.8 101.7 %reduce-scatter.8.cloned.1.call-start = ((), (), s32[]{:S(2)}) async-start(), calls=%async_computation.8 | async-start | bytes 2359296 | tf_op jit(solution)/shard_map/reduce_scatter | solution.py:586
  325.8 1.0 copy-start.31
  326.9 1.4 copy-start.35
  328.3 1.5 copy-start.37
  329.8 1.2 copy-start.39
  331.0 27.2 %copy-start.1 = (bf16[512,1024]{1,0:T(8,128)(2,1)S(1)}, bf16[512,1024]{1,0:T(8,128)(2,1)}, u32[]{:S(2)}) copy-start(bf16[512,1024]{1,0:T(8,128)(2,1)} %all-gather.11.cloned.1.call-done.refs_1_.refs_4_) | copy-start | bytes 3145732
  331.0 27.2 %copy-start.4 = (f32[1024]{0:T(1024)S(1)}, f32[1024]{0:T(1024)}, u32[]{:S(2)}) copy-start(f32[1024]{0:T(1024)} %param.24) | copy-start | bytes 12292
  331.0 27.2 %copy-start.11 = (bf16[512,256]{1,0:T(8,128)(2,1)S(1)}, bf16[512,256]{1,0:T(8,128)(2,1)}, u32[]{:S(2)}) copy-start(bf16[512,256]{1,0:T(8,128)(2,1)} %copy-done.10) | copy-start | bytes 786436
  331.0 27.3 %copy-start.13 = (bf16[512,256]{1,0:T(8,128)(2,1)S(1)}, bf16[512,256]{1,0:T(8,128)(2,1)}, u32[]{:S(2)}) copy-start(bf16[512,256]{1,0:T(8,128)(2,1)} %copy-done.12) | copy-start | bytes 786436
  331.0 27.3 %copy-start.15 = (bf16[512,256]{1,0:T(8,128)(2,1)S(1)}, bf16[512,256]{1,0:T(8,128)(2,1)}, u32[]{:S(2)}) copy-start(bf16[512,256]{1,0:T(8,128)(2,1)} %copy-done.14) | copy-start | bytes 786436
  331.0 27.3 %copy-start.17 = (bf16[512,256]{1,0:T(8,128)(2,1)S(1)}, bf16[512,256]{1,0:T(8,128)(2,1)}, u32[]{:S(2)}) copy-start(bf16[512,256]{1,0:T(8,128)(2,1)} %copy-done.16) | copy-start | bytes 786436
  331.0 27.3 %copy-start.29 = (f32[512,256]{1,0:T(8,128)S(1)}, f32[512,256]{1,0:T(8,128)}, u32[]{:S(2)}) copy-start(f32[512,256]{1,0:T(8,128)} %copy-done.28) | copy-start | bytes 1572868
  389.7 93.9 %reduce-scatter.14.cloned.1.call-start = ((), (), s32[]{:S(2)}) async-start(), calls=%async_computation.11 | async-start | bytes 5308416 | tf_op jit(solution)/shard_map/reduce_scatter | solution.py:586
  390.3 149.1 %reduce-scatter.10.cloned.1.call-start = ((), (), s32[]{:S(2)}) async-start(), calls=%async_computation.9 | async-start | bytes 5308416 | tf_op jit(solution)/shard_map/reduce_scatter | solution.py:586
Sparse Core Ops, SparseCore 0:
  10.5 29.3 all-gather.10
  42.0 29.0 all-gather.14
  72.8 47.9 all-gather.16
  122.3 47.1 all-gather.20
  171.5 27.8 all-gather.18
  201.1 38.8 all-gather.12
  277.3 32.3 reduce-scatter.5
  324.9 33.7 reduce-scatter.11
  389.8 36.6 reduce-scatter.7
  428.8 54.7 reduce-scatter.13
  486.0 53.3 reduce-scatter.9

commit v2 on v1

v2 whole, which is shorter than its diff:
```python
import functools
import types

import jax
import jax.numpy as jnp
import numpy as np
from jax import lax
from jax.experimental import pallas as pl
from jax.experimental.pallas import tpu as pltpu
from jax.sharding import PartitionSpec as P

HD = 64
epsilon = 1e-06
rope_base = 10000.0
MESH = pl.DeviceIdType.MESH
VMEM = pl.BlockSpec(memory_space=pltpu.VMEM)
ANY = pl.BlockSpec(memory_space=pl.ANY)
F32 = jnp.float32
BF16 = jnp.bfloat16


def mm(left, right):
    return jnp.dot(left, right, preferred_element_type=F32)


def mm_nt(left, right):
    return lax.dot_general(left, right, (((1,), (1,)), ((), ())), preferred_element_type=F32)


def mm_tn(left, right):
    return lax.dot_general(left, right, (((0,), (0,)), ((), ())), preferred_element_type=F32)


def normalize(values, gain):
    return values * lax.rsqrt(jnp.mean(values * values, axis=-1, keepdims=True) + epsilon) * gain


def norm_back(values, gain, grads):
    scaling = lax.rsqrt(jnp.mean(values * values, axis=-1, keepdims=True) + epsilon)
    weighted = gain * grads
    inner = jnp.mean(weighted * values, axis=-1, keepdims=True)
    return (
        scaling * weighted - values * scaling * scaling * scaling * inner,
        jnp.sum(grads * values * scaling, axis=0, keepdims=True),
    )


def other(me, k):
    result, bit = me, 1
    while bit <= k:
        if k & bit:
            result = result + bit * (1 - 2 * lax.rem(lax.div(me, bit), 2))
        bit *= 2
    return result


def swap_halves(values):
    width = values.shape[-1]
    lane = lax.broadcasted_iota(jnp.int32, values.shape, 1)
    half = HD // 2
    return jnp.where(
        lax.rem(lane, HD) < half,
        pltpu.roll(values, width - half, 1),
        pltpu.roll(values, half, 1),
    )


def head_masks(width, kind):
    lane = lax.broadcasted_iota(jnp.int32, (1, width), 1)
    return [(lax.div(lane, HD) == h).astype(kind) for h in range(width // HD)]


def stack_heads(block, masks):
    return jnp.concatenate([block * mask for mask in masks], axis=0)


def unstack_heads(stacked, masks, rows):
    total = None
    for h, mask in enumerate(masks):
        piece = stacked[h * rows:(h + 1) * rows] * mask
        total = piece if total is None else total + piece
    return total


def softmax_parts(scores, allowed, heads, rows):
    result = []
    for h in range(heads):
        masked = jnp.where(allowed, scores[h * rows:(h + 1) * rows] * (HD ** -0.5), -1000000000.0)
        weights = jnp.exp(masked - jnp.max(masked, axis=-1, keepdims=True))
        result.append(weights * (1.0 / jnp.sum(weights, axis=-1, keepdims=True)))
    return result


def rows_of(index, count):
    return pl.ds(pl.multiple_of(index * count, count), count)


def remote(source, target, send, recv, **place):
    return pltpu.make_async_remote_copy(
        src_ref=source, dst_ref=target, send_sem=send, recv_sem=recv, device_id=place, device_id_type=MESH
    )


class Step:
    def __init__(self, n, g, refs):
        self.n, self.g, self.zs = n, g, g // 2
        self.r = refs
        self.ha, self.af = lax.axis_index("ha"), lax.axis_index("af")
        self.z, self.c = lax.div(self.af, 2), lax.rem(self.af, 2)
        self.sibling = self.af + 1 - 2 * self.c
        self.rows, self.depth = refs.x.shape
        self.bucket = self.rows * n
        self.width = refs.q[0].shape[1]
        self.heads = self.width // HD
        self.hidden = refs.gate.shape[1]
        self.count = self.depth // g
        self.flip = refs.w[1].shape[3] == self.count
        self.ends = self.zs > 3
        self.reach = self.zs - 2 if self.ends else self.zs - 1


    def token_copy(self, buffer, slot, owner, k):
        block = buffer.at[rows_of(owner, self.rows)]
        return remote(block, block, self.r.ags.at[slot, k], self.r.agr.at[slot, k], ha=other(self.ha, k))

    def spread(self, buffer, slot):
        for k in range(1, self.n):
            self.token_copy(buffer, slot, self.ha, k).start()

    def arrived(self, buffer, slot, k):
        self.token_copy(buffer, slot, other(self.ha, k), k).wait_recv()

    def spread_done(self, buffer, slot):
        for k in range(1, self.n):
            self.token_copy(buffer, slot, self.ha, k).wait_send()

    def part_copy(self, slot, k, target):
        return remote(self.r.sbuf.at[k], self.r.rbuf.at[k], self.r.pss.at[slot, k], self.r.psr.at[slot, k], ha=target)

    def ship(self, part, slot, index):
        for k in range(self.n):
            @pl.when(self.ha == (index ^ k))
            def _(k=k):
                if k == 0:
                    self.r.own[...] = part
                else:
                    self.r.sbuf[k] = part.astype(BF16)
                    self.part_copy(slot, k, index).start()

    def collect(self, slot):
        total = self.r.own[...]
        for k in range(1, self.n):
            self.part_copy(slot, k, other(self.ha, k)).wait_recv()
            total = total + self.r.rbuf[k].astype(F32)
        for k in range(1, self.n):
            self.part_copy(slot, k, other(self.ha, k)).wait_send()
        return total

    def output_copy(self, k):
        target = other(self.ha, k)
        return remote(
            self.r.ypart.at[rows_of(target, self.rows)], self.r.yrecv.at[k],
            self.r.pss.at[7, k], self.r.psr.at[7, k], ha=target,
        )


    def block(self, i, z, c):
        return self.r.w[i].at[z * 2 + c]

    def local_copy(self, i, j):
        return pltpu.make_async_copy(self.r.whbm[i, j], self.r.w[i].at[self.af, j], self.r.lsem.at[i, j])

    def to_sibling(self, i, z):
        block = self.block(i, z, self.c)
        return remote(block, block, self.r.gs.at[i, 0, z], self.r.gr.at[i, 0, z], af=self.sibling)

    def along(self, i, source, z, slot):
        block = self.block(i, source, self.c)
        return remote(block, block, self.r.gs.at[i, 1, slot], self.r.gr.at[i, 1, source], af=z * 2 + self.c)

    def neighbours(self, do, far_first=False):
        distances = range(1, self.reach + 1)
        for d in reversed(distances) if far_first else distances:
            for t in (self.z + d, self.z - d):
                pl.when((t >= 0) & (t < self.zs))(functools.partial(do, t))

    def gather_start(self, i):
        for j in range(self.r.w[i].shape[1]):
            self.local_copy(i, j).wait()
        self.neighbours(lambda t: self.along(i, self.z, t, t).start(), far_first=True)
        self.to_sibling(i, self.z).start()

    def gather_mid(self, i):
        last = self.zs - 1

        def take(t):
            self.along(i, t, t, t).wait_recv()
            self.to_sibling(i, t).start()

        self.neighbours(take)
        if self.ends:
            pl.when(self.z == last - 1)(lambda: self.along(i, 0, last, last + 1).start())
            pl.when(self.z == 1)(lambda: self.along(i, last, 0, last + 2).start())

    def gather_end(self, i):
        last = self.zs - 1

        def take(t):
            self.along(i, t, t, t).wait_recv()
            self.to_sibling(i, t).start()

        if self.ends:
            pl.when(self.z == last)(functools.partial(take, 0))
            pl.when(self.z == 0)(functools.partial(take, last))
        for t in range(self.zs):
            block = self.block(i, t, 1 - self.c)
            remote(block, block, self.r.gs.at[i, 0, t], self.r.gr.at[i, 0, t], af=self.sibling).wait_recv()

    def gather_drain(self, i):
        last = self.zs - 1
        self.neighbours(lambda t: self.along(i, self.z, t, t).wait_send())
        for t in range(self.zs):
            self.to_sibling(i, t).wait_send()
        if self.ends:
            pl.when(self.z == last - 1)(lambda: self.along(i, 0, last, last + 1).wait_send())
            pl.when(self.z == 1)(lambda: self.along(i, last, 0, last + 2).wait_send())


    def swap_copy(self, i):
        return remote(
            self.r.part[i % 2].at[1 - self.c], self.r.swapped[i % 2], self.r.rs.at[i, 0], self.r.rr.at[i, 0],
            af=self.sibling,
        )

    def sum_copy(self, i, source, z):
        return remote(
            self.r.part[i % 2].at[self.c, z], self.r.zrecv[i].at[source],
            self.r.rs.at[i, 1 + z], self.r.rr.at[i, 1 + source], af=z * 2 + self.c,
        )

    def merge_copy(self, i, up):
        last = self.zs - 1
        block, target = (last, 1) if up else (0, last - 1)
        slot = self.zs + (1 if up else 2)
        return remote(
            self.r.part[i % 2].at[self.c, block], self.r.zrecv[i].at[target],
            self.r.rs.at[i, slot], self.r.rr.at[i, slot], af=target * 2 + self.c,
        )

    def reduce_start(self, i):
        self.swap_copy(i).start()

    def reduce_mid(self, i):
        part, swapped, last = self.r.part[i % 2], self.r.swapped[i % 2], self.zs - 1
        self.swap_copy(i).wait_recv()

        def add(t, carry):
            part[self.c, t] = (part[self.c, t].astype(F32) + swapped[t].astype(F32)).astype(BF16)
            return carry

        lax.fori_loop(0, self.zs, add, 0)
        if self.ends:
            pl.when(self.z == 0)(lambda: self.merge_copy(i, True).start())
            pl.when(self.z == last)(lambda: self.merge_copy(i, False).start())

        def send(t):
            if self.ends:
                held = ((self.z == 1) & (t == last)) | ((self.z == last - 1) & (t == 0))
                pl.when(jnp.logical_not(held))(lambda: self.sum_copy(i, self.z, t).start())
            else:
                self.sum_copy(i, self.z, t).start()

        self.neighbours(send, far_first=True)

    def reduce_merge(self, i):
        part, last = self.r.part[i % 2], self.zs - 1
        if self.ends:
            def merge(up):
                block = last if up else 0
                self.merge_copy(i, up).wait_recv()
                part[self.c, block] = (
                    part[self.c, block].astype(F32) + self.r.zrecv[i][1 if up else last - 1].astype(F32)
                ).astype(BF16)
                self.sum_copy(i, self.z, block).start()

            pl.when(self.z == 1)(functools.partial(merge, True))
            pl.when(self.z == last - 1)(functools.partial(merge, False))

    def reduce_end(self, i):
        part, out, last = self.r.part[i % 2], self.r.sums[i], self.zs - 1
        out[...] = part[self.c, self.z].astype(F32)

        def take(t):
            self.sum_copy(i, t, t).wait_recv()
            out[...] += self.r.zrecv[i][t].astype(F32)

        self.neighbours(take)
        self.swap_copy(i).wait_send()
        self.neighbours(lambda t: self.sum_copy(i, self.z, t).wait_send())
        if self.ends:
            pl.when(self.z == 0)(lambda: self.merge_copy(i, True).wait_send())
            pl.when(self.z == last)(lambda: self.merge_copy(i, False).wait_send())

    def products(self, i, pairs):
        part, count = self.r.part[i % 2], self.count

        def chip(z, carry):
            here = pl.ds(pl.multiple_of(z * 2 * count, 2 * count), 2 * count)
            for j, left, right in pairs:
                if i % 2 == 0 and self.flip:
                    product = mm(right[...], left[:, here]).astype(BF16)
                    part[0, z, j] = product[:, :count]
                    part[1, z, j] = product[:, count:]
                else:
                    product = mm_tn(left[:, here], right[...]).astype(BF16)
                    part[0, z, j] = product[:count]
                    part[1, z, j] = product[count:]
            return carry

        lax.fori_loop(0, self.zs, chip, 0)


    def tables(self):
        r = self.r
        count = r.lengths.shape[1]
        places = lax.broadcasted_iota(jnp.int32, (self.bucket, 1), 0)
        beginning = jnp.zeros((self.bucket, 1), jnp.int32)
        end = 0
        for s in range(count):
            start, end = end, end + r.lengths[0, s]
            beginning = jnp.where((places >= start) & (places < end), start, beginning)
        angles = (places - beginning).astype(F32) * r.wave[0:1]
        r.cos[...] = jnp.cos(angles)
        r.sin[...] = jnp.sin(angles) * r.wave[1:2]

    def turning(self, where):
        copies = self.width // 128
        return (
            jnp.concatenate([self.r.cos[where]] * copies, axis=1),
            jnp.concatenate([self.r.sin[where]] * copies, axis=1),
        )

    def allowed(self, i):
        span = (i + 1) * self.rows
        places_q = i * self.rows + lax.broadcasted_iota(jnp.int32, (self.rows, 1), 0)
        places_k = lax.broadcasted_iota(jnp.int32, (1, span), 1)
        qdoc = jnp.zeros((self.rows, 1), jnp.int32)
        kdoc = jnp.zeros((1, span), jnp.int32)
        end = 0
        for s in range(self.r.lengths.shape[1]):
            end = end + self.r.lengths[0, s]
            qdoc = qdoc + (places_q >= end).astype(jnp.int32)
            kdoc = kdoc + (places_k >= end).astype(jnp.int32)
        qdoc = jnp.where(places_q >= end, -1, qdoc)
        return ((qdoc == kdoc) & (places_k <= places_q)) | (places_k == places_q)

    def matrix(self, i, j):
        return self.r.w[i][:, j].reshape(self.depth, self.r.w[i].shape[-1])

    def turned(self, i, j):
        return jnp.concatenate([self.r.w[i][owner, j] for owner in range(self.g)], axis=1)

    def into_hidden(self, source, i, j):
        return mm_nt(source, self.turned(i, j)) if self.flip else mm(source, self.matrix(i, j))

    def out_of_hidden(self, source, i, j):
        return mm(source, self.turned(i, j)) if self.flip else mm_nt(source, self.matrix(i, j))


    def project(self, layer, block):
        r = self.r
        where = rows_of(block, self.rows)
        source = r.ng[2 * layer][where]
        cosine, sine = self.turning(where)
        raw = mm(source, self.matrix(3 * layer, 0))
        r.q[layer][where] = (raw * cosine + swap_halves(raw) * sine).astype(BF16)
        raw = mm(source, self.matrix(3 * layer, 1))
        r.k[layer][where] = (raw * cosine + swap_halves(raw) * sine).astype(BF16)
        raw = mm(source, self.matrix(3 * layer, 2))
        if layer == 0:
            r.first[where] = raw
            r.v[layer][where] = raw.astype(BF16)
        else:
            r.v[layer][where] = (0.5 * raw + 0.5 * r.first[where]).astype(BF16)

    def attend(self, layer, slot):
        r, rows = self.r, self.rows
        masks, masks32 = head_masks(self.width, BF16), head_masks(self.width, F32)
        for i in range(self.n):
            span = (i + 1) * rows
            here = slice(i * rows, span)
            scores = mm_nt(stack_heads(r.q[layer][here], masks), r.k[layer][:span])
            probs = [p.astype(BF16) for p in softmax_parts(scores, self.allowed(i), self.heads, rows)]
            mixed = mm(jnp.concatenate(probs, axis=0), r.v[layer][:span])
            block = unstack_heads(mixed, masks32, rows).astype(BF16)
            r.att[layer][here] = block
            self.ship(mm_nt(block, self.matrix(3 * layer, 3)), slot, i)

    def attend_back(self, layer, slot):
        r, rows = self.r, self.rows
        masks, masks32 = head_masks(self.width, BF16), head_masks(self.width, F32)
        scale = HD ** -0.5
        for i in reversed(range(self.n)):
            span = (i + 1) * rows
            here = slice(i * rows, span)
            keys, vals = r.k[layer][:span], r.v[layer][:span]
            qs = stack_heads(r.q[layer][here], masks)
            gas = stack_heads(r.gat[here], masks)
            probs = softmax_parts(mm_nt(qs, keys), self.allowed(i), self.heads, rows)
            gprobs = mm_nt(gas, vals)
            raws = []
            for h in range(self.heads):
                p, gp = probs[h], gprobs[h * rows:(h + 1) * rows]
                inner = jnp.sum(p * gp, axis=-1, keepdims=True)
                raws.append((p * (gp - inner) * scale).astype(BF16))
            raw = jnp.concatenate(raws, axis=0)
            low = jnp.concatenate([p.astype(BF16) for p in probs], axis=0)
            if i == self.n - 1:
                r.gva[...] = mm_tn(low, gas)
                r.gka[...] = mm_tn(raw, qs)
            else:
                r.gva[:span] += mm_tn(low, gas)
                r.gka[:span] += mm_tn(raw, qs)
            cosine, sine = self.turning(here)
            gqr = unstack_heads(mm(raw, keys), masks32, rows)
            gqr = (gqr * cosine - swap_halves(gqr) * sine).astype(BF16)
            gkr = r.gka[here]
            gkr = (gkr * cosine - swap_halves(gkr) * sine).astype(BF16)
            if layer == 1:
                half = 0.5 * r.gva[here]
                r.carry[here] = half
                gvr = half.astype(BF16)
            else:
                gvr = (r.gva[here] + r.carry[here]).astype(BF16)
            r.gq[here], r.gk[here], r.gv[here] = gqr, gkr, gvr
            part = (
                mm_nt(gqr, self.matrix(3 * layer, 0))
                + mm_nt(gkr, self.matrix(3 * layer, 1))
                + mm_nt(gvr, self.matrix(3 * layer, 2))
            )
            self.ship(part, slot, i)

    def feed(self, layer, slot, buffer, agslot, turn, ready):
        r = self.r

        def first(where):
            source = r.ng[2 * layer + 1][where]
            g = self.into_hidden(source, 3 * layer + 1, 0)
            u = self.into_hidden(source, 3 * layer + 1, 1)
            if not turn:
                r.gate[where], r.up[where] = g, u
            return g, u

        def second(where, g, u):
            if not turn:
                return self.out_of_hidden((g * jax.nn.sigmoid(g) * u).astype(BF16), 3 * layer + 2, 0)
            part, h = self.feed_back(layer, where, 0, g, u)
            r.ypart[where] = self.out_of_hidden(h, 3 * layer + 2, 0).astype(BF16)
            return part

        mine = rows_of(self.ha, self.rows)
        g, u = first(mine)
        ready()
        r.own[...] = second(mine, g, u)
        for k in range(1, self.n):
            self.arrived(buffer, agslot, k)
            where = rows_of(other(self.ha, k), self.rows)
            r.sbuf[k] = second(where, *first(where)).astype(BF16)
            self.part_copy(slot, k, other(self.ha, k)).start()

    def feed_back(self, layer, where, gg, g, u):
        r = self.r
        s = jax.nn.sigmoid(g)
        h = (g * s * u).astype(BF16)
        gh = self.into_hidden(r.gg[gg][where], 3 * layer + 2, 0)
        a = (gh * u * s * (1.0 + g * (1.0 - s))).astype(BF16)
        b = (gh * g * s).astype(BF16)
        for j, value in enumerate((a, b, h)):
            if self.flip:
                r.units[j][:, where] = value.T
            else:
                r.units[j][where] = value
        return self.out_of_hidden(a, 3 * layer + 1, 0) + self.out_of_hidden(b, 3 * layer + 1, 1), h

    def feed_grads(self, layer):
        r = self.r
        normed = r.ng[2 * layer + 1]
        self.products(2 * layer, [(0, normed, r.units[0]), (1, normed, r.units[1]), (2, r.gg[0], r.units[2])])

    def attend_grads(self, layer):
        r = self.r
        normed = r.ng[2 * layer]
        self.products(2 * layer + 1, [(0, normed, r.gq), (1, normed, r.gk), (2, normed, r.gv), (3, r.gg[1], r.att[layer])])


    def gain_phase(self, slot, axis, me, count, place):
        buffer = self.r.gbuf[slot]
        for t in range(count):
            copy = remote(
                buffer.at[me], buffer.at[me], self.r.gns.at[slot, t], self.r.gnr.at[slot, me], **{axis: place(t)}
            )
            pl.when(me != t)(copy.start)

    def gain_sum(self, slot, axis, me, count, place):
        buffer = self.r.gbuf[slot]
        for t in range(count):
            copy = remote(
                buffer.at[t], buffer.at[t], self.r.gns.at[slot, t], self.r.gnr.at[slot, t], **{axis: place(t)}
            )
            pl.when(me != t)(copy.wait)
        total = buffer[0]
        for t in range(1, count):
            total = total + buffer[t]
        return total

    def run(self):
        r, n = self.r, self.n
        barrier = pltpu.get_barrier_semaphore()
        for k in range(1, n):
            pl.semaphore_signal(barrier, inc=1, device_id={"ha": other(self.ha, k)}, device_id_type=MESH)
        pl.semaphore_signal(barrier, inc=1, device_id={"af": self.sibling}, device_id_type=MESH)
        for d in range(1, self.zs):
            t = lax.rem(self.z + d, self.zs)
            pl.semaphore_signal(barrier, inc=1, device_id={"af": t * 2 + self.c}, device_id_type=MESH)
        for i in range(6):
            for j in range(r.w[i].shape[1]):
                self.local_copy(i, j).start()
        mine = rows_of(self.ha, self.rows)
        x = r.x[...].astype(F32)
        r.ng[0][mine] = normalize(x, r.gains[0][...]).astype(BF16)
        r.gg[0][mine] = r.cot[...]
        pl.semaphore_wait(barrier, n - 1 + 1 + self.zs - 1)

        self.gather_start(0)
        self.spread(r.ng[0], 0)
        self.spread(r.gg[0], 1)
        self.tables()
        self.gather_mid(0)
        self.gather_start(1)
        self.gather_end(0)
        self.project(0, self.ha)
        for k in range(1, n):
            self.arrived(r.ng[0], 0, k)
            self.project(0, other(self.ha, k))
        self.attend(0, 0)
        r.middle[0][...] = x + self.collect(0)

        r.ng[1][mine] = normalize(r.middle[0][...], r.gains[1][...]).astype(BF16)
        self.spread(r.ng[1], 2)
        self.gather_mid(1)
        self.gather_start(2)
        self.gather_end(1)

        def ready_early():
            self.gather_mid(2)
            self.gather_start(3)
            self.gather_end(2)

        self.feed(0, 1, r.ng[1], 2, False, ready_early)
        r.between[...] = r.middle[0][...] + self.collect(1)

        r.ng[2][mine] = normalize(r.between[...], r.gains[2][...]).astype(BF16)
        self.spread(r.ng[2], 3)
        self.gather_mid(3)
        self.gather_start(4)
        self.gather_end(3)
        self.project(1, self.ha)
        for k in range(1, n):
            self.arrived(r.ng[2], 3, k)
            self.project(1, other(self.ha, k))
        self.attend(1, 2)
        self.gather_mid(4)
        self.gather_start(5)
        r.middle[1][...] = r.between[...] + self.collect(2)

        r.ng[3][mine] = normalize(r.middle[1][...], r.gains[3][...]).astype(BF16)
        self.spread(r.ng[3], 4)
        self.gather_end(4)
        for k in range(1, n):
            self.arrived(r.gg[0], 1, k)

        def ready_later():
            self.gather_mid(5)
            self.gather_end(5)

        self.feed(1, 3, r.ng[3], 4, True, ready_later)
        self.feed_grads(1)
        self.reduce_start(2)
        back, gain = norm_back(r.middle[1][...], r.gains[3][...], self.collect(3))
        r.gmid[...] = r.cot[...].astype(F32) + back
        r.gsum[3:4] = gain

        r.gg[1][mine] = r.gmid[...].astype(BF16)
        self.spread_done(r.gg[0], 1)
        self.spread(r.gg[1], 5)
        self.reduce_mid(2)
        self.pull(1, 5)
        for k in range(1, n):
            self.output_copy(k).start()
        self.attend_back(1, 4)
        self.attend_grads(1)
        self.reduce_start(3)
        self.reduce_merge(2)
        back, gain = norm_back(r.between[...], r.gains[2][...], self.collect(4))
        r.between[...] = r.gmid[...] + back
        r.gsum[2:3] = gain

        r.gg[0][mine] = r.between[...].astype(BF16)
        self.spread(r.gg[0], 6)
        self.reduce_mid(3)
        out = r.middle[1][...] + r.ypart[mine].astype(F32)
        for k in range(1, n):
            self.output_copy(k).wait_recv()
            out = out + r.yrecv[k].astype(F32)
        r.out[...] = out.astype(BF16)

        def back_block(where):
            return self.feed_back(0, where, 0, r.gate[where], r.up[where])[0]

        r.own[...] = back_block(mine)
        for k in range(1, n):
            self.arrived(r.gg[0], 6, k)
            where = rows_of(other(self.ha, k), self.rows)
            r.sbuf[k] = back_block(where).astype(BF16)
            self.part_copy(5, k, other(self.ha, k)).start()
        self.reduce_end(2)
        self.feed_grads(0)
        self.reduce_start(0)
        back, gain = norm_back(r.middle[0][...], r.gains[1][...], self.collect(5))
        r.gmid[...] = r.between[...] + back
        r.gsum[1:2] = gain

        self.spread_done(r.gg[1], 5)
        r.gg[1][mine] = r.gmid[...].astype(BF16)
        self.spread(r.gg[1], 7)
        self.reduce_mid(0)
        self.reduce_merge(3)
        self.pull(0, 7)
        self.attend_back(0, 6)
        self.reduce_end(3)
        self.attend_grads(0)
        self.reduce_start(1)
        self.reduce_merge(0)
        self.reduce_mid(1)
        back, gain = norm_back(x, r.gains[0][...], self.collect(6))
        r.gx[...] = r.gmid[...] + back
        r.gsum[0:1] = gain

        r.gbuf[0][self.ha] = r.gsum[...]
        self.gain_phase(0, "ha", self.ha, n, lambda t: t)
        self.reduce_end(0)
        r.gbuf[1][self.c] = self.gain_sum(0, "ha", self.ha, n, lambda t: t)
        self.gain_phase(1, "af", self.c, 2, lambda t: self.z * 2 + t)
        self.reduce_merge(1)
        r.gbuf[2][self.z] = self.gain_sum(1, "af", self.c, 2, lambda t: self.z * 2 + t)
        self.gain_phase(2, "af", self.z, self.zs, lambda t: t * 2 + self.c)
        total = self.gain_sum(2, "af", self.z, self.zs, lambda t: t * 2 + self.c)
        for i in range(4):
            r.gainsum[i] = total[i:i + 1]
        self.reduce_end(1)
        for slot, buffer in ((0, r.ng[0]), (2, r.ng[1]), (3, r.ng[2]), (4, r.ng[3]), (6, r.gg[0]), (7, r.gg[1])):
            self.spread_done(buffer, slot)
        for k in range(1, n):
            self.output_copy(k).wait_send()
        for i in range(6):
            self.gather_drain(i)

    def pull(self, layer, slot):
        r = self.r

        def block(where):
            r.gat[where] = mm(r.gg[1][where], self.matrix(3 * layer, 3)).astype(BF16)

        block(rows_of(self.ha, self.rows))
        for k in range(1, self.n):
            self.arrived(r.gg[1], slot, k)
            block(rows_of(other(self.ha, k), self.rows))


def step_kernel(n, g, names, *refs):
    found = {}
    for (name, index), ref in zip(names, refs):
        if index is None:
            found[name] = ref
        else:
            found.setdefault(name, {})[index] = ref
    Step(n, g, types.SimpleNamespace(**found)).run()


def finish_kernel(*refs):
    sums, gains, out, gx = refs[:4], refs[4], refs[5], refs[6]
    results, sem = refs[7:-1], refs[-1]
    pairs = [(out, results[0]), (gx, results[1])]
    for layer in range(2):
        first = 2 + 9 * layer
        pairs.append((gains.at[2 * layer], results[first]))
        pairs.append((gains.at[2 * layer + 1], results[first + 5]))
        pairs += [(sums[2 * layer + 1].at[j], results[first + 1 + j]) for j in range(4)]
        pairs += [(sums[2 * layer].at[j], results[first + 6 + j]) for j in range(3)]
    copies = [pltpu.make_async_copy(source, target, sem.at[k]) for k, (source, target) in enumerate(pairs)]
    for copy in copies:
        copy.start()
    for copy in copies:
        copy.wait()


def per_device(
    block_input, lengths, cotangent,
    attngain_early, query_early, keys_early, values_early, output_early,
    ffngain_early, gate_early, upward_early, down_early,
    attngain_later, query_later, keys_later, values_later, output_later,
    ffngain_later, gate_later, upward_later, down_later,
):
    n, g = lax.axis_size("ha"), lax.axis_size("af")
    zs = g // 2
    rows, depth = block_input.shape
    bucket = rows * n
    wrows, width = query_early.shape
    hidden = gate_early.shape[1]
    lane = np.arange(128)
    halfway = HD // 2
    frequency = np.float32(rope_base) ** (-(lane % halfway).astype(np.float32) / np.float32(halfway))
    wave = jnp.asarray(np.stack([frequency, np.where(lane % HD < halfway, -1.0, 1.0)]).astype(np.float32))
    flip = wrows % 128 == 0
    if flip:
        gate_early, upward_early, down_early = gate_early.T, upward_early.T, down_early.T
        gate_later, upward_later, down_later = gate_later.T, upward_later.T, down_later.T
    groups = [
        (query_early, keys_early, values_early, output_early), (gate_early, upward_early), (down_early,),
        (query_later, keys_later, values_later, output_later), (gate_later, upward_later), (down_later,),
    ]
    gains = [v[None, :] for v in (attngain_early, ffngain_early, attngain_later, ffngain_later)]

    names, args, in_specs = [], [], []

    def take(name, index, value, spec=VMEM):
        names.append((name, index))
        args.append(value)
        in_specs.append(spec)

    take("x", None, block_input)
    take("cot", None, cotangent)
    take("lengths", None, lengths, pl.BlockSpec(memory_space=pltpu.SMEM))
    take("wave", None, wave)
    for i, v in enumerate(gains):
        take("gains", i, v)
    for i, group in enumerate(groups):
        for j, v in enumerate(group):
            take("whbm", (i, j), v, ANY)

    outs = []

    def give(name, index, shape, kind):
        names.append((name, index))
        outs.append(jax.ShapeDtypeStruct(shape, kind))

    blocks = [(3, *down_early.shape), (4, wrows, width)] * 2
    for i, shape in enumerate(blocks):
        give("sums", i, shape, F32)
    give("gainsum", None, (4, 1, depth), F32)
    give("out", None, (rows, depth), BF16)
    give("gx", None, (rows, depth), F32)

    scratch = []

    def hold(name, index, shape, kind):
        names.append((name, index))
        scratch.append(pltpu.VMEM(shape, kind))

    for i, group in enumerate(groups):
        hold("w", i, (g, len(group), *group[0].shape), BF16)
    for i in range(4):
        hold("ng", i, (bucket, depth), BF16)
        hold("zrecv", i, (zs, *blocks[i]), BF16)
    for i in range(2):
        hold("part", i, (2, zs, *blocks[i]), BF16)
        hold("swapped", i, (zs, *blocks[i]), BF16)
        hold("gg", i, (bucket, depth), BF16)
        for name in ("q", "k", "v", "att"):
            hold(name, i, (bucket, width), BF16)
        hold("middle", i, (rows, depth), F32)
    for name in ("cos", "sin"):
        hold(name, None, (bucket, 128), F32)
    for name in ("first", "carry", "gva", "gka"):
        hold(name, None, (bucket, width), F32)
    for name in ("gat", "gq", "gk", "gv"):
        hold(name, None, (bucket, width), BF16)
    for name in ("gate", "up"):
        hold(name, None, (bucket, hidden), F32)
    for i in range(3):
        hold("units", i, (hidden, bucket) if flip else (bucket, hidden), BF16)
    for name in ("own", "between", "gmid"):
        hold(name, None, (rows, depth), F32)
    for name in ("sbuf", "rbuf", "yrecv"):
        hold(name, None, (n, rows, depth), BF16)
    hold("ypart", None, (bucket, depth), BF16)
    hold("gsum", None, (4, depth), F32)
    for i, count in enumerate((n, 2, zs)):
        hold("gbuf", i, (count, 4, depth), F32)
    for name, shape in (
        ("ags", (8, n)), ("agr", (8, n)), ("pss", (8, n)), ("psr", (8, n)), ("lsem", (6, 4)),
        ("gs", (6, 2, zs + 2)), ("gr", (6, 2, zs + 2)), ("rs", (4, zs + 3)), ("rr", (4, zs + 3)),
        ("gns", (3, max(n, zs))), ("gnr", (3, max(n, zs))),
    ):
        names.append((name, None))
        scratch.append(pltpu.SemaphoreType.DMA(shape))

    results = pl.pallas_call(
        functools.partial(step_kernel, n, g, names),
        out_shape=outs, in_specs=in_specs, out_specs=[VMEM] * len(outs), scratch_shapes=scratch,
        compiler_params=pltpu.CompilerParams(
            collective_id=0, has_side_effects=True, vmem_limit_bytes=63 * 1024 * 1024
        ),
        cost_estimate=pl.CostEstimate(flops=2 * 10**10, bytes_accessed=10**7, transcendentals=0),
        name="step",
    )(*args)

    shape = jax.ShapeDtypeStruct
    layer = (
        [shape((1, depth), F32)] + [shape((wrows, width), F32)] * 4
        + [shape((1, depth), F32)] + [shape(down_early.shape, F32)] * 3
    )
    finals = pl.pallas_call(
        finish_kernel,
        out_shape=[shape((rows, depth), BF16), shape((rows, depth), F32), *layer, *layer],
        in_specs=[ANY] * 7, out_specs=[VMEM] * 20, scratch_shapes=[pltpu.SemaphoreType.DMA((20,))], name="finish",
        compiler_params=pltpu.CompilerParams(vmem_limit_bytes=62 * 1024 * 1024),
    )(*results)
    finals = [v[0] if v.shape[0] == 1 else v for v in finals]
    if flip:
        finals = [v.T if v.shape == down_early.shape else v for v in finals]
    return tuple(finals)


def solution(mesh):
    tokens = P(("af", "ha"), None)
    matrix = P("af", "ha")
    layer = (P(), matrix, matrix, matrix, matrix, P(), matrix, matrix, matrix)
    return jax.shard_map(
        per_device, mesh=mesh,
        in_specs=(tokens, P("af", None), tokens, *layer, *layer),
        out_specs=(tokens, tokens, *layer, *layer),
        check_vma=False,
    )
```

time: 557 us -> 299 us (0.54)
  waiting for transfers between devices: 250 us -> 0 us
  Pallas kernels: 223 us -> 293 us
  local copies, waits for them, and re-layouts: 47.8 us -> 0 us
  other arithmetic: 15.1 us -> 0 us
  between operations: 14.7 us -> 1.14 us
    reduce_scatter x5 -> x0, waiting for transfers between devices: 124 us -> none  [the longest x4 124 us: scatter(): lax.psum_scatter(partial_sums, 'af', scatter_dimension=0, tiled=False)]
    all_gather x6 -> x0, waiting for transfers between devices: 124 us -> none  [the longest x4 102 us: gather(): return lax.all_gather(jnp.stack(matrices), 'af', axis=0, tiled=False)]
    pallas_call x8 -> x2, Pallas kernels: 223 us -> 293 us  [the longest x1 288 us: per_device(): pl.pallas_call(functools.partial(step_kernel, n, g, names), out_shape=out...]
    unnamed x105 -> x0, local copies, waits for them, and re-layouts: 31.6 us -> none
    all_gather x2 -> x0, local copies, waits for them, and re-layouts: 13.1 us -> none  [gather(): return lax.all_gather(jnp.stack(matrices), 'af', axis=0, tiled=False)]
    convert_element_type x8 -> x0, other arithmetic: 7.84 us -> none  [the longest x4 4.27 us: scatter(): lax.psum_scatter(partial_sums, 'af', scatter_dimension=0, tiled=False)]
  transfers between devices with their start and end apart: 11 -> 0, of which waited for: 7 -> 0; matrix products, arithmetic and copies ran while one was open for 5% -> 0% of each run, Pallas kernels for 35% -> 0%
where the time goes in v2:
time: 299 us; the launch traced here: 294 us
  Pallas kernels  293 us (98%)
    pallas_call x1, Pallas kernels, per_device(): pl.pallas_call(functools.partial(step_kernel, n, g, names), out_shape=out...  288 us

profile of v2, /device:TPU:0, one launch (start us, length us, event | category | flops | bytes accessed | tf_op | source)
XLA Modules:
  0.0 293.6 jit_solution(1392772845447187221)
XLA Ops:
  0.7 288.3 %step.1 = (f32[3,704,128]{2,1,0:T(8,128)}, f32[4,128,256]{2,1,0:T(8,128)}, f32[3,704,128]{2,1,0:T(8,128)}, f32[4,128,256]{2,1,0:T(8,128)}, f32[4,1,1024]{2,1,0:T...) custom-call(bf16[128,1024]{1,0:T(8,128)(2,1)} %refs_0_.1, bf16[128,1024]{1,0:T(8,128)(2,1)} %refs_1_.1, ...), custom_call_target="tpu_custom_call" | custom-call | flops 20000000000 | bytes 10000000 | tf_op jit(solution)/shard_map/step/pallas_call | solution.py:808
  288.9 4.2 %finish.1 = (bf16[128,1024]{1,0:T(8,128)(2,1)}, f32[128,1024]{1,0:T(8,128)}, f32[1,1024]{1,0:T(1,128)}, f32[128,256]{1,0:T(8,128)}, f32[128,256]{1,0:T(8,128)}, ...) custom-call(f32[3,704,128]{2,1,0:T(8,128)} %get-tuple-element.47.ref, ...), custom_call_target="tpu_custom_call" | custom-call | tf_op jit(solution)/shard_map/finish/pallas_call | solution.py:823

commit v3 on v2

--- a/solution.py
+++ b/solution.py
@@ -104,6 +104,7 @@
 class Step:
     def __init__(self, n, g, refs):
         self.n, self.g, self.zs = n, g, g // 2
+        self.square = n == 4
         self.r = refs
         self.ha, self.af = lax.axis_index("ha"), lax.axis_index("af")
         self.z, self.c = lax.div(self.af, 2), lax.rem(self.af, 2)
@@ -114,25 +115,43 @@
         self.heads = self.width // HD
         self.hidden = refs.gate.shape[1]
         self.count = self.depth // g
-        self.flip = refs.w[1].shape[3] == self.count
+        self.flip = refs.w[2].shape[3] == self.count
         self.ends = self.zs > 3
         self.reach = self.zs - 2 if self.ends else self.zs - 1
 
 
-    def token_copy(self, buffer, slot, owner, k):
-        block = buffer.at[rows_of(owner, self.rows)]
-        return remote(block, block, self.r.ags.at[slot, k], self.r.agr.at[slot, k], ha=other(self.ha, k))
+    def token_copy(self, buffer, slot, owner, k, target, half=None):
+        rows = self.rows if half is None else self.rows // 2
+        first = owner * self.rows if half is None else owner * self.rows + half * rows
+        block = buffer.at[pl.ds(pl.multiple_of(first, rows), rows)]
+        return remote(block, block, self.r.ags.at[slot, k], self.r.agr.at[slot, k], ha=target)
+
+    def relay_copy(self, buffer, slot, k):
+        return self.token_copy(buffer, slot, other(self.ha, k), 3 if k == 1 else 0, other(self.ha, 3 - k), k - 1)
 
     def spread(self, buffer, slot):
-        for k in range(1, self.n):
-            self.token_copy(buffer, slot, self.ha, k).start()
+        for k in range(1, 3 if self.square else self.n):
+            self.token_copy(buffer, slot, self.ha, k, other(self.ha, k)).start()
 
     def arrived(self, buffer, slot, k):
-        self.token_copy(buffer, slot, other(self.ha, k), k).wait_recv()
+        if not self.square:
+            self.token_copy(buffer, slot, other(self.ha, k), k, other(self.ha, k)).wait_recv()
+        elif k == 1:
+            for j in (1, 2):
+                self.token_copy(buffer, slot, other(self.ha, j), j, other(self.ha, j)).wait_recv()
+                self.relay_copy(buffer, slot, j).start()
+        elif k == 3:
+            for half in (0, 1):
+                self.token_copy(
+                    buffer, slot, other(self.ha, 3), 0 if half else 3, other(self.ha, 1 + half), half
+                ).wait_recv()
 
     def spread_done(self, buffer, slot):
-        for k in range(1, self.n):
-            self.token_copy(buffer, slot, self.ha, k).wait_send()
+        for k in range(1, 3 if self.square else self.n):
+            self.token_copy(buffer, slot, self.ha, k, other(self.ha, k)).wait_send()
+        if self.square:
+            for k in (1, 2):
+                self.relay_copy(buffer, slot, k).wait_send()
 
     def part_copy(self, slot, k, target):
         return remote(self.r.sbuf.at[k], self.r.rbuf.at[k], self.r.pss.at[slot, k], self.r.psr.at[slot, k], ha=target)
@@ -184,57 +203,57 @@
             for t in (self.z + d, self.z - d):
                 pl.when((t >= 0) & (t < self.zs))(functools.partial(do, t))
 
+    def onward(self, i, hop):
+        result = []
+        for side, sign in enumerate((1, -1)):
+            source, target = self.z - sign * hop, self.z + sign
+            valid = (source >= 0) & (source < self.zs) & (target >= 0) & (target < self.zs)
+            result.append((valid, functools.partial(self.along, i, source, target, 2 * hop + side)))
+        return result
+
     def gather_start(self, i):
         for j in range(self.r.w[i].shape[1]):
             self.local_copy(i, j).wait()
-        self.neighbours(lambda t: self.along(i, self.z, t, t).start(), far_first=True)
+        for valid, copy in self.onward(i, 0):
+            pl.when(valid)(lambda copy=copy: copy().start())
         self.to_sibling(i, self.z).start()
 
-    def gather_mid(self, i):
-        last = self.zs - 1
-
-        def take(t):
-            self.along(i, t, t, t).wait_recv()
-            self.to_sibling(i, t).start()
-
-        self.neighbours(take)
-        if self.ends:
-            pl.when(self.z == last - 1)(lambda: self.along(i, 0, last, last + 1).start())
-            pl.when(self.z == 1)(lambda: self.along(i, last, 0, last + 2).start())
+    def gather_hop(self, i, third):
+        hops = self.zs - 1
+        for hop in range((third - 1) * hops // 3 + 1, third * hops // 3 + 1):
+            onward = self.onward(i, hop)
+            for side, sign in enumerate((1, -1)):
+                source = self.z - sign * hop
+
+                def take(source=source, onward=onward[side]):
+                    self.along(i, source, source, 0).wait_recv()
+                    pl.when(onward[0])(lambda: onward[1]().start())
+                    self.to_sibling(i, source).start()
+
+                pl.when((source >= 0) & (source < self.zs))(take)
 
     def gather_end(self, i):
-        last = self.zs - 1
-
-        def take(t):
-            self.along(i, t, t, t).wait_recv()
-            self.to_sibling(i, t).start()
-
-        if self.ends:
-            pl.when(self.z == last)(functools.partial(take, 0))
-            pl.when(self.z == 0)(functools.partial(take, last))
         for t in range(self.zs):
             block = self.block(i, t, 1 - self.c)
             remote(block, block, self.r.gs.at[i, 0, t], self.r.gr.at[i, 0, t], af=self.sibling).wait_recv()
 
     def gather_drain(self, i):
-        last = self.zs - 1
-        self.neighbours(lambda t: self.along(i, self.z, t, t).wait_send())
+        for hop in range(self.zs - 1):
+            for valid, copy in self.onward(i, hop):
+                pl.when(valid)(lambda copy=copy: copy().wait_send())
         for t in range(self.zs):
             self.to_sibling(i, t).wait_send()
-        if self.ends:
-            pl.when(self.z == last - 1)(lambda: self.along(i, 0, last, last + 1).wait_send())
-            pl.when(self.z == 1)(lambda: self.along(i, last, 0, last + 2).wait_send())
 
 
     def swap_copy(self, i):
         return remote(
-            self.r.part[i % 2].at[1 - self.c], self.r.swapped[i % 2], self.r.rs.at[i, 0], self.r.rr.at[i, 0],
+            self.r.part[i % 4].at[1 - self.c], self.r.swapped[i % 4], self.r.rs.at[i, 0], self.r.rr.at[i, 0],
             af=self.sibling,
         )
 
     def sum_copy(self, i, source, z):
         return remote(
-            self.r.part[i % 2].at[self.c, z], self.r.zrecv[i].at[source],
+            self.r.part[i % 4].at[self.c, z], self.r.zrecv[i].at[source],
             self.r.rs.at[i, 1 + z], self.r.rr.at[i, 1 + source], af=z * 2 + self.c,
         )
 
@@ -243,7 +262,7 @@
         block, target = (last, 1) if up else (0, last - 1)
         slot = self.zs + (1 if up else 2)
         return remote(
-            self.r.part[i % 2].at[self.c, block], self.r.zrecv[i].at[target],
+            self.r.part[i % 4].at[self.c, block], self.r.zrecv[i].at[target],
             self.r.rs.at[i, slot], self.r.rr.at[i, slot], af=target * 2 + self.c,
         )
 
@@ -251,7 +270,7 @@
         self.swap_copy(i).start()
 
     def reduce_mid(self, i):
-        part, swapped, last = self.r.part[i % 2], self.r.swapped[i % 2], self.zs - 1
+        part, swapped, last = self.r.part[i % 4], self.r.swapped[i % 4], self.zs - 1
         self.swap_copy(i).wait_recv()
 
         def add(t, carry):
@@ -273,7 +292,7 @@
         self.neighbours(send, far_first=True)
 
     def reduce_merge(self, i):
-        part, last = self.r.part[i % 2], self.zs - 1
+        part, last = self.r.part[i % 4], self.zs - 1
         if self.ends:
             def merge(up):
                 block = last if up else 0
@@ -287,7 +306,7 @@
             pl.when(self.z == last - 1)(functools.partial(merge, False))
 
     def reduce_end(self, i):
-        part, out, last = self.r.part[i % 2], self.r.sums[i], self.zs - 1
+        part, out, last = self.r.part[i % 4], self.r.sums[i], self.zs - 1
         out[...] = part[self.c, self.z].astype(F32)
 
         def take(t):
@@ -302,12 +321,12 @@
             pl.when(self.z == last)(lambda: self.merge_copy(i, False).wait_send())
 
     def products(self, i, pairs):
-        part, count = self.r.part[i % 2], self.count
+        part, count = self.r.part[i % 4], self.count
 
         def chip(z, carry):
             here = pl.ds(pl.multiple_of(z * 2 * count, 2 * count), 2 * count)
             for j, left, right in pairs:
-                if i % 2 == 0 and self.flip:
+                if i % 4 >= 2 and self.flip:
                     product = mm(right[...], left[:, here]).astype(BF16)
                     part[0, z, j] = product[:, :count]
                     part[1, z, j] = product[:, count:]
@@ -372,11 +391,11 @@
         where = rows_of(block, self.rows)
         source = r.ng[2 * layer][where]
         cosine, sine = self.turning(where)
-        raw = mm(source, self.matrix(3 * layer, 0))
+        raw = mm(source, self.matrix(4 * layer, 0))
         r.q[layer][where] = (raw * cosine + swap_halves(raw) * sine).astype(BF16)
-        raw = mm(source, self.matrix(3 * layer, 1))
+        raw = mm(source, self.matrix(4 * layer, 1))
         r.k[layer][where] = (raw * cosine + swap_halves(raw) * sine).astype(BF16)
-        raw = mm(source, self.matrix(3 * layer, 2))
+        raw = mm(source, self.matrix(4 * layer, 2))
         if layer == 0:
             r.first[where] = raw
             r.v[layer][where] = raw.astype(BF16)
@@ -394,7 +413,7 @@
             mixed = mm(jnp.concatenate(probs, axis=0), r.v[layer][:span])
             block = unstack_heads(mixed, masks32, rows).astype(BF16)
             r.att[layer][here] = block
-            self.ship(mm_nt(block, self.matrix(3 * layer, 3)), slot, i)
+            self.ship(mm_nt(block, self.matrix(4 * layer + 1, 0)), slot, i)
 
     def attend_back(self, layer, slot):
         r, rows = self.r, self.rows
@@ -434,45 +453,60 @@
                 gvr = (r.gva[here] + r.carry[here]).astype(BF16)
             r.gq[here], r.gk[here], r.gv[here] = gqr, gkr, gvr
             part = (
-                mm_nt(gqr, self.matrix(3 * layer, 0))
-                + mm_nt(gkr, self.matrix(3 * layer, 1))
-                + mm_nt(gvr, self.matrix(3 * layer, 2))
+                mm_nt(gqr, self.matrix(4 * layer, 0))
+                + mm_nt(gkr, self.matrix(4 * layer, 1))
+                + mm_nt(gvr, self.matrix(4 * layer, 2))
             )
             self.ship(part, slot, i)
 
-    def feed(self, layer, slot, buffer, agslot, turn, ready):
+    def feed(self, slot, buffer, agslot, ready):
         r = self.r
 
         def first(where):
-            source = r.ng[2 * layer + 1][where]
-            g = self.into_hidden(source, 3 * layer + 1, 0)
-            u = self.into_hidden(source, 3 * layer + 1, 1)
-            if not turn:
-                r.gate[where], r.up[where] = g, u
-            return g, u
-
-        def second(where, g, u):
-            if not turn:
-                return self.out_of_hidden((g * jax.nn.sigmoid(g) * u).astype(BF16), 3 * layer + 2, 0)
-            part, h = self.feed_back(layer, where, 0, g, u)
-            r.ypart[where] = self.out_of_hidden(h, 3 * layer + 2, 0).astype(BF16)
-            return part
-
-        mine = rows_of(self.ha, self.rows)
-        g, u = first(mine)
-        ready()
-        r.own[...] = second(mine, g, u)
+            source = buffer[where]
+            r.gate[where] = self.into_hidden(source, 2, 0)
+            r.up[where] = self.into_hidden(source, 2, 1)
+
+        def second(where):
+            g, u = r.gate[where], r.up[where]
+            return self.out_of_hidden((g * jax.nn.sigmoid(g) * u).astype(BF16), 3, 0)
+
+        places = [rows_of(other(self.ha, k), self.rows) for k in range(self.n)]
+        first(places[0])
         for k in range(1, self.n):
+            if k == self.n - 1:
+                ready()
+                r.own[...] = second(places[0])
+                for j in range(1, k):
+                    self.send_part(slot, j, second(places[j]))
             self.arrived(buffer, agslot, k)
+            first(places[k])
+        self.send_part(slot, self.n - 1, second(places[self.n - 1]))
+
+    def feed_turn(self, slot, buffer, agslot):
+        r = self.r
+        for k in range(self.n):
+            if k > 0:
+                self.arrived(buffer, agslot, k)
             where = rows_of(other(self.ha, k), self.rows)
-            r.sbuf[k] = second(where, *first(where)).astype(BF16)
-            self.part_copy(slot, k, other(self.ha, k)).start()
+            source = buffer[where]
+            g, u = self.into_hidden(source, 6, 0), self.into_hidden(source, 6, 1)
+            part, h = self.feed_back(1, where, 0, g, u)
+            if k == 0:
+                r.own[...] = part
+            else:
+                self.send_part(slot, k, part)
+            r.ypart[where] = self.out_of_hidden(h, 7, 0).astype(BF16)
+
+    def send_part(self, slot, k, part):
+        self.r.sbuf[k] = part.astype(BF16)
+        self.part_copy(slot, k, other(self.ha, k)).start()
 
     def feed_back(self, layer, where, gg, g, u):
         r = self.r
         s = jax.nn.sigmoid(g)
         h = (g * s * u).astype(BF16)
-        gh = self.into_hidden(r.gg[gg][where], 3 * layer + 2, 0)
+        gh = self.into_hidden(r.gg[gg][where], 4 * layer + 3, 0)
         a = (gh * u * s * (1.0 + g * (1.0 - s))).astype(BF16)
         b = (gh * g * s).astype(BF16)
         for j, value in enumerate((a, b, h)):
@@ -480,17 +514,26 @@
                 r.units[j][:, where] = value.T
             else:
                 r.units[j][where] = value
-        return self.out_of_hidden(a, 3 * layer + 1, 0) + self.out_of_hidden(b, 3 * layer + 1, 1), h
-
-    def feed_grads(self, layer):
-        r = self.r
-        normed = r.ng[2 * layer + 1]
-        self.products(2 * layer, [(0, normed, r.units[0]), (1, normed, r.units[1]), (2, r.gg[0], r.units[2])])
-
-    def attend_grads(self, layer):
+        return self.out_of_hidden(a, 4 * layer + 2, 0) + self.out_of_hidden(b, 4 * layer + 2, 1), h
+
+    def down_grads(self, layer):
+        self.products(4 * layer + 3, [(0, self.r.gg[0], self.r.units[2])])
+        self.reduce_start(4 * layer + 3)
+
+    def gate_grads(self, layer):
+        normed = self.r.ng[2 * layer + 1]
+        self.products(4 * layer + 2, [(0, normed, self.r.units[0]), (1, normed, self.r.units[1])])
+        self.reduce_start(4 * layer + 2)
+
+    def output_grads(self, layer):
+        self.products(4 * layer + 1, [(0, self.r.gg[1], self.r.att[layer])])
+        self.reduce_start(4 * layer + 1)
+
+    def head_grads(self, layer):
         r = self.r
         normed = r.ng[2 * layer]
-        self.products(2 * layer + 1, [(0, normed, r.gq), (1, normed, r.gk), (2, normed, r.gv), (3, r.gg[1], r.att[layer])])
+        self.products(4 * layer, [(0, normed, r.gq), (1, normed, r.gk), (2, normed, r.gv)])
+        self.reduce_start(4 * layer)
 
 
     def gain_phase(self, slot, axis, me, count, place):
@@ -522,7 +565,7 @@
         for d in range(1, self.zs):
             t = lax.rem(self.z + d, self.zs)
             pl.semaphore_signal(barrier, inc=1, device_id={"af": t * 2 + self.c}, device_id_type=MESH)
-        for i in range(6):
+        for i in range(8):
             for j in range(r.w[i].shape[1]):
                 self.local_copy(i, j).start()
         mine = rows_of(self.ha, self.rows)
@@ -532,60 +575,81 @@
         pl.semaphore_wait(barrier, n - 1 + 1 + self.zs - 1)
 
         self.gather_start(0)
+        self.gather_start(1)
         self.spread(r.ng[0], 0)
+        self.tables()
+        self.gather_hop(0, 1)
+        self.gather_start(2)
+        self.arrived(r.ng[0], 0, 1)
+        self.gather_hop(1, 1)
+        self.gather_hop(0, 2)
+        for k in range(2, n):
+            self.arrived(r.ng[0], 0, k)
         self.spread(r.gg[0], 1)
-        self.tables()
-        self.gather_mid(0)
-        self.gather_start(1)
+        self.gather_hop(1, 2)
+        self.gather_hop(0, 3)
         self.gather_end(0)
-        self.project(0, self.ha)
-        for k in range(1, n):
-            self.arrived(r.ng[0], 0, k)
+        for k in range(n):
             self.project(0, other(self.ha, k))
+        self.gather_hop(1, 3)
+        self.gather_end(1)
+        self.gather_hop(2, 1)
+        self.gather_start(3)
         self.attend(0, 0)
+        self.arrived(r.gg[0], 1, 1)
+        self.gather_hop(2, 2)
         r.middle[0][...] = x + self.collect(0)
 
         r.ng[1][mine] = normalize(r.middle[0][...], r.gains[1][...]).astype(BF16)
         self.spread(r.ng[1], 2)
-        self.gather_mid(1)
-        self.gather_start(2)
-        self.gather_end(1)
-
-        def ready_early():
-            self.gather_mid(2)
-            self.gather_start(3)
-            self.gather_end(2)
-
-        self.feed(0, 1, r.ng[1], 2, False, ready_early)
+        self.gather_hop(3, 1)
+        self.gather_start(4)
+        self.gather_start(5)
+        self.gather_hop(2, 3)
+        self.gather_end(2)
+        self.gather_hop(3, 2)
+
+        def ready():
+            self.gather_hop(3, 3)
+            self.gather_start(6)
+            self.gather_end(3)
+
+        self.feed(1, r.ng[1], 2, ready)
+        for third in (1, 2):
+            self.gather_hop(4, third)
+            self.gather_hop(5, third)
         r.between[...] = r.middle[0][...] + self.collect(1)
 
         r.ng[2][mine] = normalize(r.between[...], r.gains[2][...]).astype(BF16)
         self.spread(r.ng[2], 3)
-        self.gather_mid(3)
-        self.gather_start(4)
-        self.gather_end(3)
+        self.gather_hop(4, 3)
+        self.gather_hop(5, 3)
+        self.gather_start(7)
+        self.gather_end(4)
         self.project(1, self.ha)
+        self.gather_hop(6, 1)
         for k in range(1, n):
             self.arrived(r.ng[2], 3, k)
             self.project(1, other(self.ha, k))
+        self.gather_end(5)
+        self.gather_hop(6, 2)
         self.attend(1, 2)
-        self.gather_mid(4)
-        self.gather_start(5)
+        self.gather_hop(7, 1)
+        self.gather_hop(6, 3)
         r.middle[1][...] = r.between[...] + self.collect(2)
 
         r.ng[3][mine] = normalize(r.middle[1][...], r.gains[3][...]).astype(BF16)
         self.spread(r.ng[3], 4)
-        self.gather_end(4)
-        for k in range(1, n):
+        self.gather_hop(7, 2)
+        self.gather_end(6)
+        for k in range(2, n):
             self.arrived(r.gg[0], 1, k)
-
-        def ready_later():
-            self.gather_mid(5)
-            self.gather_end(5)
-
-        self.feed(1, 3, r.ng[3], 4, True, ready_later)
-        self.feed_grads(1)
-        self.reduce_start(2)
+        self.gather_hop(7, 3)
+        self.gather_end(7)
+        self.feed_turn(3, r.ng[3], 4)
+        self.down_grads(1)
+        self.gate_grads(1)
+        self.reduce_mid(7)
         back, gain = norm_back(r.middle[1][...], r.gains[3][...], self.collect(3))
         r.gmid[...] = r.cot[...].astype(F32) + back
         r.gsum[3:4] = gain
@@ -593,26 +657,31 @@
         r.gg[1][mine] = r.gmid[...].astype(BF16)
         self.spread_done(r.gg[0], 1)
         self.spread(r.gg[1], 5)
-        self.reduce_mid(2)
+        self.reduce_mid(6)
         self.pull(1, 5)
         for k in range(1, n):
             self.output_copy(k).start()
+        self.output_grads(1)
         self.attend_back(1, 4)
-        self.attend_grads(1)
-        self.reduce_start(3)
-        self.reduce_merge(2)
+        self.reduce_merge(7)
+        self.head_grads(1)
+        self.reduce_mid(5)
+        self.reduce_merge(6)
         back, gain = norm_back(r.between[...], r.gains[2][...], self.collect(4))
         r.between[...] = r.gmid[...] + back
         r.gsum[2:3] = gain
 
         r.gg[0][mine] = r.between[...].astype(BF16)
+        self.spread_done(r.gg[1], 5)
         self.spread(r.gg[0], 6)
-        self.reduce_mid(3)
+        self.reduce_mid(4)
         out = r.middle[1][...] + r.ypart[mine].astype(F32)
         for k in range(1, n):
             self.output_copy(k).wait_recv()
             out = out + r.yrecv[k].astype(F32)
         r.out[...] = out.astype(BF16)
+        self.reduce_merge(5)
+        self.reduce_end(7)
 
         def back_block(where):
             return self.feed_back(0, where, 0, r.gate[where], r.up[where])[0]
@@ -620,56 +689,60 @@
         r.own[...] = back_block(mine)
         for k in range(1, n):
             self.arrived(r.gg[0], 6, k)
-            where = rows_of(other(self.ha, k), self.rows)
-            r.sbuf[k] = back_block(where).astype(BF16)
-            self.part_copy(5, k, other(self.ha, k)).start()
-        self.reduce_end(2)
-        self.feed_grads(0)
-        self.reduce_start(0)
+            self.send_part(5, k, back_block(rows_of(other(self.ha, k), self.rows)))
+        self.down_grads(0)
+        self.reduce_end(6)
+        self.gate_grads(0)
+        self.reduce_mid(3)
+        self.reduce_merge(4)
         back, gain = norm_back(r.middle[0][...], r.gains[1][...], self.collect(5))
         r.gmid[...] = r.between[...] + back
         r.gsum[1:2] = gain
 
-        self.spread_done(r.gg[1], 5)
         r.gg[1][mine] = r.gmid[...].astype(BF16)
         self.spread(r.gg[1], 7)
+        self.reduce_mid(2)
+        self.reduce_end(5)
+        self.pull(0, 7)
+        self.output_grads(0)
+        self.attend_back(0, 6)
+        self.reduce_merge(3)
+        self.reduce_end(4)
+        self.head_grads(0)
+        self.reduce_mid(1)
+        self.reduce_merge(2)
         self.reduce_mid(0)
-        self.reduce_merge(3)
-        self.pull(0, 7)
-        self.attend_back(0, 6)
-        self.reduce_end(3)
-        self.attend_grads(0)
-        self.reduce_start(1)
-        self.reduce_merge(0)
-        self.reduce_mid(1)
         back, gain = norm_back(x, r.gains[0][...], self.collect(6))
         r.gx[...] = r.gmid[...] + back
         r.gsum[0:1] = gain
 
         r.gbuf[0][self.ha] = r.gsum[...]
         self.gain_phase(0, "ha", self.ha, n, lambda t: t)
-        self.reduce_end(0)
+        self.reduce_merge(1)
+        self.reduce_end(3)
         r.gbuf[1][self.c] = self.gain_sum(0, "ha", self.ha, n, lambda t: t)
         self.gain_phase(1, "af", self.c, 2, lambda t: self.z * 2 + t)
-        self.reduce_merge(1)
+        self.reduce_merge(0)
         r.gbuf[2][self.z] = self.gain_sum(1, "af", self.c, 2, lambda t: self.z * 2 + t)
         self.gain_phase(2, "af", self.z, self.zs, lambda t: t * 2 + self.c)
+        self.reduce_end(2)
         total = self.gain_sum(2, "af", self.z, self.zs, lambda t: t * 2 + self.c)
         for i in range(4):
             r.gainsum[i] = total[i:i + 1]
         self.reduce_end(1)
+        self.reduce_end(0)
         for slot, buffer in ((0, r.ng[0]), (2, r.ng[1]), (3, r.ng[2]), (4, r.ng[3]), (6, r.gg[0]), (7, r.gg[1])):
             self.spread_done(buffer, slot)
         for k in range(1, n):
             self.output_copy(k).wait_send()
-        for i in range(6):
+        for i in range(8):
             self.gather_drain(i)
 
     def pull(self, layer, slot):
         r = self.r
 
         def block(where):
-            r.gat[where] = mm(r.gg[1][where], self.matrix(3 * layer, 3)).astype(BF16)
+            r.gat[where] = mm(r.gg[1][where], self.matrix(4 * layer + 1, 0)).astype(BF16)
 
         block(rows_of(self.ha, self.rows))
         for k in range(1, self.n):
@@ -688,19 +761,24 @@
 
 
 def finish_kernel(*refs):
-    sums, gains, out, gx = refs[:4], refs[4], refs[5], refs[6]
-    results, sem = refs[7:-1], refs[-1]
-    pairs = [(out, results[0]), (gx, results[1])]
+    sums, gains, out, gx = refs[:8], refs[8], refs[9], refs[10]
+    results, held, sem = refs[11:31], refs[31:-1], refs[-1]
+    pairs = [(out, 0), (gx, 1)]
     for layer in range(2):
         first = 2 + 9 * layer
-        pairs.append((gains.at[2 * layer], results[first]))
-        pairs.append((gains.at[2 * layer + 1], results[first + 5]))
-        pairs += [(sums[2 * layer + 1].at[j], results[first + 1 + j]) for j in range(4)]
-        pairs += [(sums[2 * layer].at[j], results[first + 6 + j]) for j in range(3)]
-    copies = [pltpu.make_async_copy(source, target, sem.at[k]) for k, (source, target) in enumerate(pairs)]
-    for copy in copies:
+        pairs += [(gains.at[2 * layer], first), (gains.at[2 * layer + 1], first + 5)]
+        pairs += [(sums[4 * layer].at[j], first + 1 + j) for j in range(3)]
+        pairs.append((sums[4 * layer + 1].at[0], first + 4))
+        pairs += [(sums[4 * layer + 2].at[j], first + 6 + j) for j in range(2)]
+        pairs.append((sums[4 * layer + 3].at[0], first + 8))
+    into = [pltpu.make_async_copy(source, held[k], sem.at[0, k]) for source, k in pairs]
+    onward = [pltpu.make_async_copy(held[k], results[k], sem.at[1, k]) for _, k in pairs]
+    for copy in into:
         copy.start()
-    for copy in copies:
+    for first, second in zip(into, onward):
+        first.wait()
+        second.start()
+    for copy in onward:
         copy.wait()
 
 
@@ -726,8 +804,8 @@
         gate_early, upward_early, down_early = gate_early.T, upward_early.T, down_early.T
         gate_later, upward_later, down_later = gate_later.T, upward_later.T, down_later.T
     groups = [
-        (query_early, keys_early, values_early, output_early), (gate_early, upward_early), (down_early,),
-        (query_later, keys_later, values_later, output_later), (gate_later, upward_later), (down_later,),
+        (query_early, keys_early, values_early), (output_early,), (gate_early, upward_early), (down_early,),
+        (query_later, keys_later, values_later), (output_later,), (gate_later, upward_later), (down_later,),
     ]
     gains = [v[None, :] for v in (attngain_early, ffngain_early, attngain_later, ffngain_later)]
 
@@ -754,7 +832,7 @@
         names.append((name, index))
         outs.append(jax.ShapeDtypeStruct(shape, kind))
 
-    blocks = [(3, *down_early.shape), (4, wrows, width)] * 2
+    blocks = [(len(group), *group[0].shape) for group in groups]
     for i, shape in enumerate(blocks):
         give("sums", i, shape, F32)
     give("gainsum", None, (4, 1, depth), F32)
@@ -769,12 +847,13 @@
 
     for i, group in enumerate(groups):
         hold("w", i, (g, len(group), *group[0].shape), BF16)
+    for i in range(8):
+        hold("zrecv", i, (zs, *blocks[i]), BF16)
     for i in range(4):
         hold("ng", i, (bucket, depth), BF16)
-        hold("zrecv", i, (zs, *blocks[i]), BF16)
-    for i in range(2):
         hold("part", i, (2, zs, *blocks[i]), BF16)
         hold("swapped", i, (zs, *blocks[i]), BF16)
+    for i in range(2):
         hold("gg", i, (bucket, depth), BF16)
         for name in ("q", "k", "v", "att"):
             hold(name, i, (bucket, width), BF16)
@@ -798,8 +877,8 @@
     for i, count in enumerate((n, 2, zs)):
         hold("gbuf", i, (count, 4, depth), F32)
     for name, shape in (
-        ("ags", (8, n)), ("agr", (8, n)), ("pss", (8, n)), ("psr", (8, n)), ("lsem", (6, 4)),
-        ("gs", (6, 2, zs + 2)), ("gr", (6, 2, zs + 2)), ("rs", (4, zs + 3)), ("rr", (4, zs + 3)),
+        ("ags", (8, n)), ("agr", (8, n)), ("pss", (8, n)), ("psr", (8, n)), ("lsem", (8, 3)),
+        ("gs", (8, 2, 2 * zs)), ("gr", (8, 2, zs)), ("rs", (8, zs + 3)), ("rr", (8, zs + 3)),
         ("gns", (3, max(n, zs))), ("gnr", (3, max(n, zs))),
     ):
         names.append((name, None))
@@ -820,11 +899,12 @@
         [shape((1, depth), F32)] + [shape((wrows, width), F32)] * 4
         + [shape((1, depth), F32)] + [shape(down_early.shape, F32)] * 3
     )
+    final_shapes = [shape((rows, depth), BF16), shape((rows, depth), F32), *layer, *layer]
     finals = pl.pallas_call(
         finish_kernel,
-        out_shape=[shape((rows, depth), BF16), shape((rows, depth), F32), *layer, *layer],
-        in_specs=[ANY] * 7, out_specs=[VMEM] * 20, scratch_shapes=[pltpu.SemaphoreType.DMA((20,))], name="finish",
-        compiler_params=pltpu.CompilerParams(vmem_limit_bytes=62 * 1024 * 1024),
+        out_shape=final_shapes, in_specs=[ANY] * 11, out_specs=[ANY] * 20,
+        scratch_shapes=[*(pltpu.VMEM(v.shape, v.dtype) for v in final_shapes), pltpu.SemaphoreType.DMA((2, 20))],
+        compiler_params=pltpu.CompilerParams(vmem_limit_bytes=62 * 1024 * 1024), name="finish",
     )(*results)
     finals = [v[0] if v.shape[0] == 1 else v for v in finals]
     if flip:

time: 299 us -> 261 us (0.87)
  Pallas kernels: 293 us -> 255 us
    pallas_call x1, Pallas kernels: 288 us -> 251 us  [per_device(): pl.pallas_call(functools.partial(step_kernel, n, g, names), out_shape=out...]
where the time goes in v3:
time: 261 us; the launch traced here: 256 us
  Pallas kernels  255 us (98%)
    pallas_call x1, Pallas kernels, per_device(): pl.pallas_call(functools.partial(step_kernel, n, g, names), out_shape=out...  251 us

profile of v3, /device:TPU:0, one launch (start us, length us, event | category | flops | bytes accessed | tf_op | source)
XLA Modules:
  0.0 256.1 jit_solution(15459224888195936363)
XLA Ops:
  0.7 251.2 %step.1 = (f32[3,128,256]{2,1,0:T(8,128)}, f32[1,128,256]{2,1,0:T(8,128)}, f32[2,704,128]{2,1,0:T(8,128)}, f32[1,704,128]{2,1,0:T(8,128)}, f32[3,128,256]{2,1,0:...) custom-call(bf16[128,1024]{1,0:T(8,128)(2,1)} %refs_0_.1, ...), custom_call_target="tpu_custom_call" | custom-call | flops 20000000000 | bytes 10000000 | tf_op jit(solution)/shard_map/step/pallas_call | solution.py:887
  251.9 3.7 %finish.1 = (bf16[128,1024]{1,0:T(8,128)(2,1)}, f32[128,1024]{1,0:T(8,128)}, f32[1,1024]{1,0:T(1,128)}, f32[128,256]{1,0:T(8,128)}, f32[128,256]{1,0:T(8,128)}, ...) custom-call(f32[3,128,256]{2,1,0:T(8,128)} %get-tuple-element.51.ref, ...), custom_call_target="tpu_custom_call" | custom-call | tf_op jit(solution)/shard_map/finish/pallas_call | solution.py:903

commit v4 on v3

--- a/solution.py
+++ b/solution.py
@@ -10,6 +10,7 @@
 from jax.sharding import PartitionSpec as P
 
 HD = 64
+CHUNKS = 1
 epsilon = 1e-06
 rope_base = 10000.0
 MESH = pl.DeviceIdType.MESH
@@ -105,56 +106,88 @@
     def __init__(self, n, g, refs):
         self.n, self.g, self.zs = n, g, g // 2
         self.square = n == 4
+        self.chunks = refs.agr.shape[2]
         self.r = refs
         self.ha, self.af = lax.axis_index("ha"), lax.axis_index("af")
         self.z, self.c = lax.div(self.af, 2), lax.rem(self.af, 2)
         self.sibling = self.af + 1 - 2 * self.c
         self.rows, self.depth = refs.x.shape
         self.bucket = self.rows * n
+        self.step = self.rows // self.chunks
+        if self.square:
+            self.near, self.far = [(c, (1, 2)) for c in range(self.chunks)], [(c, (3,)) for c in range(self.chunks)]
+            self.order = self.near[:1]
+            for c in range(1, self.chunks):
+                self.order += [self.near[c], self.far[c - 1]]
+            self.order.append(self.far[-1])
+        else:
+            self.near, self.far = [(c, (k,)) for c in range(self.chunks) for k in range(1, n)], []
+            self.order = self.near
         self.width = refs.q[0].shape[1]
         self.heads = self.width // HD
         self.hidden = refs.gate.shape[1]
         self.count = self.depth // g
         self.flip = refs.w[2].shape[3] == self.count
-        self.ends = self.zs > 3
-        self.reach = self.zs - 2 if self.ends else self.zs - 1
-
-
-    def token_copy(self, buffer, slot, owner, k, target, half=None):
-        rows = self.rows if half is None else self.rows // 2
-        first = owner * self.rows if half is None else owner * self.rows + half * rows
-        block = buffer.at[pl.ds(pl.multiple_of(first, rows), rows)]
-        return remote(block, block, self.r.ags.at[slot, k], self.r.agr.at[slot, k], ha=target)
-
-    def relay_copy(self, buffer, slot, k):
-        return self.token_copy(buffer, slot, other(self.ha, k), 3 if k == 1 else 0, other(self.ha, 3 - k), k - 1)
-
-    def spread(self, buffer, slot):
+
+
+    def chunk(self, c):
+        return slice(c * self.step, (c + 1) * self.step)
+
+    def chunk_of(self, owner, c):
+        return pl.ds(pl.multiple_of(owner * self.rows + c * self.step, self.step), self.step)
+
+    def token_copy(self, buffer, slot, owner, c, k, target, half=None):
+        count = self.step if half is None else self.step // 2
+        first = owner * self.rows + c * self.step + (0 if half is None else half * count)
+        block = buffer.at[pl.ds(pl.multiple_of(first, count), count)]
+        return remote(block, block, self.r.ags.at[slot, k, c], self.r.agr.at[slot, k, c], ha=target)
+
+    def relay_copy(self, buffer, slot, c, k):
+        return self.token_copy(buffer, slot, other(self.ha, k), c, 3 if k == 1 else 0, other(self.ha, 3 - k), k - 1)
+
+    def spread(self, buffer, slot, c):
         for k in range(1, 3 if self.square else self.n):
-            self.token_copy(buffer, slot, self.ha, k, other(self.ha, k)).start()
-
-    def arrived(self, buffer, slot, k):
-        if not self.square:
-            self.token_copy(buffer, slot, other(self.ha, k), k, other(self.ha, k)).wait_recv()
-        elif k == 1:
-            for j in (1, 2):
-                self.token_copy(buffer, slot, other(self.ha, j), j, other(self.ha, j)).wait_recv()
-                self.relay_copy(buffer, slot, j).start()
-        elif k == 3:
-            for half in (0, 1):
-                self.token_copy(
-                    buffer, slot, other(self.ha, 3), 0 if half else 3, other(self.ha, 1 + half), half
-                ).wait_recv()
+            self.token_copy(buffer, slot, self.ha, c, k, other(self.ha, k)).start()
+
+    def spread_all(self, buffer, slot):
+        for c in range(self.chunks):
+            self.spread(buffer, slot, c)
+
+    def arrived(self, buffer, slot, places):
+        for c, ks in places:
+            for k in ks:
+                partner = other(self.ha, k)
+                if self.square and k == 3:
+                    for half in (0, 1):
+                        self.token_copy(
+                            buffer, slot, partner, c, 0 if half else 3, other(self.ha, 1 + half), half
+                        ).wait_recv()
+                else:
+                    self.token_copy(buffer, slot, partner, c, k, partner).wait_recv()
+                    if self.square:
+                        self.relay_copy(buffer, slot, c, k).start()
 
     def spread_done(self, buffer, slot):
-        for k in range(1, 3 if self.square else self.n):
-            self.token_copy(buffer, slot, self.ha, k, other(self.ha, k)).wait_send()
-        if self.square:
-            for k in (1, 2):
-                self.relay_copy(buffer, slot, k).wait_send()
-
-    def part_copy(self, slot, k, target):
-        return remote(self.r.sbuf.at[k], self.r.rbuf.at[k], self.r.pss.at[slot, k], self.r.psr.at[slot, k], ha=target)
+        for c in range(self.chunks):
+            for k in range(1, 3 if self.square else self.n):
+                self.token_copy(buffer, slot, self.ha, c, k, other(self.ha, k)).wait_send()
+            if self.square:
+                for k in (1, 2):
+                    self.relay_copy(buffer, slot, c, k).wait_send()
+
+    def each_block(self, buffer, slot, do):
+        do(self.ha)
+        for places in (self.near, self.far):
+            self.arrived(buffer, slot, places)
+            for k in sorted({k for _, ks in places for k in ks}):
+                do(other(self.ha, k))
+
+    def part_copy(self, slot, k, c, target):
+        here = self.chunk(c)
+        return remote(
+            self.r.sbuf.at[k, here], self.r.rbuf.at[k, here], self.r.pss.at[slot, k, c], self.r.psr.at[slot, k, c],
+            ha=target,
+        )
 
     def ship(self, part, slot, index):
         for k in range(self.n):
@@ -164,22 +197,32 @@
                     self.r.own[...] = part
                 else:
                     self.r.sbuf[k] = part.astype(BF16)
-                    self.part_copy(slot, k, index).start()
-
-    def collect(self, slot):
-        total = self.r.own[...]
+                    for c in range(self.chunks):
+                        self.part_copy(slot, k, c, index).start()
+
+    def send_parts(self, slot, c, ks, part):
+        for j, k in enumerate(ks):
+            self.r.sbuf[k, self.chunk(c)] = part[self.chunk(j)].astype(BF16)
+            self.part_copy(slot, k, c, other(self.ha, k)).start()
+
+    def collect(self, slot, c):
+        here = self.chunk(c)
+        total = self.r.own[here]
         for k in range(1, self.n):
-            self.part_copy(slot, k, other(self.ha, k)).wait_recv()
-            total = total + self.r.rbuf[k].astype(F32)
-        for k in range(1, self.n):
-            self.part_copy(slot, k, other(self.ha, k)).wait_send()
+            self.part_copy(slot, k, c, other(self.ha, k)).wait_recv()
+            total = total + self.r.rbuf[k, here].astype(F32)
         return total
+
+    def parts_done(self, slot):
+        for c in range(self.chunks):
+            for k in range(1, self.n):
+                self.part_copy(slot, k, c, other(self.ha, k)).wait_send()
 
     def output_copy(self, k):
         target = other(self.ha, k)
         return remote(
             self.r.ypart.at[rows_of(target, self.rows)], self.r.yrecv.at[k],
-            self.r.pss.at[7, k], self.r.psr.at[7, k], ha=target,
+            self.r.pss.at[7, k, 0], self.r.psr.at[7, k, 0], ha=target,
         )
 
 
@@ -196,12 +239,6 @@
     def along(self, i, source, z, slot):
         block = self.block(i, source, self.c)
         return remote(block, block, self.r.gs.at[i, 1, slot], self.r.gr.at[i, 1, source], af=z * 2 + self.c)
-
-    def neighbours(self, do, far_first=False):
-        distances = range(1, self.reach + 1)
-        for d in reversed(distances) if far_first else distances:
-            for t in (self.z + d, self.z - d):
-                pl.when((t >= 0) & (t < self.zs))(functools.partial(do, t))
 
     def onward(self, i, hop):
         result = []
@@ -251,20 +288,43 @@
             af=self.sibling,
         )
 
-    def sum_copy(self, i, source, z):
-        return remote(
-            self.r.part[i % 4].at[self.c, z], self.r.zrecv[i].at[source],
-            self.r.rs.at[i, 1 + z], self.r.rr.at[i, 1 + source], af=z * 2 + self.c,
+    def flow(self, i, stage, side):
+        last = self.zs - 1
+        target = self.z + (1 if side == 0 else -1)
+        upper = lax.div(2 * target, self.zs)
+        if side == 0:
+            valid = (target <= last) & (target <= stage)
+            block = last - stage + target
+            slot = block if stage < last else target * (1 - upper)
+        else:
+            valid = (target >= 0) & (last - target <= stage)
+            block = stage - last + target
+            slot = block if stage < last else target + (last - target) * (1 - upper)
+        sem = 2 * stage + side
+        return valid, functools.partial(
+            remote, self.r.part[i % 4].at[self.c, block], self.r.zrecv[i].at[slot],
+            self.r.rs.at[i, sem], self.r.rr.at[i, sem], af=target * 2 + self.c,
         )
 
-    def merge_copy(self, i, up):
+    def taken(self, i, stage, side, use):
         last = self.zs - 1
-        block, target = (last, 1) if up else (0, last - 1)
-        slot = self.zs + (1 if up else 2)
-        return remote(
-            self.r.part[i % 4].at[self.c, block], self.r.zrecv[i].at[target],
-            self.r.rs.at[i, slot], self.r.rr.at[i, slot], af=target * 2 + self.c,
-        )
+        upper = lax.div(2 * self.z, self.zs)
+        if side == 0:
+            valid = (self.z >= 1) & (self.z <= stage)
+            block = last - stage + self.z
+            slot = block if stage < last else self.z * (1 - upper)
+        else:
+            valid = (last - self.z >= 1) & (last - self.z <= stage)
+            block = stage - last + self.z
+            slot = block if stage < last else self.z + (last - self.z) * (1 - upper)
+        sem = 2 * stage + side
+        here = self.r.zrecv[i].at[slot]
+
+        def take():
+            remote(here, here, self.r.rs.at[i, sem], self.r.rr.at[i, sem], af=self.af).wait_recv()
+            use(block, slot)
+
+        pl.when(valid)(take)
 
     def reduce_start(self, i):
         self.swap_copy(i).start()
@@ -278,65 +338,63 @@
             return carry
 
         lax.fori_loop(0, self.zs, add, 0)
-        if self.ends:
-            pl.when(self.z == 0)(lambda: self.merge_copy(i, True).start())
-            pl.when(self.z == last)(lambda: self.merge_copy(i, False).start())
-
-        def send(t):
-            if self.ends:
-                held = ((self.z == 1) & (t == last)) | ((self.z == last - 1) & (t == 0))
-                pl.when(jnp.logical_not(held))(lambda: self.sum_copy(i, self.z, t).start())
-            else:
-                self.sum_copy(i, self.z, t).start()
-
-        self.neighbours(send, far_first=True)
-
-    def reduce_merge(self, i):
-        part, last = self.r.part[i % 4], self.zs - 1
-        if self.ends:
-            def merge(up):
-                block = last if up else 0
-                self.merge_copy(i, up).wait_recv()
-                part[self.c, block] = (
-                    part[self.c, block].astype(F32) + self.r.zrecv[i][1 if up else last - 1].astype(F32)
-                ).astype(BF16)
-                self.sum_copy(i, self.z, block).start()
-
-            pl.when(self.z == 1)(functools.partial(merge, True))
-            pl.when(self.z == last - 1)(functools.partial(merge, False))
+        for side, end in ((0, 0), (1, last)):
+            @pl.when(self.z == end)
+            def _(side=side):
+                for stage in range(1, last + 1):
+                    self.flow(i, stage, side)[1]().start()
+
+    def reduce_hop(self, i, half):
+        part, hops = self.r.part[i % 4], self.zs - 2
+
+        def add(block, slot):
+            part[self.c, block] = (
+                part[self.c, block].astype(F32) + self.r.zrecv[i][slot].astype(F32)
+            ).astype(BF16)
+
+        for stage in range((half - 1) * hops // 2 + 1, half * hops // 2 + 1):
+            for side in (0, 1):
+                self.taken(i, stage, side, add)
+            for side, end in ((0, 0), (1, self.zs - 1)):
+                valid, copy = self.flow(i, stage + 1, side)
+                pl.when(valid & (self.z != end))(lambda copy=copy: copy().start())
 
     def reduce_end(self, i):
-        part, out, last = self.r.part[i % 4], self.r.sums[i], self.zs - 1
-        out[...] = part[self.c, self.z].astype(F32)
-
-        def take(t):
-            self.sum_copy(i, t, t).wait_recv()
-            out[...] += self.r.zrecv[i][t].astype(F32)
-
-        self.neighbours(take)
+        out, last = self.r.sums[i], self.zs - 1
+        out[...] = self.r.part[i % 4][self.c, self.z].astype(F32)
+
+        def add(block, slot):
+            out[...] += self.r.zrecv[i][slot].astype(F32)
+
+        for side in (0, 1):
+            self.taken(i, last, side, add)
         self.swap_copy(i).wait_send()
-        self.neighbours(lambda t: self.sum_copy(i, self.z, t).wait_send())
-        if self.ends:
-            pl.when(self.z == 0)(lambda: self.merge_copy(i, True).wait_send())
-            pl.when(self.z == last)(lambda: self.merge_copy(i, False).wait_send())
+        for stage in range(1, last + 1):
+            for side in (0, 1):
+                valid, copy = self.flow(i, stage, side)
+                pl.when(valid)(lambda copy=copy: copy().wait_send())
 
     def products(self, i, pairs):
         part, count = self.r.part[i % 4], self.count
-
-        def chip(z, carry):
-            here = pl.ds(pl.multiple_of(z * 2 * count, 2 * count), 2 * count)
-            for j, left, right in pairs:
-                if i % 4 >= 2 and self.flip:
-                    product = mm(right[...], left[:, here]).astype(BF16)
-                    part[0, z, j] = product[:, :count]
-                    part[1, z, j] = product[:, count:]
-                else:
-                    product = mm_tn(left[:, here], right[...]).astype(BF16)
-                    part[0, z, j] = product[:count]
-                    part[1, z, j] = product[count:]
-            return carry
-
-        lax.fori_loop(0, self.zs, chip, 0)
+        turn = i % 4 >= 2 and self.flip
+        for group in [[pair] for pair in pairs] if turn else [pairs]:
+            if turn:
+                self.r.turned[...] = group[0][2][...].T
+
+            def chip(z, carry, group=group):
+                here = pl.ds(pl.multiple_of(z * 2 * count, 2 * count), 2 * count)
+                for j, left, right in group:
+                    if turn:
+                        product = mm(self.r.turned[...], left[:, here]).astype(BF16)
+                        part[0, z, j] = product[:, :count]
+                        part[1, z, j] = product[:, count:]
+                    else:
+                        product = mm_tn(left[:, here], right[...]).astype(BF16)
+                        part[0, z, j] = product[:count]
+                        part[1, z, j] = product[count:]
+                return carry
+
+            lax.fori_loop(0, self.zs, chip, 0)
 
 
     def tables(self):
@@ -459,61 +517,80 @@
             )
             self.ship(part, slot, i)
 
+    def gathered(self, ref, wheres):
+        blocks = [ref[where] for where in wheres]
+        return blocks[0] if len(blocks) == 1 else jnp.concatenate(blocks, axis=0)
+
+    def scattered(self, ref, wheres, value):
+        count = value.shape[0] // len(wheres)
+        for j, where in enumerate(wheres):
+            ref[where] = value[j * count:(j + 1) * count]
+
     def feed(self, slot, buffer, agslot, ready):
         r = self.r
 
-        def first(where):
-            source = buffer[where]
-            r.gate[where] = self.into_hidden(source, 2, 0)
-            r.up[where] = self.into_hidden(source, 2, 1)
-
-        def second(where):
-            g, u = r.gate[where], r.up[where]
+        def first(wheres):
+            source = self.gathered(buffer, wheres)
+            g, u = self.into_hidden(source, 2, 0), self.into_hidden(source, 2, 1)
+            self.scattered(r.gate, wheres, g)
+            self.scattered(r.up, wheres, u)
+            return g, u
+
+        def second(g, u):
             return self.out_of_hidden((g * jax.nn.sigmoid(g) * u).astype(BF16), 3, 0)
 
-        places = [rows_of(other(self.ha, k), self.rows) for k in range(self.n)]
-        first(places[0])
-        for k in range(1, self.n):
-            if k == self.n - 1:
+        mine = rows_of(self.ha, self.rows)
+        first([mine])
+        for index, (c, ks) in enumerate(self.order):
+            self.arrived(buffer, agslot, [(c, ks)])
+            g, u = first([self.chunk_of(other(self.ha, k), c) for k in ks])
+            if index == 0:
                 ready()
-                r.own[...] = second(places[0])
-                for j in range(1, k):
-                    self.send_part(slot, j, second(places[j]))
-            self.arrived(buffer, agslot, k)
-            first(places[k])
-        self.send_part(slot, self.n - 1, second(places[self.n - 1]))
+            self.send_parts(slot, c, ks, second(g, u))
+            if index == 0:
+                r.own[...] = second(r.gate[mine], r.up[mine])
 
     def feed_turn(self, slot, buffer, agslot):
         r = self.r
-        for k in range(self.n):
-            if k > 0:
-                self.arrived(buffer, agslot, k)
-            where = rows_of(other(self.ha, k), self.rows)
-            source = buffer[where]
+
+        def branch(wheres):
+            source = self.gathered(buffer, wheres)
             g, u = self.into_hidden(source, 6, 0), self.into_hidden(source, 6, 1)
-            part, h = self.feed_back(1, where, 0, g, u)
-            if k == 0:
-                r.own[...] = part
-            else:
-                self.send_part(slot, k, part)
-            r.ypart[where] = self.out_of_hidden(h, 7, 0).astype(BF16)
-
-    def send_part(self, slot, k, part):
-        self.r.sbuf[k] = part.astype(BF16)
-        self.part_copy(slot, k, other(self.ha, k)).start()
-
-    def feed_back(self, layer, where, gg, g, u):
+            return self.feed_back(1, wheres, g, u)
+
+        def output(wheres, h):
+            self.scattered(r.ypart, wheres, self.out_of_hidden(h, 7, 0).astype(BF16))
+
+        mine = [rows_of(self.ha, self.rows)]
+        r.own[...], h = branch(mine)
+        output(mine, h)
+        for c, ks in self.order:
+            self.arrived(buffer, agslot, [(c, ks)])
+            wheres = [self.chunk_of(other(self.ha, k), c) for k in ks]
+            part, h = branch(wheres)
+            self.send_parts(slot, c, ks, part)
+            output(wheres, h)
+
+    def feed_return(self, slot, buffer, agslot):
+        r = self.r
+
+        def branch(wheres):
+            return self.feed_back(0, wheres, self.gathered(r.gate, wheres), self.gathered(r.up, wheres))[0]
+
+        r.own[...] = branch([rows_of(self.ha, self.rows)])
+        for c, ks in self.order:
+            self.arrived(buffer, agslot, [(c, ks)])
+            self.send_parts(slot, c, ks, branch([self.chunk_of(other(self.ha, k), c) for k in ks]))
+
+    def feed_back(self, layer, wheres, g, u):
         r = self.r
         s = jax.nn.sigmoid(g)
         h = (g * s * u).astype(BF16)
-        gh = self.into_hidden(r.gg[gg][where], 4 * layer + 3, 0)
+        gh = self.into_hidden(self.gathered(r.gg[0], wheres), 4 * layer + 3, 0)
         a = (gh * u * s * (1.0 + g * (1.0 - s))).astype(BF16)
         b = (gh * g * s).astype(BF16)
         for j, value in enumerate((a, b, h)):
-            if self.flip:
-                r.units[j][:, where] = value.T
-            else:
-                r.units[j][where] = value
+            self.scattered(r.units[j], wheres, value)
         return self.out_of_hidden(a, 4 * layer + 2, 0) + self.out_of_hidden(b, 4 * layer + 2, 1), h
 
     def down_grads(self, layer):
@@ -576,16 +653,14 @@
 
         self.gather_start(0)
         self.gather_start(1)
-        self.spread(r.ng[0], 0)
+        self.spread_all(r.ng[0], 0)
         self.tables()
         self.gather_hop(0, 1)
         self.gather_start(2)
-        self.arrived(r.ng[0], 0, 1)
+        self.arrived(r.ng[0], 0, self.near)
         self.gather_hop(1, 1)
         self.gather_hop(0, 2)
-        for k in range(2, n):
-            self.arrived(r.ng[0], 0, k)
-        self.spread(r.gg[0], 1)
+        self.arrived(r.ng[0], 0, self.far)
         self.gather_hop(1, 2)
         self.gather_hop(0, 3)
         self.gather_end(0)
@@ -596,12 +671,15 @@
         self.gather_hop(2, 1)
         self.gather_start(3)
         self.attend(0, 0)
-        self.arrived(r.gg[0], 1, 1)
         self.gather_hop(2, 2)
-        r.middle[0][...] = x + self.collect(0)
-
-        r.ng[1][mine] = normalize(r.middle[0][...], r.gains[1][...]).astype(BF16)
-        self.spread(r.ng[1], 2)
+
+        for c in range(self.chunks):
+            here = self.chunk(c)
+            value = x[here] + self.collect(0, c)
+            r.middle[0][here] = value
+            r.ng[1][self.chunk_of(self.ha, c)] = normalize(value, r.gains[1][...]).astype(BF16)
+            self.spread(r.ng[1], 2, c)
+        self.parts_done(0)
         self.gather_hop(3, 1)
         self.gather_start(4)
         self.gather_start(5)
@@ -610,6 +688,7 @@
         self.gather_hop(3, 2)
 
         def ready():
+            self.spread_all(r.gg[0], 1)
             self.gather_hop(3, 3)
             self.gather_start(6)
             self.gather_end(3)
@@ -618,118 +697,149 @@
         for third in (1, 2):
             self.gather_hop(4, third)
             self.gather_hop(5, third)
-        r.between[...] = r.middle[0][...] + self.collect(1)
-
-        r.ng[2][mine] = normalize(r.between[...], r.gains[2][...]).astype(BF16)
-        self.spread(r.ng[2], 3)
+
+        for c in range(self.chunks):
+            here = self.chunk(c)
+            value = r.middle[0][here] + self.collect(1, c)
+            r.between[here] = value
+            r.ng[2][self.chunk_of(self.ha, c)] = normalize(value, r.gains[2][...]).astype(BF16)
+            self.spread(r.ng[2], 3, c)
+        self.parts_done(1)
         self.gather_hop(4, 3)
         self.gather_hop(5, 3)
         self.gather_start(7)
         self.gather_end(4)
-        self.project(1, self.ha)
+        self.each_block(r.ng[2], 3, functools.partial(self.project, 1))
         self.gather_hop(6, 1)
-        for k in range(1, n):
-            self.arrived(r.ng[2], 3, k)
-            self.project(1, other(self.ha, k))
+        self.arrived(r.gg[0], 1, self.near)
         self.gather_end(5)
+        self.attend(1, 2)
         self.gather_hop(6, 2)
-        self.attend(1, 2)
         self.gather_hop(7, 1)
         self.gather_hop(6, 3)
-        r.middle[1][...] = r.between[...] + self.collect(2)
-
-        r.ng[3][mine] = normalize(r.middle[1][...], r.gains[3][...]).astype(BF16)
-        self.spread(r.ng[3], 4)
+
+        for c in range(self.chunks):
+            here = self.chunk(c)
+            value = r.between[here] + self.collect(2, c)
+            r.middle[1][here] = value
+            r.ng[3][self.chunk_of(self.ha, c)] = normalize(value, r.gains[3][...]).astype(BF16)
+            self.spread(r.ng[3], 4, c)
+        self.parts_done(2)
         self.gather_hop(7, 2)
         self.gather_end(6)
-        for k in range(2, n):
-            self.arrived(r.gg[0], 1, k)
+        self.arrived(r.gg[0], 1, self.far)
         self.gather_hop(7, 3)
         self.gather_end(7)
         self.feed_turn(3, r.ng[3], 4)
         self.down_grads(1)
         self.gate_grads(1)
         self.reduce_mid(7)
-        back, gain = norm_back(r.middle[1][...], r.gains[3][...], self.collect(3))
-        r.gmid[...] = r.cot[...].astype(F32) + back
+        self.spread_done(r.gg[0], 1)
+
+        gain = 0.0
+        for c in range(self.chunks):
+            here = self.chunk(c)
+            back, share = norm_back(r.middle[1][here], r.gains[3][...], self.collect(3, c))
+            gain = gain + share
+            value = r.cot[here].astype(F32) + back
+            r.gmid[here] = value
+            r.gg[1][self.chunk_of(self.ha, c)] = value.astype(BF16)
+            self.spread(r.gg[1], 5, c)
         r.gsum[3:4] = gain
-
-        r.gg[1][mine] = r.gmid[...].astype(BF16)
-        self.spread_done(r.gg[0], 1)
-        self.spread(r.gg[1], 5)
+        self.parts_done(3)
         self.reduce_mid(6)
+        self.reduce_hop(7, 1)
         self.pull(1, 5)
-        for k in range(1, n):
+        for k in range(3, n):
             self.output_copy(k).start()
+        self.reduce_hop(7, 2)
         self.output_grads(1)
+        self.reduce_hop(6, 1)
         self.attend_back(1, 4)
-        self.reduce_merge(7)
+        self.reduce_end(7)
+        self.reduce_mid(5)
+        self.reduce_hop(6, 2)
         self.head_grads(1)
-        self.reduce_mid(5)
-        self.reduce_merge(6)
-        back, gain = norm_back(r.between[...], r.gains[2][...], self.collect(4))
-        r.between[...] = r.gmid[...] + back
+        self.reduce_hop(5, 1)
+        self.reduce_mid(4)
+        self.spread_done(r.gg[1], 5)
+
+        gain = 0.0
+        for c in range(self.chunks):
+            here = self.chunk(c)
+            back, share = norm_back(r.between[here], r.gains[2][...], self.collect(4, c))
+            gain = gain + share
+            value = r.gmid[here] + back
+            r.between[here] = value
+            r.gg[0][self.chunk_of(self.ha, c)] = value.astype(BF16)
+            self.spread(r.gg[0], 6, c)
         r.gsum[2:3] = gain
-
-        r.gg[0][mine] = r.between[...].astype(BF16)
-        self.spread_done(r.gg[1], 5)
-        self.spread(r.gg[0], 6)
-        self.reduce_mid(4)
+        self.parts_done(4)
+        self.reduce_hop(5, 2)
+        self.reduce_end(6)
+        self.reduce_hop(4, 1)
+        self.feed_return(5, r.gg[0], 6)
+        self.down_grads(0)
+        self.reduce_end(5)
+        self.reduce_hop(4, 2)
+        self.gate_grads(0)
+        self.reduce_mid(3)
+        self.reduce_end(4)
+
+        gain = 0.0
+        for c in range(self.chunks):
+            here = self.chunk(c)
+            back, share = norm_back(r.middle[0][here], r.gains[1][...], self.collect(5, c))
+            gain = gain + share
+            value = r.between[here] + back
+            r.gmid[here] = value
+            r.gg[1][self.chunk_of(self.ha, c)] = value.astype(BF16)
+            self.spread(r.gg[1], 7, c)
+        r.gsum[1:2] = gain
+        self.parts_done(5)
+        self.reduce_mid(2)
+        self.reduce_hop(3, 1)
+        self.pull(0, 7)
+        for k in (1, 2):
+            self.output_copy(k).start()
+        self.reduce_hop(3, 2)
+        self.output_grads(0)
+        self.reduce_hop(2, 1)
+        self.attend_back(0, 6)
+        self.reduce_mid(1)
+        self.reduce_hop(2, 2)
+        self.head_grads(0)
+        self.reduce_end(3)
+        self.reduce_hop(1, 1)
+        self.reduce_mid(0)
+        gain = 0.0
+        for c in range(self.chunks):
+            here = self.chunk(c)
+            back, share = norm_back(x[here], r.gains[0][...], self.collect(6, c))
+            gain = gain + share
+            r.gx[here] = r.gmid[here] + back
+        r.gsum[0:1] = gain
+        self.parts_done(6)
+
+        r.gbuf[0][self.ha] = r.gsum[...]
+        self.gain_phase(0, "ha", self.ha, n, lambda t: t)
         out = r.middle[1][...] + r.ypart[mine].astype(F32)
         for k in range(1, n):
             self.output_copy(k).wait_recv()
             out = out + r.yrecv[k].astype(F32)
         r.out[...] = out.astype(BF16)
-        self.reduce_merge(5)
-        self.reduce_end(7)
-
-        def back_block(where):
-            return self.feed_back(0, where, 0, r.gate[where], r.up[where])[0]
-
-        r.own[...] = back_block(mine)
-        for k in range(1, n):
-            self.arrived(r.gg[0], 6, k)
-            self.send_part(5, k, back_block(rows_of(other(self.ha, k), self.rows)))
-        self.down_grads(0)
-        self.reduce_end(6)
-        self.gate_grads(0)
-        self.reduce_mid(3)
-        self.reduce_merge(4)
-        back, gain = norm_back(r.middle[0][...], r.gains[1][...], self.collect(5))
-        r.gmid[...] = r.between[...] + back
-        r.gsum[1:2] = gain
-
-        r.gg[1][mine] = r.gmid[...].astype(BF16)
-        self.spread(r.gg[1], 7)
-        self.reduce_mid(2)
-        self.reduce_end(5)
-        self.pull(0, 7)
-        self.output_grads(0)
-        self.attend_back(0, 6)
-        self.reduce_merge(3)
-        self.reduce_end(4)
-        self.head_grads(0)
-        self.reduce_mid(1)
-        self.reduce_merge(2)
-        self.reduce_mid(0)
-        back, gain = norm_back(x, r.gains[0][...], self.collect(6))
-        r.gx[...] = r.gmid[...] + back
-        r.gsum[0:1] = gain
-
-        r.gbuf[0][self.ha] = r.gsum[...]
-        self.gain_phase(0, "ha", self.ha, n, lambda t: t)
-        self.reduce_merge(1)
-        self.reduce_end(3)
+        self.reduce_hop(1, 2)
+        self.reduce_hop(0, 1)
         r.gbuf[1][self.c] = self.gain_sum(0, "ha", self.ha, n, lambda t: t)
         self.gain_phase(1, "af", self.c, 2, lambda t: self.z * 2 + t)
-        self.reduce_merge(0)
+        self.reduce_end(2)
         r.gbuf[2][self.z] = self.gain_sum(1, "af", self.c, 2, lambda t: self.z * 2 + t)
         self.gain_phase(2, "af", self.z, self.zs, lambda t: t * 2 + self.c)
-        self.reduce_end(2)
+        self.reduce_hop(0, 2)
+        self.reduce_end(1)
         total = self.gain_sum(2, "af", self.z, self.zs, lambda t: t * 2 + self.c)
         for i in range(4):
             r.gainsum[i] = total[i:i + 1]
-        self.reduce_end(1)
         self.reduce_end(0)
         for slot, buffer in ((0, r.ng[0]), (2, r.ng[1]), (3, r.ng[2]), (4, r.ng[3]), (6, r.gg[0]), (7, r.gg[1])):
             self.spread_done(buffer, slot)
@@ -741,13 +851,11 @@
     def pull(self, layer, slot):
         r = self.r
 
-        def block(where):
+        def block(owner):
+            where = rows_of(owner, self.rows)
             r.gat[where] = mm(r.gg[1][where], self.matrix(4 * layer + 1, 0)).astype(BF16)
 
-        block(rows_of(self.ha, self.rows))
-        for k in range(1, self.n):
-            self.arrived(r.gg[1], slot, k)
-            block(rows_of(other(self.ha, k), self.rows))
+        self.each_block(r.gg[1], slot, block)
 
 
 def step_kernel(n, g, names, *refs):
@@ -791,6 +899,7 @@
 ):
     n, g = lax.axis_size("ha"), lax.axis_size("af")
     zs = g // 2
+    chunks = CHUNKS if n == 4 else 1
     rows, depth = block_input.shape
     bucket = rows * n
     wrows, width = query_early.shape
@@ -867,7 +976,9 @@
     for name in ("gate", "up"):
         hold(name, None, (bucket, hidden), F32)
     for i in range(3):
-        hold("units", i, (hidden, bucket) if flip else (bucket, hidden), BF16)
+        hold("units", i, (bucket, hidden), BF16)
+    if flip:
+        hold("turned", None, (hidden, bucket), BF16)
     for name in ("own", "between", "gmid"):
         hold(name, None, (rows, depth), F32)
     for name in ("sbuf", "rbuf", "yrecv"):
@@ -877,8 +988,8 @@
     for i, count in enumerate((n, 2, zs)):
         hold("gbuf", i, (count, 4, depth), F32)
     for name, shape in (
-        ("ags", (8, n)), ("agr", (8, n)), ("pss", (8, n)), ("psr", (8, n)), ("lsem", (8, 3)),
-        ("gs", (8, 2, 2 * zs)), ("gr", (8, 2, zs)), ("rs", (8, zs + 3)), ("rr", (8, zs + 3)),
+        ("ags", (8, n, chunks)), ("agr", (8, n, chunks)), ("pss", (8, n, chunks)), ("psr", (8, n, chunks)), ("lsem", (8, 3)),
+        ("gs", (8, 2, 2 * zs)), ("gr", (8, 2, zs)), ("rs", (8, 2 * zs)), ("rr", (8, 2 * zs)),
         ("gns", (3, max(n, zs))), ("gnr", (3, max(n, zs))),
     ):
         names.append((name, None))

time: 261 us -> 254 us (0.973)
  the two profiles are of different devices: /device:TPU:0 before, /device:TPU:4 now
where the time goes in v4:
time: 254 us; the launch traced here: 250 us
  Pallas kernels  248 us (98%)
    pallas_call x1, Pallas kernels, per_device(): pl.pallas_call(functools.partial(step_kernel, n, g, names), out_shape=out...  245 us

profile of v4, /device:TPU:4, one launch (start us, length us, event | category | flops | bytes accessed | tf_op | source)
XLA Modules:
  0.0 249.5 jit_solution(14657566413180814791)
XLA Ops:
  0.7 244.7 %step.1 = (f32[3,128,256]{2,1,0:T(8,128)}, f32[1,128,256]{2,1,0:T(8,128)}, f32[2,704,128]{2,1,0:T(8,128)}, f32[1,704,128]{2,1,0:T(8,128)}, f32[3,128,256]{2,1,0:...) custom-call(bf16[128,1024]{1,0:T(8,128)(2,1)} %refs_0_.1, ...), custom_call_target="tpu_custom_call" | custom-call | flops 20000000000 | bytes 10000000 | tf_op jit(solution)/shard_map/step/pallas_call | solution.py:998
  245.3 3.7 %finish.1 = (bf16[128,1024]{1,0:T(8,128)(2,1)}, f32[128,1024]{1,0:T(8,128)}, f32[1,1024]{1,0:T(1,128)}, f32[128,256]{1,0:T(8,128)}, f32[128,256]{1,0:T(8,128)}, ...) custom-call(f32[3,128,256]{2,1,0:T(8,128)} %get-tuple-element.51.ref, ...), custom_call_target="tpu_custom_call" | custom-call | tf_op jit(solution)/shard_map/finish/pallas_call | solution.py:1014
